TPU v7x, 32 devices: a whole 2x2x4 slice. The times are simulated.
32 devices in a mesh: gz: 8 (over z, y), gy: 4 (over x, core).
Axes of the slice: x: 2, y: 2, z: 4, core: 2. Of those that a mesh axis runs over, the one named last changes fastest.
Arguments:
- test_vectors: float32 [4, 32, 384, 256], P(None, 'gz', 'gy'), may hold values from -18 to 18
- conductivity: float32 [32, 384, 256], P('gz', 'gy'), may hold values from 0.1 to 10
Outputs:
- prolongator: float32 [4, 32, 384, 256], P(None, 'gz', 'gy')
- coarse_factors: float32 [10, 8, 96, 64], P(None, 'gz', 'gy')
All inputs are finite; a program needn't handle non-finite values.
Results may differ from a plain program's by a relative error of at most 0.0003.
Values sent between devices are 32-bit elements; how exact they have to be, the bound alone decides.
No kernel may reach another device: no remote copies, remote signals or barrier semaphores. Data moves between devices by JAX's collectives and lax.ppermute only.
A program may use at most 64 MiB of HBM per device.

v0:
```python
import jax
import jax.numpy as jnp
from jax import lax
from jax.sharding import PartitionSpec as P

RELAX_WEIGHT = 2.0 / 3.0
PAIR_LIST = ((0, 0), (0, 1), (0, 2), (0, 3), (1, 1), (1, 2), (1, 3), (2, 2), (2, 3), (3, 3))


def extended(array, sides, width):
    for axis, dim in sides:
        devices, length = (lax.axis_size(axis), array.shape[dim])
        up = [(i, (i + 1) % devices) for i in range(devices)]
        down = [(j, i) for i, j in up]
        last = lax.slice_in_dim(array, length - width, length, axis=dim)
        leading = lax.slice_in_dim(array, 0, width, axis=dim)
        before = lax.ppermute(last, axis, up)
        after = lax.ppermute(leading, axis, down)
        array = jnp.concatenate([before, array, after], axis=dim)
    return array


def from_behind(array, axis, by):
    devices = lax.axis_size(axis)
    return lax.ppermute(array, axis, [(i, (i + by) % devices) for i in range(devices)])


def sweep(values_ext, coef_ext):
    center_coef = coef_ext[1:-1, 1:-1]
    center_vals = values_ext[:, 1:-1, 1:-1]
    neighbours = [
        (coef_ext[2:, 1:-1], values_ext[:, 2:, 1:-1]),
        (coef_ext[:-2, 1:-1], values_ext[:, :-2, 1:-1]),
        (coef_ext[1:-1, 2:], values_ext[:, 1:-1, 2:]),
        (coef_ext[1:-1, :-2], values_ext[:, 1:-1, :-2]),
        (jnp.roll(center_coef, -1, axis=-1), jnp.roll(center_vals, -1, axis=-1)),
        (jnp.roll(center_coef, 1, axis=-1), jnp.roll(center_vals, 1, axis=-1)),
    ]
    diagonal = jnp.zeros_like(center_coef)
    fluxes = jnp.zeros_like(center_vals)
    for next_coef, next_vals in neighbours:
        weight = 2.0 * center_coef * next_coef / (center_coef + next_coef)
        diagonal = diagonal + weight
        fluxes = fluxes + weight * (center_vals - next_vals)
    return center_vals - RELAX_WEIGHT * fluxes / diagonal


def block_table(across):
    cells = jnp.arange(across) // 4
    return (cells[:, None] == jnp.arange(across // 4)[None, :]).astype(jnp.float32)


def pair_products(fields):
    return jnp.stack([fields[left_idx] * fields[right_idx] for left_idx, right_idx in PAIR_LIST])


def block_sums(values):
    number, layers, height, across = values.shape
    folded = values.reshape(number, layers // 4, 4, height // 4, 4, across).sum(axis=(2, 4))
    flat = jnp.dot(folded.reshape(-1, across), block_table(across), precision=lax.Precision.HIGHEST)
    return flat.reshape(number, layers // 4, height // 4, across // 4)


def spread_blocks(values, across):
    number, layers, height, blocks_x = values.shape
    flat = jnp.dot(
        values.reshape(-1, blocks_x), block_table(across).T, precision=lax.Precision.HIGHEST
    )
    spread = flat.reshape(number, layers, height, across)
    spread = jnp.repeat(spread, 4, axis=1)
    return jnp.repeat(spread, 4, axis=2)


def factor(blocks, grams):
    matrix = [[None] * 4 for _ in range(4)]
    for position, pair in enumerate(PAIR_LIST):
        matrix[pair[0]][pair[1]] = grams[position]
    trace = matrix[0][0] + matrix[1][1] + matrix[2][2] + matrix[3][3]
    ridge = 0.64 * (trace / 256.0 + 1e-06)
    upper = [[None] * 4 for _ in range(4)]
    for row_index in range(4):
        for col_index in range(row_index, 4):
            accum = matrix[row_index][col_index]
            if row_index == col_index:
                accum = accum + ridge
            for inner_index in range(row_index):
                accum = accum - upper[inner_index][row_index] * upper[inner_index][col_index]
            if row_index == col_index:
                upper[row_index][row_index] = jnp.sqrt(accum)
            else:
                upper[row_index][col_index] = accum / upper[row_index][row_index]
    listed = jnp.stack([upper[pair[0]][pair[1]] for pair in PAIR_LIST])
    inverse_list = jnp.stack(
        [
            1.0 / upper[pair[0]][pair[1]] if pair[0] == pair[1] else upper[pair[0]][pair[1]]
            for pair in PAIR_LIST
        ]
    )
    spread = spread_blocks(inverse_list, blocks.shape[3])
    lookup = {}
    for position, pair in enumerate(PAIR_LIST):
        lookup[pair] = spread[position]
    columns = []
    for col_index in range(4):
        accum = blocks[col_index]
        for inner_index in range(col_index):
            accum = accum - lookup[inner_index, col_index] * columns[inner_index]
        columns.append(accum * lookup[col_index, col_index])
    return (jnp.stack(columns), listed)


def factorize(region, scales):
    scaled = region * scales[:, None, None, None]
    grams = block_sums(pair_products(scaled))
    return factor(scaled, grams)


def body(test_vectors, conductivity):
    stacked = jnp.concatenate((test_vectors, conductivity[None]), axis=0)
    padded = extended(stacked, (("gz", 1), ("gy", 2)), 1)
    coef_ext = padded[4]
    first = sweep(padded[:4], coef_ext)
    second_pad = extended(first, (("gz", 1), ("gy", 2)), 1)
    relaxed = sweep(second_pad, coef_ext)
    squares = jnp.sum(relaxed * relaxed, axis=(1, 2, 3))
    cell_total = (
        relaxed.shape[1]
        * lax.axis_size("gz")
        * relaxed.shape[2]
        * lax.axis_size("gy")
        * relaxed.shape[3]
    )
    totals = lax.psum(squares, ("gz", "gy"))
    scales = lax.rsqrt(totals / cell_total + 1e-06)
    rolled = jnp.roll(relaxed, -2, axis=3)
    lead_planes = from_behind(rolled[:, :2], "gz", -1)
    z_region = jnp.concatenate((rolled[:, 2:], lead_planes), axis=1)
    lead_rows = from_behind(z_region[:, :, :2], "gy", -1)
    region = jnp.concatenate((z_region[:, :, 2:], lead_rows), axis=2)
    prolong_ext, factors = factorize(region, scales)
    back_rows = from_behind(prolong_ext[:, :, -2:], "gy", 1)
    y_cells = jnp.concatenate((back_rows, prolong_ext[:, :, :-2]), axis=2)
    back_planes = from_behind(y_cells[:, -2:], "gz", 1)
    cells = jnp.concatenate((back_planes, y_cells[:, :-2]), axis=1)
    return (jnp.roll(cells, 2, axis=3), factors)


def solution(mesh):
    return jax.shard_map(
        body,
        mesh=mesh,
        in_specs=(P(None, "gz", "gy", None), P("gz", "gy", None)),
        out_specs=(P(None, "gz", "gy", None), P(None, "gz", "gy", None)),
        check_vma=False,
    )
```

profile of v0, /device:TPU:0, one launch (start us, length us, event | category | flops | bytes accessed | tf_op | source)
XLA Modules:
  0.0 177.1 jit_solution(12672440913896904453)
XLA Ops:
  0.6 1.4 pad_maximum_fusion.31
  2.1 3.0 %collective-permute-start = (f32[5,1,96,256]{3,2,1,0:T(8,128)S(1)}, f32[5,1,96,256]{3,2,1,0:T(8,128)S(1)}, u32[]{:S(2)}, u32[]{:S(2)}) collective-permute-start(f32[5,1,96,256]{3,2,1,0:T(8,128)S(1)} %get-tuple-element.33), channel_id=1, source_target_pairs={{0,4},{4,8},{8,12},{12,16},{16,20},{20,24},{24,28},{28,0},{1,5},{5... | collective-permute-start | bytes 1474568 | tf_op jit(solution)/shard_map/ppermute | solution.py:17
  5.1 3.1 %collective-permute-start.1 = (f32[5,1,96,256]{3,2,1,0:T(8,128)S(1)}, f32[5,1,96,256]{3,2,1,0:T(8,128)S(1)}, u32[]{:S(2)}, u32[]{:S(2)}) collective-permute-start(f32[5,1,96,256]{3,2,1,0:T(8,128)S(1)} %get-tuple-element.34), channel_id=1, source_target_pairs={{4,0},{8,4},{12,8},{16,12},{20,16},{24,20},{28,24},{0,28},{5,1},{9... | collective-permute-start | bytes 1474568 | tf_op jit(solution)/shard_map/ppermute | solution.py:18
  8.2 0.6 fusion.61
  8.8 17.3 %collective-permute-done = f32[5,1,96,256]{3,2,1,0:T(8,128)S(1)} collective-permute-done((f32[5,1,96,256]{3,2,1,0:T(8,128)S(1)}, f32[5,1,96,256]{3,2,1,0:T(8,128)S(1)}, u32[]{:S(2)}, u32[]{:S(2)}) %collective-permute-start) | collective-permute-done | bytes 491552 | tf_op jit(solution)/shard_map/ppermute | solution.py:17
  26.1 2.2 %collective-permute-done.1 = f32[5,1,96,256]{3,2,1,0:T(8,128)S(1)} collective-permute-done((f32[5,1,96,256]{3,2,1,0:T(8,128)S(1)}, f32[5,1,96,256]{3,2,1,0:T(8,128)S(1)}, u32[]{:S(2)}, u32[]{:S(2)}) %collective-permute-start.1) | collective-permute-done | bytes 491552 | tf_op jit(solution)/shard_map/ppermute | solution.py:18
  28.4 1.7 collective-permute-start.3
  30.2 0.3 fusion.60
  30.4 1.3 collective-permute-done.2
  31.8 0.2 fusion.63
  32.0 0.1 fusion.62
  32.1 0.5 add_add_fusion
  32.7 2.8 %fusion.25 = f32[4,4,96,256]{3,2,1,0:T(8,128)S(1)} fusion(f32[4,4,96,256]{3,2,1,0:T(8,128)S(1)} %copy-done, f32[5,6,1,256]{3,2,1,0:T(1,128)S(1)} %collective-permute-done.2, f32[5,1,96,256]{3,2,1,0:T(8,128)S(1)} %collective-permute-done.1, f32[5,1,96,256]{3,2,1,0:T(8,128)S(1)} %collective-permute-done, f32[1,4,96,256]{3,2,1,0:T(8,128)S(1)} %bitcast.72, ...), kind=kLoop, calls=%fused_computation.39 | loop fusion | flops 13369344 | bytes 10481664 | tf_op jit(solution)/shard_map/sub | solution.py:45
  35.5 3.4 %collective-permute-start.4 = (f32[4,1,96,256]{3,2,1,0:T(8,128)S(1)}, f32[4,1,96,256]{3,2,1,0:T(8,128)S(1)}, u32[]{:S(2)}, u32[]{:S(2)}) collective-permute-start(f32[4,1,96,256]{3,2,1,0:T(8,128)S(1)} %get-tuple-element.48), channel_id=1, source_target_pairs={{4,0},{8,4},{12,8},{16,12},{20,16},{24,20},{28,24},{0,28},{5,1},{9... | collective-permute-start | bytes 1179656 | tf_op jit(solution)/shard_map/ppermute | solution.py:18
  38.9 0.5 fusion.58
  39.4 16.0 %collective-permute-done.4 = f32[4,1,96,256]{3,2,1,0:T(8,128)S(1)} collective-permute-done((f32[4,1,96,256]{3,2,1,0:T(8,128)S(1)}, f32[4,1,96,256]{3,2,1,0:T(8,128)S(1)}, u32[]{:S(2)}, u32[]{:S(2)}) %collective-permute-start.4) | collective-permute-done | bytes 393248 | tf_op jit(solution)/shard_map/ppermute | solution.py:18
  55.4 1.2 collective-permute-start.6
  56.6 0.3 fusion.59
  56.9 1.2 collective-permute-done.6
  58.1 1.7 collective-permute-done.7
  59.9 3.1 %multiply_reduce_fusion = (f32[4]{0:T(128)S(1)}, f32[4,4,96,256]{3,2,1,0:T(8,128)S(1)}) fusion(f32[4,4,96,256]{3,2,1,0:T(8,128)S(1)} %fusion.25, f32[4,96,256]{2,1,0:T(8,128)S(1)} %get-tuple-element.20, f32[4,4,96,255]{3,2,1,0:T(8,128)S(1)} %get-tuple-element.50, f32[4,4,96,1]{3,2,1,0:T(8,128)S(1)} %get-tuple-element.52, ...), kind=kLoop, calls=%fused_computation.72 | loop fusion | flops 12582908 | bytes 9879568 | tf_op jit(solution)/shard_map/reduce_sum | solution.py:125
  63.0 0.5 slice.419
  63.5 0.3 fusion.39
  63.8 4.5 %collective-permute-start.8 = (f32[4,2,96,256]{3,2,1,0:T(8,128)S(1)}, f32[4,2,96,256]{3,2,1,0:T(8,128)S(1)}, u32[]{:S(2)}, u32[]{:S(2)}) collective-permute-start(f32[4,2,96,256]{3,2,1,0:T(8,128)S(1)} %get-tuple-element.30), channel_id=1, source_target_pairs={{0,28},{4,0},{8,4},{12,8},{16,12},{20,16},{24,20},{28,24},{1,29},{... | collective-permute-start | bytes 2359304 | tf_op jit(solution)/shard_map/ppermute | solution.py:25
  68.3 51.8 %psum.7 = f32[4]{0:T(128)S(1)} all-reduce(f32[4]{0:T(128)S(1)} %get-tuple-element.18), channel_id=1, replica_groups=mesh['gz'=8,'gy'=4] {'gz','gy'}, use_global_device_ids=true, to_apply=%region_1.2 | all-reduce | flops 4 | bytes 32 | tf_op jit(solution)/shard_map/psum | solution.py:133
  120.1 0.2 collective-permute-start.9
  120.4 0.1 slice_maximum_fusion
  120.5 1.5 collective-permute-done.9
  122.0 0.2 maximum_multiply_fusion
  122.2 1.6 slice_multiply_fusion
  123.8 1.1 stack.94
  124.9 0.8 constant_dynamic-update-slice_fusion.9
  125.6 1.9 %stack.95 = f32[1,1,4,24,4,256]{5,4,3,2,1,0:T(4,128)} reshape(f32[1,4,96,256]{3,2,1,0:T(8,128)} %get-tuple-element.45) | data formatting | bytes 786432 | tf_op jit(solution)/shard_map/stack | solution.py:54
  127.5 1.9 %stack.96 = f32[1,1,4,24,4,256]{5,4,3,2,1,0:T(4,128)} reshape(f32[1,4,96,256]{3,2,1,0:T(8,128)} %get-tuple-element.44) | data formatting | bytes 786432 | tf_op jit(solution)/shard_map/stack | solution.py:54
  129.4 1.9 %stack.97 = f32[1,1,4,24,4,256]{5,4,3,2,1,0:T(4,128)} reshape(f32[1,4,96,256]{3,2,1,0:T(8,128)} %get-tuple-element.43) | data formatting | bytes 786432 | tf_op jit(solution)/shard_map/stack | solution.py:54
  131.3 0.9 stack.98
  132.1 0.1 stack.99
  132.3 0.1 stack.100
  132.4 0.1 stack.101
  132.5 0.1 stack.102
  132.6 1.1 stack.103
  133.7 1.8 %constant_dynamic-update-slice_fusion.8 = f32[10,1,4,24,4,256]{5,4,3,2,1,0:T(4,128)} fusion(f32[10,1,4,24,4,256]{5,4,3,2,1,0:T(4,128)} %constant_dynamic-update-slice_fusion.9, f32[1,1,4,24,4,256]{5,4,3,2,1,0:T(4,128)} %stack.95), kind=kLoop, calls=%fused_computation.120 | loop fusion | bytes 786432
  135.6 1.8 %constant_dynamic-update-slice_fusion.7 = f32[10,1,4,24,4,256]{5,4,3,2,1,0:T(4,128)} fusion(f32[10,1,4,24,4,256]{5,4,3,2,1,0:T(4,128)} %constant_dynamic-update-slice_fusion.8, f32[1,1,4,24,4,256]{5,4,3,2,1,0:T(4,128)} %stack.96), kind=kLoop, calls=%fused_computation.119 | loop fusion | bytes 786432
  137.4 0.8 constant_dynamic-update-slice_fusion.6
  138.2 0.8 constant_dynamic-update-slice_fusion.5
  138.9 0.8 constant_dynamic-update-slice_fusion.4
  139.7 0.8 constant_dynamic-update-slice_fusion.3
  140.5 0.8 constant_dynamic-update-slice_fusion.2
  141.3 0.8 constant_dynamic-update-slice_fusion.1
  142.0 0.8 constant_dynamic-update-slice_fusion
  142.8 3.3 %reduce_sum.19 = f32[10,24,256]{2,1,0:T(8,128)S(1)} reduce(f32[10,1,4,24,4,256]{5,4,3,2,1,0:T(4,128)} %constant_dynamic-update-slice_fusion, f32[]{:T(128)} %constant.28.clone.1), dimensions={1,2,4}, to_apply=%region_2.3 | reduce | flops 921600 | bytes 4177924 | tf_op jit(solution)/shard_map/reduce_sum | solution.py:59
  146.1 0.3 fusion.44
  146.4 0.2 divide_bitcast_fusion
  147.7 0.2 fusion.41
  148.7 0.1 subtract_multiply_fusion.1
  148.9 0.2 subtract_multiply_fusion
  149.1 2.4 %collective-permute-start.10 = (f32[4,4,2,256]{3,2,1,0:T(2,128)S(1)}, f32[4,4,2,256]{3,2,1,0:T(2,128)S(1)}, u32[]{:S(2)}, u32[]{:S(2)}) collective-permute-start(f32[4,4,2,256]{3,2,1,0:T(2,128)S(1)} %pad_maximum_fusion.34), channel_id=1, source_target_pairs={{0,1},{1,2},{2,3},{3,0},{4,5},{5,6},{6,7},{7,4},{8,9},{9,10},{10,1... | collective-permute-start | bytes 98312 | tf_op jit(solution)/shard_map/ppermute | solution.py:25
  151.5 1.0 collective-permute-done.10
  152.4 0.1 fusion.1
  152.6 0.1 fusion.56
  152.7 2.3 %collective-permute-start.11 = (f32[4,2,96,256]{3,2,1,0:T(8,128)S(1)}, f32[4,2,96,256]{3,2,1,0:T(8,128)S(1)}, u32[]{:S(2)}, u32[]{:S(2)}) collective-permute-start(f32[4,2,96,256]{3,2,1,0:T(8,128)S(1)} %get-tuple-element.35), channel_id=1, source_target_pairs={{0,4},{4,8},{8,12},{12,16},{16,20},{20,24},{24,28},{28,0},{1,5},{5... | collective-permute-start | bytes 2359304 | tf_op jit(solution)/shard_map/ppermute | solution.py:25
  155.1 20.1 %collective-permute-done.11 = f32[4,2,96,256]{3,2,1,0:T(8,128)S(1)} collective-permute-done((f32[4,2,96,256]{3,2,1,0:T(8,128)S(1)}, f32[4,2,96,256]{3,2,1,0:T(8,128)S(1)}, u32[]{:S(2)}, u32[]{:S(2)}) %collective-permute-start.11) | collective-permute-done | bytes 786464 | tf_op jit(solution)/shard_map/ppermute | solution.py:25
  175.2 0.3 fusion.38
  175.4 1.6 fusion
  (77 shorter events, 2.0 us)
Async XLA Ops:
  0.6 7.6 %copy-start = (f32[4,4,96,256]{3,2,1,0:T(8,128)S(1)}, f32[4,4,96,256]{3,2,1,0:T(8,128)}, u32[]{:S(2)}) copy-start(f32[4,4,96,256]{3,2,1,0:T(8,128)} %param.2) | copy-start | bytes 4718596
  2.1 24.0 %collective-permute-start = (f32[5,1,96,256]{3,2,1,0:T(8,128)S(1)}, f32[5,1,96,256]{3,2,1,0:T(8,128)S(1)}, u32[]{:S(2)}, u32[]{:S(2)}) collective-permute-start(f32[5,1,96,256]{3,2,1,0:T(8,128)S(1)} %get-tuple-element.33), channel_id=1, source_target_pairs={{0,4},{4,8},{8,12},{12,16},{16,20},{20,24},{24,28},{28,0},{1,5},{5... | collective-permute-start | bytes 1474568 | tf_op jit(solution)/shard_map/ppermute | solution.py:17
  5.1 23.2 %copy-start.1 = (f32[4,96,256]{2,1,0:T(8,128)S(1)}, f32[4,96,256]{2,1,0:T(8,128)}, u32[]{:S(2)}) copy-start(f32[4,96,256]{2,1,0:T(8,128)} %param.3) | copy-start | bytes 1179652
  5.1 23.2 %collective-permute-start.1 = (f32[5,1,96,256]{3,2,1,0:T(8,128)S(1)}, f32[5,1,96,256]{3,2,1,0:T(8,128)S(1)}, u32[]{:S(2)}, u32[]{:S(2)}) collective-permute-start(f32[5,1,96,256]{3,2,1,0:T(8,128)S(1)} %get-tuple-element.34), channel_id=1, source_target_pairs={{4,0},{8,4},{12,8},{16,12},{20,16},{24,20},{28,24},{0,28},{5,1},{9... | collective-permute-start | bytes 1474568 | tf_op jit(solution)/shard_map/ppermute | solution.py:18
  28.4 3.4 %collective-permute-start.2 = (f32[5,6,1,256]{3,2,1,0:T(1,128)S(1)}, f32[5,6,1,256]{3,2,1,0:T(1,128)S(1)}, u32[]{:S(2)}, u32[]{:S(2)}) collective-permute-start(f32[5,6,1,256]{3,2,1,0:T(1,128)S(1)} %get-tuple-element.28), channel_id=1, source_target_pairs={{0,1},{1,2},{2,3},{3,0},{4,5},{5,6},{6,7},{7,4},{8,9},{9,10},{10,1... | collective-permute-start | bytes 92168 | tf_op jit(solution)/shard_map/ppermute | solution.py:17
  28.4 3.3 %collective-permute-start.3 = (f32[5,6,1,256]{3,2,1,0:T(1,128)S(1)}, f32[5,6,1,256]{3,2,1,0:T(1,128)S(1)}, u32[]{:S(2)}, u32[]{:S(2)}) collective-permute-start(f32[5,6,1,256]{3,2,1,0:T(1,128)S(1)} %get-tuple-element.27), channel_id=1, source_target_pairs={{1,0},{2,1},{3,2},{0,3},{5,4},{6,5},{7,6},{4,7},{9,8},{10,9},{11,1... | collective-permute-start | bytes 92168 | tf_op jit(solution)/shard_map/ppermute | solution.py:18
  35.5 19.9 %collective-permute-start.4 = (f32[4,1,96,256]{3,2,1,0:T(8,128)S(1)}, f32[4,1,96,256]{3,2,1,0:T(8,128)S(1)}, u32[]{:S(2)}, u32[]{:S(2)}) collective-permute-start(f32[4,1,96,256]{3,2,1,0:T(8,128)S(1)} %get-tuple-element.48), channel_id=1, source_target_pairs={{4,0},{8,4},{12,8},{16,12},{20,16},{24,20},{28,24},{0,28},{5,1},{9... | collective-permute-start | bytes 1179656 | tf_op jit(solution)/shard_map/ppermute | solution.py:18
  38.9 16.5 %collective-permute-start.5 = (f32[4,1,96,256]{3,2,1,0:T(8,128)S(1)}, f32[4,1,96,256]{3,2,1,0:T(8,128)S(1)}, u32[]{:S(2)}, u32[]{:S(2)}) collective-permute-start(f32[4,1,96,256]{3,2,1,0:T(8,128)S(1)} %get-tuple-element.47), channel_id=1, source_target_pairs={{0,4},{4,8},{8,12},{12,16},{16,20},{20,24},{24,28},{28,0},{1,5},{5... | collective-permute-start | bytes 1179656 | tf_op jit(solution)/shard_map/ppermute | solution.py:17
  55.4 2.7 %collective-permute-start.6 = (f32[4,6,1,256]{3,2,1,0:T(1,128)S(1)}, f32[4,6,1,256]{3,2,1,0:T(1,128)S(1)}, u32[]{:S(2)}, u32[]{:S(2)}) collective-permute-start(f32[4,6,1,256]{3,2,1,0:T(1,128)S(1)} %get-tuple-element.31), channel_id=1, source_target_pairs={{1,0},{2,1},{3,2},{0,3},{5,4},{6,5},{7,6},{4,7},{9,8},{10,9},{11,1... | collective-permute-start | bytes 73736 | tf_op jit(solution)/shard_map/ppermute | solution.py:18
  56.6 3.3 %collective-permute-start.7 = (f32[4,6,1,256]{3,2,1,0:T(1,128)S(1)}, f32[4,6,1,256]{3,2,1,0:T(1,128)S(1)}, u32[]{:S(2)}, u32[]{:S(2)}) collective-permute-start(f32[4,6,1,256]{3,2,1,0:T(1,128)S(1)} %get-tuple-element.32), channel_id=1, source_target_pairs={{0,1},{1,2},{2,3},{3,0},{4,5},{5,6},{6,7},{7,4},{8,9},{9,10},{10,1... | collective-permute-start | bytes 73736 | tf_op jit(solution)/shard_map/ppermute | solution.py:17
  63.8 56.3 %collective-permute-start.8 = (f32[4,2,96,256]{3,2,1,0:T(8,128)S(1)}, f32[4,2,96,256]{3,2,1,0:T(8,128)S(1)}, u32[]{:S(2)}, u32[]{:S(2)}) collective-permute-start(f32[4,2,96,256]{3,2,1,0:T(8,128)S(1)} %get-tuple-element.30), channel_id=1, source_target_pairs={{0,28},{4,0},{8,4},{12,8},{16,12},{20,16},{24,20},{28,24},{1,29},{... | collective-permute-start | bytes 2359304 | tf_op jit(solution)/shard_map/ppermute | solution.py:25
  120.1 1.8 %collective-permute-start.9 = (f32[4,4,2,256]{3,2,1,0:T(2,128)S(1)}, f32[4,4,2,256]{3,2,1,0:T(2,128)S(1)}, u32[]{:S(2)}, u32[]{:S(2)}) collective-permute-start(f32[4,4,2,256]{3,2,1,0:T(2,128)S(1)} %pad_maximum_fusion.35), channel_id=1, source_target_pairs={{0,3},{1,0},{2,1},{3,2},{4,7},{5,4},{6,5},{7,6},{8,11},{9,8},{10,9... | collective-permute-start | bytes 98312 | tf_op jit(solution)/shard_map/ppermute | solution.py:25
  125.6 5.6 %copy-start.4 = (f32[1,4,96,256]{3,2,1,0:T(8,128)S(1)}, f32[1,4,96,256]{3,2,1,0:T(8,128)}, u32[]{:S(2)}) copy-start(f32[1,4,96,256]{3,2,1,0:T(8,128)} %get-tuple-element.38) | copy-start | bytes 1179652
  133.7 3.7 %copy-start.3 = (f32[1,1,4,24,4,256]{5,4,3,2,1,0:T(4,128)S(1)}, f32[1,1,4,24,4,256]{5,4,3,2,1,0:T(4,128)}, u32[]{:S(2)}) copy-start(f32[1,1,4,24,4,256]{5,4,3,2,1,0:T(4,128)} %stack.97) | copy-start | bytes 1179652
  133.7 4.4 %copy-start.2 = (f32[1,1,4,24,4,256]{5,4,3,2,1,0:T(4,128)S(1)}, f32[1,1,4,24,4,256]{5,4,3,2,1,0:T(4,128)}, u32[]{:S(2)}) copy-start(f32[1,1,4,24,4,256]{5,4,3,2,1,0:T(4,128)} %stack.98) | copy-start | bytes 1179652
  149.1 3.4 %collective-permute-start.10 = (f32[4,4,2,256]{3,2,1,0:T(2,128)S(1)}, f32[4,4,2,256]{3,2,1,0:T(2,128)S(1)}, u32[]{:S(2)}, u32[]{:S(2)}) collective-permute-start(f32[4,4,2,256]{3,2,1,0:T(2,128)S(1)} %pad_maximum_fusion.34), channel_id=1, source_target_pairs={{0,1},{1,2},{2,3},{3,0},{4,5},{5,6},{6,7},{7,4},{8,9},{9,10},{10,1... | collective-permute-start | bytes 98312 | tf_op jit(solution)/shard_map/ppermute | solution.py:25
  152.7 22.4 %collective-permute-start.11 = (f32[4,2,96,256]{3,2,1,0:T(8,128)S(1)}, f32[4,2,96,256]{3,2,1,0:T(8,128)S(1)}, u32[]{:S(2)}, u32[]{:S(2)}) collective-permute-start(f32[4,2,96,256]{3,2,1,0:T(8,128)S(1)} %get-tuple-element.35), channel_id=1, source_target_pairs={{0,4},{4,8},{8,12},{12,16},{16,20},{20,24},{24,28},{28,0},{1,5},{5... | collective-permute-start | bytes 2359304 | tf_op jit(solution)/shard_map/ppermute | solution.py:25
  155.1 22.0 %copy-start.5 = (f32[10,1,24,64]{3,2,1,0:T(8,128)}, f32[10,1,24,64]{3,2,1,0:T(8,128)S(1)}, u32[]{:S(2)}) copy-start(f32[10,1,24,64]{3,2,1,0:T(8,128)S(1)} %constant_dynamic-update-slice_fusion.20) | copy-start | bytes 184324
where the time goes:
time: 178 us; the launch traced here: 177 us
  waiting for transfers between devices  62.2 us (35%)
  blocking collectives  51.8 us (29%)
  local copies, waits for them, and re-layouts  23.2 us (13%)
  starting transfers between devices  22 us (12%)
  other arithmetic  16.1 us (9%)
    psum x1, blocking collectives, body(): totals = lax.psum(squares, ('gz', 'gy'))  51.8 us
    ppermute x4, waiting for transfers between devices, from_behind(): lax.ppermute(array, axis, [(i, (i + by) % devices) for i in range(devices)])  22.5 us
    ppermute x4, waiting for transfers between devices, extended(): before = lax.ppermute(last, axis, up)  20.4 us
    ppermute x4, waiting for transfers between devices, extended(): after = lax.ppermute(leading, axis, down)  19.4 us
    another operation x11, local copies, waits for them, and re-layouts, pair_products(): jnp.stack([fields[left_idx] * fields[right_idx] for left_idx, right_idx i...  9.93 us
    ppermute x4, starting transfers between devices, from_behind(): lax.ppermute(array, axis, [(i, (i + by) % devices) for i in range(devices)])  9.51 us
    ppermute x4, starting transfers between devices, extended(): after = lax.ppermute(leading, axis, down)  9.4 us
    unnamed x32, local copies, waits for them, and re-layouts  9.12 us
  transfers between devices with their start and end apart: 12, of which 9 were waited for; matrix products, arithmetic and copies ran while one was open for 1% of the time, Pallas kernels for 0%

commit v1 on v0

v1 whole, which is shorter than its diff:
```python
import functools
import jax
import jax.numpy as jnp
from jax import lax
from jax.experimental import pallas as pl
from jax.experimental.pallas import tpu as pltpu
from jax.sharding import PartitionSpec as P

RELAX_WEIGHT = 2.0 / 3.0
PAIRS = ((0, 0), (0, 1), (0, 2), (0, 3), (1, 1), (1, 2), (1, 3), (2, 2), (2, 3), (3, 3))
AT = {pair: k for k, pair in enumerate(PAIRS)}
BLOCK = 4
EDGE = 8
VMEM_LIMIT = 40 * 1024 * 1024


def call(body, ins, outs, scratch=(), flops=0):
    names_in, names_out = list(ins), list(outs)

    def kernel(*refs):
        cut = len(names_in) + len(names_out)
        body(dict(zip(names_in, refs)), dict(zip(names_out, refs[len(names_in) :])), *refs[cut:])

    got = pl.pallas_call(
        kernel,
        out_shape=[jax.ShapeDtypeStruct(outs[k], jnp.float32) for k in names_out],
        in_specs=[pl.BlockSpec(memory_space=pltpu.VMEM)] * len(names_in),
        out_specs=[pl.BlockSpec(memory_space=pltpu.VMEM)] * len(names_out),
        scratch_shapes=list(scratch),
        compiler_params=pltpu.CompilerParams(vmem_limit_bytes=VMEM_LIMIT),
        cost_estimate=pl.CostEstimate(flops=flops, bytes_accessed=flops, transcendentals=0),
        name=body.__name__,
    )(*[ins[k] for k in names_in])
    return dict(zip(names_out, got))


def parity():
    return lax.rem(lax.axis_index("gz"), 2)


def natural(k, odd, planes):
    return k + odd * (planes - 1 - 2 * k)


def half_of_tile(shape):
    return lax.broadcasted_iota(jnp.int32, shape, 0) // BLOCK


def source(i, f, k, start, size, odd):
    planes = i["coef"].shape[0]
    rows = pl.ds(pl.multiple_of(start, 8), size)
    if f == i["tv"].shape[0]:
        return i["coef"][natural(k, odd, planes), rows, :]
    return i["tv"][f, natural(k, odd, planes), rows, :]


def pack_send(i, o):
    odd = parity()
    fields, planes, rows, width = i["tv"].shape
    half = rows // 2
    for k in range(2):
        for f in range(fields + 1):
            o["far"][k, f] = source(i, f, k, (1 - odd) * half, half, odd)
    which = half_of_tile((EDGE, width))
    for name, start, side in (
        ("extra", half - EDGE * (1 - odd), 1 - odd),
        ("halo", (rows - EDGE) * (1 - odd), 1 - odd),
        ("cross", (rows - EDGE) * odd, odd),
    ):
        for q in range(planes // 2):
            for f in range(fields + 1):
                u = source(i, f, 2 * q, start, EDGE, odd)
                v = source(i, f, 2 * q + 1, start, EDGE, odd)
                o[name][q, f] = jnp.where(which == side, u, pltpu.roll(v, BLOCK, 0))


def pack_keep(i, o):
    odd = parity()
    fields, planes, rows, width = i["tv"].shape
    half = rows // 2
    for k in range(planes):
        for f in range(fields + 1):
            o["far" if k < 2 else "near"][k % 2, f] = source(i, f, k, odd * half, half, odd)
            if k >= 2:
                o["send"][k % 2, f] = source(i, f, k, (1 - odd) * half, half, odd)


def edges(i, o):
    odd = parity()
    fields, planes, rows, width = i["tv"].shape
    half = rows // 2
    which = half_of_tile((EDGE, width))
    for k in range(planes):
        for f in range(fields + 1):

            def unpack(ref):
                tile = ref[k // 2, f]
                return tile if k % 2 == 0 else pltpu.roll(tile, BLOCK, 0)

            own = source(i, f, k, half - EDGE * odd, EDGE, odd)
            o["own_far" if k < 2 else "own_near"][k % 2, f] = jnp.where(which == odd, own, unpack(i["halo"]))
            o["par_far" if k < 2 else "par_near"][k % 2, f] = jnp.where(
                which == odd, unpack(i["extra"]), unpack(i["cross"])
            )


def inverse(x):
    guess = pl.reciprocal(x, approx=True)
    return guess * (2.0 - x * guess)


def onward(x, axis):
    return pltpu.roll(x, x.shape[axis] - 1, axis)


def backward(x, axis):
    return pltpu.roll(x, 1, axis)


def joint(a, b):
    return a * b * inverse(a + b)


def weigh(before, here, after, c):
    wx = joint(here, onward(here, 1))
    wy = joint(here, onward(here, 0))
    wm = joint(here, before)
    wp = joint(here, after)
    c[0] = wx
    c[1] = wy
    c[2] = wm
    c[3] = wp
    c[4] = RELAX_WEIGHT * inverse(wx + backward(wx, 1) + wy + backward(wy, 0) + wm + wp)


def step(before, here, after, c):
    fx = c[0] * (here - onward(here, 1))
    fy = c[1] * (here - onward(here, 0))
    flux = (fx - backward(fx, 1)) + (fy - backward(fy, 0))
    flux = flux + c[2] * (here - before) + c[3] * (here - after)
    return here - c[4] * flux


def window(keep, edge, at):
    return lambda f: jnp.concatenate([keep[at, f], edge[at, f]], axis=0)


def sweep_first(planes, z, c, out):
    last = 4
    weigh(planes[z - 1](last), planes[z](last), planes[z + 1](last), c)
    for f in range(last):
        out[f] = step(planes[z - 1](f), planes[z](f), planes[z + 1](f), c)


def sweep_second(first, z, c, keep, edge, at):
    half = keep.shape[2]
    for f in range(first[z].shape[0]):
        value = step(first[z - 1][f], first[z][f], first[z + 1][f], c)
        keep[at, f] = value[:half]
        edge[at, f] = value[half:]


def early(i, o):
    planes = {k: window(i["far"], i["far_edge"], k) for k in (0, 1)}
    planes |= {k + 2: window(i["near"], i["near_edge"], k) for k in (0, 1)}
    sweep_first(planes, 1, o["c1"], o["f1"])
    sweep_first(planes, 2, o["c2"], o["f2"])


def outer(i, o, c8):
    planes = {7 - k: window(i["far"], i["far_edge"], k) for k in (0, 1)}
    planes |= {8 + k: window(i["next"], i["next_edge"], k) for k in (0, 1)}
    sweep_first(planes, 7, o["c7"], o["f7"])
    sweep_first(planes, 8, c8, o["f8"])


def inner_far(i, o, c6):
    planes = {7 - k: window(i["far"], i["far_edge"], k) for k in (0, 1)}
    planes |= {5 - k: window(i["near"], i["near_edge"], k) for k in (0, 1)}
    sweep_first(planes, 6, c6, o["f6"])
    sweep_first(planes, 5, o["c5"], o["f5"])
    first = {5: o["f5"], 6: o["f6"], 7: i["f7"], 8: i["f8"]}
    sweep_second(first, 7, i["c7"], o["rel"], o["rel_edge"], 0)
    sweep_second(first, 6, c6, o["rel"], o["rel_edge"], 1)


def inner_near(i, o, c4):
    planes = {2 + k: window(i["own"], i["own_edge"], k) for k in (0, 1)}
    planes |= {5 - k: window(i["near"], i["near_edge"], k) for k in (0, 1)}
    sweep_first(planes, 4, c4, o["f4"])
    sweep_first(planes, 3, o["c3"], o["f3"])
    first = {3: o["f3"], 4: o["f4"], 5: i["f5"], 6: i["f6"]}
    sweep_second(first, 5, i["c5"], o["rel"], o["rel_edge"], 0)
    sweep_second(first, 4, c4, o["rel"], o["rel_edge"], 1)


def split(x):
    high = x.astype(jnp.bfloat16)
    return high, (x - high.astype(jnp.float32)).astype(jnp.bfloat16)


def times_table(x, table):
    high, low = split(x)
    return jnp.dot(high, table, preferred_element_type=jnp.float32) + jnp.dot(
        low, table, preferred_element_type=jnp.float32
    )


def table_times(table, x):
    high, low = split(x)
    return jnp.dot(table, high, preferred_element_type=jnp.float32) + jnp.dot(
        table, low, preferred_element_type=jnp.float32
    )


def lane_table(width, transposed=False):
    shape = (width // BLOCK, width) if transposed else (width, width // BLOCK)
    cell = lax.broadcasted_iota(jnp.int32, shape, 1 if transposed else 0)
    block = lax.broadcasted_iota(jnp.int32, shape, 0 if transposed else 1)
    moved = jnp.where(cell < 2, cell + width - 2, cell - 2)
    return (moved // BLOCK == block).astype(jnp.bfloat16)


def row_table(half, groups):
    shape = (groups, half + EDGE)
    row = lax.broadcasted_iota(jnp.int32, shape, 1)
    block = lax.broadcasted_iota(jnp.int32, shape, 0)
    moved = jnp.where(row >= half + EDGE - 2, row - (half + EDGE - 2), row + 2)
    return ((moved // BLOCK == block) & (block <= half // BLOCK)).astype(jnp.bfloat16)


def group_count(half):
    return (half // BLOCK + 1 + 7) // 8 * 8


def grams(planes, out, sums, half):
    width = out.shape[-1] * BLOCK
    lanes, rows = lane_table(width), row_table(half, out.shape[1])
    for at, (a, b) in enumerate(PAIRS):
        total = None
        for keep, edge, k in planes:
            left = jnp.concatenate([keep[k, a], edge[k, a]], axis=0)
            right = left if a == b else jnp.concatenate([keep[k, b], edge[k, b]], axis=0)
            total = left * right if total is None else total + left * right
        if a == b:
            kept = jnp.sum(total[:half], axis=0, keepdims=True)
            sums[a : a + 1] = sums[a : a + 1] + kept[:, : width // 2] + kept[:, width // 2 :]
        out[at] = table_times(rows, times_table(total, lanes))


def middle(i, o):
    first = {k: i[f"f{k}"] for k in (1, 2, 3, 4)}
    sweep_second(first, 2, i["c2"], o["rel"], o["rel_edge"], 0)
    sweep_second(first, 3, i["c3"], o["rel"], o["rel_edge"], 1)
    half = o["rel"].shape[2]
    o["sums"][...] = jnp.zeros_like(o["sums"])
    near = [(o["rel"], o["rel_edge"], k) for k in (0, 1)] + [(i["pn"], i["pn_edge"], k) for k in (0, 1)]
    grams([(i["pf"], i["pf_edge"], k) for k in (0, 1)], o["gram"].at[0], o["sums"], half)
    grams(near, o["gram"].at[1], o["sums"], half)


def outmost(i, o, cm, c0, fm, f0):
    planes = {-1 - k: window(i["prev"], i["prev_edge"], k) for k in (0, 1)}
    planes |= {k: window(i["far"], i["far_edge"], k) for k in (0, 1)}
    sweep_first(planes, -1, cm, fm)
    sweep_first(planes, 0, c0, f0)
    first = {-1: fm, 0: f0, 1: i["f1"], 2: i["f2"]}
    sweep_second(first, 0, c0, o["rel"], o["rel_edge"], 0)
    sweep_second(first, 1, i["c1"], o["rel"], o["rel_edge"], 1)
    o["sums"][...] = i["sums"][...]
    grams([(o["rel"], o["rel_edge"], k) for k in (0, 1)], o["gram"], o["sums"], o["rel"].shape[2])


def finish(cells, i, o, spread):
    odd = parity()
    fields, planes, rows, width = o["prolong"].shape
    half = rows // 2
    totals = jnp.sum(jnp.sum(i["totals"][...], axis=0), axis=1, keepdims=True)
    scales = lax.rsqrt(totals / cells + 1e-06)
    scale = [jnp.broadcast_to(scales[f : f + 1], (1, 1)) for f in range(fields)]
    groups = i["own_far"].shape[1]
    matrix = {}
    for at, (a, b) in enumerate(PAIRS):
        stacked = jnp.concatenate(
            [
                i["own_far"][at] + i["same"][at],
                i["own"][1, at],
                i["other"][0, at] + i["cross"][at],
                i["other"][1, at],
            ],
            axis=0,
        )
        matrix[a, b] = stacked * (scale[a] * scale[b])
    trace = matrix[0, 0] + matrix[1, 1] + matrix[2, 2] + matrix[3, 3]
    ridge = 0.64 * (trace / 256.0 + 1e-06)
    upper, inv = {}, {}
    for a in range(fields):
        for b in range(a, fields):
            accum = matrix[a, b] + ridge if a == b else matrix[a, b]
            for c in range(a):
                accum = accum - upper[c, a] * upper[c, b]
            if a == b:
                upper[a, a] = jnp.sqrt(accum)
                inv[a] = 1.0 / upper[a, a]
            else:
                upper[a, b] = accum * inv[a]
    count = rows // BLOCK
    line = lax.broadcasted_iota(jnp.int32, (count, width // BLOCK), 0)
    lanes = lane_table(width, True)
    for at, (a, b) in enumerate(PAIRS):
        value = upper[a, b]
        part = [value[n * groups : (n + 1) * groups] for n in range(4)]
        pad = jnp.zeros((count - groups, width // BLOCK), jnp.float32)
        low = jnp.concatenate([jnp.where(odd == 0, part[1], part[2]), pad], axis=0)
        top = jnp.concatenate([jnp.where(odd == 0, part[3], part[0]), pad], axis=0)
        low, top = onward(low, 0), pltpu.roll(top, half // BLOCK - 1, 0)
        o["factors"][at, 0] = jnp.where(line < half // BLOCK, low, top)
        spread[at] = times_table(inv[a] if a == b else value, lanes)
    within = lax.broadcasted_iota(jnp.int32, (EDGE, width), 0)
    for side in range(2):
        start = (odd if side == 0 else 1 - odd) * half
        for pair in range(2):
            source_ref = i[("near" if pair else "far") if side == 0 else ("back_near" if pair else "back_far")]
            base = (2 * side + pair) * groups
            for tile in range(half // EDGE):
                entry = {}
                for at, key in enumerate(PAIRS):
                    three = [
                        jnp.broadcast_to(spread[at, pl.ds(base + 2 * tile + n, 1), :], (EDGE, width)) for n in range(3)
                    ]
                    entry[key] = jnp.where(within < 2, three[0], jnp.where(within < 6, three[1], three[2]))
                for k in range(2):
                    columns = []
                    for b in range(fields):
                        accum = source_ref[k, b, pl.ds(tile * EDGE, EDGE), :] * scale[b]
                        for a in range(b):
                            accum = accum - entry[a, b] * columns[a]
                        columns.append(accum * entry[b, b])
                        place = pl.ds(pl.multiple_of(start + tile * EDGE, 8), EDGE)
                        o["prolong"][b, natural(2 * pair + k, odd, planes), place, :] = columns[b]


def moved(x, even_by, odd_by):
    nz, ny = lax.axis_size("gz"), lax.axis_size("gy")
    route = []
    for z in range(nz):
        dz, dy = odd_by if z % 2 else even_by
        for y in range(ny):
            route.append((z * ny + y, (z + dz) % nz * ny + (y + dy) % ny))
    return lax.ppermute(x, ("gz", "gy"), route)


def body(tv, coef):
    fields, planes, rows, width = tv.shape
    half = rows // 2
    devices = lax.axis_size("gz") * lax.axis_size("gy")
    cells = devices * planes * rows * width
    groups = group_count(half)
    keep = (2, fields + 1, half, width)
    edge = (2, fields + 1, EDGE, width)
    tall = half + EDGE
    first, coefs = (fields, tall, width), (5, tall, width)
    rel, rel_edge = (2, fields, half, width), (2, fields, EDGE, width)
    gram = (len(PAIRS), groups, width // BLOCK)
    sums = (8, width // 2)

    send = call(pack_send, dict(tv=tv, coef=coef), dict(far=keep, extra=edge, halo=edge, cross=edge))
    par_far = moved(send["far"], (1, 0), (-1, 0))
    extra = moved(send["extra"], (1, 0), (-1, 0))
    cross = moved(send["cross"], (1, -1), (-1, 1))
    halo = moved(send["halo"], (0, 1), (0, -1))
    own = call(pack_keep, dict(tv=tv, coef=coef), dict(far=keep, near=keep, send=keep))
    par_near = moved(own["send"], (1, 0), (-1, 0))
    after = moved(own["far"], (-2, 0), (2, 0))
    e = call(
        edges,
        dict(tv=tv, coef=coef, extra=extra, halo=halo, cross=cross),
        dict(own_far=edge, own_near=edge, par_far=edge, par_near=edge),
    )
    after_edge = moved(e["own_far"], (-2, 0), (2, 0))
    before = moved(par_far, (2, 0), (-2, 0))
    before_edge = moved(e["par_far"], (2, 0), (-2, 0))
    a = call(
        early,
        dict(far=own["far"], far_edge=e["own_far"], near=own["near"], near_edge=e["own_near"]),
        dict(c1=coefs, c2=coefs, f1=first, f2=first),
    )
    b = call(
        outer,
        dict(far=par_far, far_edge=e["par_far"], next=after, next_edge=after_edge),
        dict(c7=coefs, f7=first, f8=first),
        [pltpu.VMEM(coefs, jnp.float32)],
    )
    far = call(
        inner_far,
        dict(far=par_far, far_edge=e["par_far"], near=par_near, near_edge=e["par_near"], **b),
        dict(c5=coefs, f5=first, f6=first, rel=rel, rel_edge=rel_edge),
        [pltpu.VMEM(coefs, jnp.float32)],
    )
    back_far = moved(far["rel"], (1, 0), (-1, 0))
    near = call(
        inner_near,
        dict(
            own=own["near"],
            own_edge=e["own_near"],
            near=par_near,
            near_edge=e["par_near"],
            c5=far["c5"],
            f5=far["f5"],
            f6=far["f6"],
        ),
        dict(c3=coefs, f3=first, f4=first, rel=rel, rel_edge=rel_edge),
        [pltpu.VMEM(coefs, jnp.float32)],
    )
    back_near = moved(near["rel"], (1, 0), (-1, 0))
    mid = call(
        middle,
        dict(
            f1=a["f1"],
            f2=a["f2"],
            f3=near["f3"],
            f4=near["f4"],
            c2=a["c2"],
            c3=near["c3"],
            pf=far["rel"],
            pf_edge=far["rel_edge"],
            pn=near["rel"],
            pn_edge=near["rel_edge"],
        ),
        dict(rel=rel, rel_edge=rel_edge, gram=(2,) + gram, sums=sums),
    )
    other = moved(mid["gram"], (1, 0), (-1, 0))
    same = moved(mid["gram"][0], (2, 0), (-2, 0))
    out = call(
        outmost,
        dict(
            prev=before,
            prev_edge=before_edge,
            far=own["far"],
            far_edge=e["own_far"],
            f1=a["f1"],
            f2=a["f2"],
            c1=a["c1"],
            sums=mid["sums"],
        ),
        dict(rel=rel, rel_edge=rel_edge, gram=gram, sums=sums),
        [pltpu.VMEM(coefs, jnp.float32)] * 2 + [pltpu.VMEM(first, jnp.float32)] * 2,
    )
    crossed = moved(out["gram"], (-1, 0), (1, 0))
    totals = lax.all_to_all(jnp.broadcast_to(out["sums"], (devices,) + sums), ("gz", "gy"), 0, 0)
    final = functools.partial(finish, float(cells))
    final.__name__ = "finish"
    done = call(
        final,
        dict(
            totals=totals,
            own_far=out["gram"],
            same=same,
            own=mid["gram"],
            other=other,
            cross=crossed,
            far=out["rel"],
            near=mid["rel"],
            back_far=back_far,
            back_near=back_near,
        ),
        dict(prolong=tv.shape, factors=(len(PAIRS), planes // BLOCK, rows // BLOCK, width // BLOCK)),
        [pltpu.VMEM((len(PAIRS), 4 * groups, width), jnp.float32)],
    )
    return done["prolong"], done["factors"]


def solution(mesh):
    return jax.shard_map(
        body,
        mesh=mesh,
        in_specs=(P(None, "gz", "gy", None), P("gz", "gy", None)),
        out_specs=(P(None, "gz", "gy", None), P(None, "gz", "gy", None)),
        check_vma=False,
    )
```

time: 178 us -> 74.1 us (0.42)
  blocking collectives: 51.8 us -> 0 us
  waiting for transfers between devices: 62.2 us -> 25.9 us
  local copies, waits for them, and re-layouts: 23.2 us -> 3.08 us
  other arithmetic: 16.1 us -> 0 us
  Pallas kernels: 0 us -> 11.3 us
  starting transfers between devices: 22 us -> 32.7 us
    psum x1 -> x0, blocking collectives: 51.8 us -> none  [body(): totals = lax.psum(squares, ('gz', 'gy'))]
    ppermute x12 -> x14, waiting for transfers between devices: 62.2 us -> 25.9 us  [moved(): return lax.ppermute(x, ('gz', 'gy'), route)]
    pallas_call x0 -> x10, Pallas kernels: none -> 11.3 us  [call(): pl.pallas_call(kernel, out_shape=[jax.ShapeDtypeStruct(outs[k], jnp.float...]
    another operation x27 -> x0, local copies, waits for them, and re-layouts: 10.8 us -> none  [the longest x11 9.93 us: pair_products(): jnp.stack([fields[left_idx] * fields[right_idx] for left_idx, right_idx i...]
    ppermute x12 -> x14, starting transfers between devices: 22 us -> 28.9 us  [moved(): return lax.ppermute(x, ('gz', 'gy'), route)]
    unnamed x32 -> x4, local copies, waits for them, and re-layouts: 9.12 us -> 2.4 us
    reduce_sum x2 -> x0, other arithmetic: 6.44 us -> none  [the longest x1 3.34 us: block_sums(): values.reshape(number, layers // 4, 4, height // 4, 4, across)]
    all_to_all x0 -> x1, starting transfers between devices: none -> 3.87 us  [body(): lax.all_to_all(jnp.broadcast_to(out['sums'], (devices,) + sums), ('gz', '...]
  transfers between devices with their start and end apart: 12 -> 15, of which waited for: 9 -> 6; matrix products, arithmetic and copies ran while one was open for 1% -> 1% of each run, Pallas kernels for 0% -> 12%
where the time goes in v1:
time: 74.1 us; the launch traced here: 73.8 us
  starting transfers between devices  32.7 us (44%)
  waiting for transfers between devices  25.9 us (35%)
  Pallas kernels  11.3 us (15%)
  local copies, waits for them, and re-layouts  3.08 us (4%)
    ppermute x14, starting transfers between devices, moved(): return lax.ppermute(x, ('gz', 'gy'), route)  28.9 us
    ppermute x14, waiting for transfers between devices, moved(): return lax.ppermute(x, ('gz', 'gy'), route)  25.9 us
    pallas_call x10, Pallas kernels, call(): pl.pallas_call(kernel, out_shape=[jax.ShapeDtypeStruct(outs[k], jnp.float...  11.3 us
    all_to_all x1, starting transfers between devices, body(): lax.all_to_all(jnp.broadcast_to(out['sums'], (devices,) + sums), ('gz', '...  3.87 us
    unnamed x4, local copies, waits for them, and re-layouts  2.4 us
  transfers between devices with their start and end apart: 15, of which 6 were waited for; matrix products, arithmetic and copies ran while one was open for 1% of the time, Pallas kernels for 12%

profile of v1, /device:TPU:0, one launch (start us, length us, event | category | flops | bytes accessed | tf_op | source)
XLA Modules:
  0.0 73.8 jit_solution(14102864740739371383)
XLA Ops:
  0.6 0.0 copy-start
  0.6 1.4 %copy-done = f32[4,4,96,256]{3,2,1,0:T(8,128)S(1)} copy-done((f32[4,4,96,256]{3,2,1,0:T(8,128)S(1)}, f32[4,4,96,256]{3,2,1,0:T(8,128)}, u32[]{:S(2)}) %copy-start) | copy-done | bytes 1572888
  2.0 0.0 copy-start.1
  2.0 1.0 %copy-done.1 = f32[4,96,256]{2,1,0:T(8,128)S(1)} copy-done((f32[4,96,256]{2,1,0:T(8,128)S(1)}, f32[4,96,256]{2,1,0:T(8,128)}, u32[]{:S(2)}) %copy-start.1) | copy-done | bytes 393240
  3.0 0.1 pack_send.1
  3.1 3.0 %collective-permute-start = (f32[2,5,48,256]{3,2,1,0:T(8,128)S(1)}, f32[2,5,48,256]{3,2,1,0:T(8,128)S(1)}, u32[]{:S(2)}, u32[]{:S(2)}) collective-permute-start(f32[2,5,48,256]{3,2,1,0:T(8,128)S(1)} %get-tuple-element.36), channel_id=1, source_target_pairs={{0,4},{1,5},{2,6},{3,7},{4,0},{5,1},{6,2},{7,3},{8,12},{9,13},{10,... | collective-permute-start | bytes 1474568 | tf_op jit(solution)/shard_map/ppermute | solution.py:350
  6.1 0.1 pack_keep.1
  6.2 3.7 %collective-permute-start.7 = (f32[2,5,48,256]{3,2,1,0:T(8,128)S(1)}, f32[2,5,48,256]{3,2,1,0:T(8,128)S(1)}, u32[]{:S(2)}, u32[]{:S(2)}) collective-permute-start(f32[2,5,48,256]{3,2,1,0:T(8,128)S(1)} %get-tuple-element.41.refs_0_.refs_2_), channel_id=1, source_target_pairs={{0,24},{1,25},{2,26},{3,27},{4,12},{5,13},{6,14},{7,15},{8,0},{9,1... | collective-permute-start | bytes 1474568 | tf_op jit(solution)/shard_map/ppermute | solution.py:350
  9.9 0.0 collective-permute-start.6
  9.9 8.3 %collective-permute-done.refs_0_ = f32[2,5,48,256]{3,2,1,0:T(8,128)S(1)} collective-permute-done((f32[2,5,48,256]{3,2,1,0:T(8,128)S(1)}, f32[2,5,48,256]{3,2,1,0:T(8,128)S(1)}, u32[]{:S(2)}, u32[]{:S(2)}) %collective-permute-start) | collective-permute-done | bytes 491552 | tf_op jit(solution)/shard_map/ppermute | solution.py:350
  18.2 2.1 %collective-permute-start.1 = (f32[2,5,48,256]{3,2,1,0:T(8,128)S(1)}, f32[2,5,48,256]{3,2,1,0:T(8,128)S(1)}, u32[]{:S(2)}, u32[]{:S(2)}) collective-permute-start(f32[2,5,48,256]{3,2,1,0:T(8,128)S(1)} %collective-permute-done.refs_0_), channel_id=1, source_target_pairs={{0,8},{1,9},{2,10},{3,11},{4,28},{5,29},{6,30},{7,31},{8,16},{9,17... | collective-permute-start | bytes 1474568 | tf_op jit(solution)/shard_map/ppermute | solution.py:350
  20.3 3.5 %collective-permute-start.2 = (f32[2,5,8,256]{3,2,1,0:T(8,128)S(1)}, f32[2,5,8,256]{3,2,1,0:T(8,128)S(1)}, u32[]{:S(2)}, u32[]{:S(2)}) collective-permute-start(f32[2,5,8,256]{3,2,1,0:T(8,128)S(1)} %get-tuple-element.37), channel_id=1, source_target_pairs={{0,4},{1,5},{2,6},{3,7},{4,0},{5,1},{6,2},{7,3},{8,12},{9,13},{10,... | collective-permute-start | bytes 245768 | tf_op jit(solution)/shard_map/ppermute | solution.py:350
  23.8 0.0 collective-permute-start.3
  23.9 5.8 %collective-permute-done.2.refs_2_ = f32[2,5,8,256]{3,2,1,0:T(8,128)S(1)} collective-permute-done((f32[2,5,8,256]{3,2,1,0:T(8,128)S(1)}, f32[2,5,8,256]{3,2,1,0:T(8,128)S(1)}, u32[]{:S(2)}, u32[]{:S(2)}) %collective-permute-start.2) | collective-permute-done | bytes 81952 | tf_op jit(solution)/shard_map/ppermute | solution.py:350
  29.6 1.2 %collective-permute-start.4 = (f32[2,5,8,256]{3,2,1,0:T(8,128)S(1)}, f32[2,5,8,256]{3,2,1,0:T(8,128)S(1)}, u32[]{:S(2)}, u32[]{:S(2)}) collective-permute-start(f32[2,5,8,256]{3,2,1,0:T(8,128)S(1)} %get-tuple-element.39), channel_id=1, source_target_pairs={{0,7},{1,4},{2,5},{3,6},{4,1},{5,2},{6,3},{7,0},{8,15},{9,12},{10,... | collective-permute-start | bytes 245768 | tf_op jit(solution)/shard_map/ppermute | solution.py:350
  30.9 0.0 collective-permute-done.3.refs_3_
  30.9 3.6 %collective-permute-done.4.refs_4_ = f32[2,5,8,256]{3,2,1,0:T(8,128)S(1)} collective-permute-done((f32[2,5,8,256]{3,2,1,0:T(8,128)S(1)}, f32[2,5,8,256]{3,2,1,0:T(8,128)S(1)}, u32[]{:S(2)}, u32[]{:S(2)}) %collective-permute-start.4) | collective-permute-done | bytes 81952 | tf_op jit(solution)/shard_map/ppermute | solution.py:350
  34.6 3.8 %collective-permute-start.8 = (f32[2,5,8,256]{3,2,1,0:T(8,128)S(1)}, f32[2,5,8,256]{3,2,1,0:T(8,128)S(1)}, u32[]{:S(2)}, u32[]{:S(2)}) collective-permute-start(f32[2,5,8,256]{3,2,1,0:T(8,128)S(1)} %get-tuple-element.42.refs_1_.refs_3_), channel_id=1, source_target_pairs={{0,24},{1,25},{2,26},{3,27},{4,12},{5,13},{6,14},{7,15},{8,0},{9,1... | collective-permute-start | bytes 245768 | tf_op jit(solution)/shard_map/ppermute | solution.py:350
  38.4 2.1 %collective-permute-done.8.refs_3_ = f32[2,5,8,256]{3,2,1,0:T(8,128)S(1)} collective-permute-done((f32[2,5,8,256]{3,2,1,0:T(8,128)S(1)}, f32[2,5,8,256]{3,2,1,0:T(8,128)S(1)}, u32[]{:S(2)}, u32[]{:S(2)}) %collective-permute-start.8) | collective-permute-done | bytes 81952 | tf_op jit(solution)/shard_map/ppermute | solution.py:350
  40.4 0.0 collective-permute-done.7.refs_2_
  40.4 0.8 %outer.1 = (f32[5,56,256]{2,1,0:T(8,128)S(1)}, f32[4,56,256]{2,1,0:T(8,128)S(1)}, f32[4,56,256]{2,1,0:T(8,128)S(1)}) custom-call(f32[2,5,48,256]{3,2,1,0:T(8,128)S(1)} %collective-permute-done.refs_0_, f32[2,5,8,256]{3,2,1,0:T(8,128)S(1)} %get-tuple-element.40.refs_1_, f32[2,5,48,256]{3,2,1,0:T(8,128)S(1)} %collective-permute-done.7.refs_2_, ...), custom_call_target="tpu_custom_call" | custom-call | tf_op jit(solution)/shard_map/outer/pallas_call | solution.py:24
  41.2 0.0 collective-permute-done.6.refs_2_
  41.2 1.6 %inner_far.1 = (f32[5,56,256]{2,1,0:T(8,128)S(1)}, f32[4,56,256]{2,1,0:T(8,128)S(1)}, f32[4,56,256]{2,1,0:T(8,128)S(1)}, f32[2,4,48,256]{3,2,1,0:T(8,128)S(1)}, f32[2,4,8,256]{3,2,1,0:T(8,128)S(1)}) custom-call(f32[2,5,48,256]{3,2,1,0:T(8,128)S(1)} %collective-permute-done.refs_0_, f32[2,5,8,256]{3,2,1,0:T(8,128)S(1)} %get-tuple-element.40.refs_1_, ...), custom_call_target="tpu_custom_call" | custom-call | tf_op jit(solution)/shard_map/inner_far/pallas_call | solution.py:24
  42.8 1.6 %inner_near.1 = (f32[5,56,256]{2,1,0:T(8,128)S(1)}, f32[4,56,256]{2,1,0:T(8,128)S(1)}, f32[4,56,256]{2,1,0:T(8,128)S(1)}, f32[2,4,48,256]{3,2,1,0:T(8,128)S(1)}, f32[2,4,8,256]{3,2,1,0:T(8,128)S(1)}) custom-call(f32[2,5,48,256]{3,2,1,0:T(8,128)S(1)} %get-tuple-element.43.refs_2_.refs_0_, f32[2,5,8,256]{3,2,1,0:T(8,128)S(1)} %get-tuple-element.44.refs_3_.refs_1_, ...), custom_call_target="tpu_custom_call" | custom-call | tf_op jit(solution)/shard_map/inner_near/pallas_call | solution.py:24
  44.4 2.1 %collective-permute-start.13 = (f32[2,4,48,256]{3,2,1,0:T(8,128)S(1)}, f32[2,4,48,256]{3,2,1,0:T(8,128)S(1)}, u32[]{:S(2)}, u32[]{:S(2)}) collective-permute-start(f32[2,4,48,256]{3,2,1,0:T(8,128)S(1)} %get-tuple-element.62.refs_8_), channel_id=1, source_target_pairs={{0,4},{1,5},{2,6},{3,7},{4,0},{5,1},{6,2},{7,3},{8,12},{9,13},{10,... | collective-permute-start | bytes 1179656 | tf_op jit(solution)/shard_map/ppermute | solution.py:350
  46.5 0.1 collective-permute-start.12
  46.6 0.3 collective-permute-start.5
  46.8 0.8 %early.1 = (f32[5,56,256]{2,1,0:T(8,128)S(1)}, f32[5,56,256]{2,1,0:T(8,128)S(1)}, f32[4,56,256]{2,1,0:T(8,128)S(1)}, f32[4,56,256]{2,1,0:T(8,128)S(1)}) custom-call(f32[2,5,48,256]{3,2,1,0:T(8,128)S(1)} %get-tuple-element.41.refs_0_.refs_2_, f32[2,5,8,256]{3,2,1,0:T(8,128)S(1)} %get-tuple-element.42.refs_1_.refs_3_, ...), custom_call_target="tpu_custom_call" | custom-call | tf_op jit(solution)/shard_map/early/pallas_call | solution.py:24
  47.6 2.3 %middle.1 = (f32[2,4,48,256]{3,2,1,0:T(8,128)S(1)}, f32[2,4,8,256]{3,2,1,0:T(8,128)}, f32[2,10,16,64]{3,2,1,0:T(8,128)S(1)}, f32[8,128]{1,0:T(8,128)S(1)}) custom-call(f32[4,56,256]{2,1,0:T(8,128)S(1)} %get-tuple-element.45.refs_0_.refs_4_, f32[4,56,256]{2,1,0:T(8,128)S(1)} %get-tuple-element.46.refs_1_.refs_5_, ...), custom_call_target="tpu_custom_call" | custom-call | tf_op jit(solution)/shard_map/middle/pallas_call | solution.py:24
  49.9 3.9 %collective-permute-start.10 = (f32[2,10,16,64]{3,2,1,0:T(8,128)S(1)}, f32[2,10,16,64]{3,2,1,0:T(8,128)S(1)}, u32[]{:S(2)}, u32[]{:S(2)}) collective-permute-start(f32[2,10,16,64]{3,2,1,0:T(8,128)S(1)} %get-tuple-element.67.refs_3_), channel_id=1, source_target_pairs={{0,4},{1,5},{2,6},{3,7},{4,0},{5,1},{6,2},{7,3},{8,12},{9,13},{10,... | collective-permute-start | bytes 245768 | tf_op jit(solution)/shard_map/ppermute | solution.py:350
  53.8 0.0 collective-permute-done.5.refs_1_
  53.8 0.0 collective-permute-done.1.refs_0_
  53.8 2.0 %outmost.1 = (f32[2,4,48,256]{3,2,1,0:T(8,128)S(1)}, f32[2,4,8,256]{3,2,1,0:T(8,128)}, f32[10,16,64]{2,1,0:T(8,128)S(1)}, f32[8,128]{1,0:T(8,128)S(1)}) custom-call(f32[2,5,48,256]{3,2,1,0:T(8,128)S(1)} %collective-permute-done.1.refs_0_, f32[2,5,8,256]{3,2,1,0:T(8,128)S(1)} %collective-permute-done.5.refs_1_, ...), custom_call_target="tpu_custom_call" | custom-call | tf_op jit(solution)/shard_map/outmost/pallas_call | solution.py:24
  55.8 0.7 broadcast_in_dim.3
  56.5 3.9 %all-to-all-start = ((f32[32,8,128]{2,1,0:T(8,128)}), f32[32,8,128]{2,1,0:T(8,128)S(1)}, u32[]{:S(2)}, u32[]{:S(2)}) async-start(f32[32,8,128]{2,1,0:T(8,128)} %broadcast_in_dim.3), calls=%async_computation | async-start | bytes 262144 | tf_op jit(solution)/shard_map/all_to_all | solution.py:450
  60.4 1.8 %collective-permute-start.9 = (f32[10,16,64]{2,1,0:T(8,128)S(1)}, f32[10,16,64]{2,1,0:T(8,128)S(1)}, u32[]{:S(2)}, u32[]{:S(2)}) collective-permute-start(f32[10,16,64]{2,1,0:T(8,128)S(1)} %slice_bitcast_fusion), channel_id=1, source_target_pairs={{0,8},{1,9},{2,10},{3,11},{4,28},{5,29},{6,30},{7,31},{8,16},{9,17... | collective-permute-start | bytes 122888 | tf_op jit(solution)/shard_map/ppermute | solution.py:350
  62.2 3.3 %collective-permute-start.11 = (f32[10,16,64]{2,1,0:T(8,128)S(1)}, f32[10,16,64]{2,1,0:T(8,128)S(1)}, u32[]{:S(2)}, u32[]{:S(2)}) collective-permute-start(f32[10,16,64]{2,1,0:T(8,128)S(1)} %get-tuple-element.66.refs_1_), channel_id=1, source_target_pairs={{0,28},{1,29},{2,30},{3,31},{4,8},{5,9},{6,10},{7,11},{8,4},{9,5},... | collective-permute-start | bytes 122888 | tf_op jit(solution)/shard_map/ppermute | solution.py:350
  65.5 3.9 %collective-permute-done.9.refs_2_ = f32[10,16,64]{2,1,0:T(8,128)S(1)} collective-permute-done((f32[10,16,64]{2,1,0:T(8,128)S(1)}, f32[10,16,64]{2,1,0:T(8,128)S(1)}, u32[]{:S(2)}, u32[]{:S(2)}) %collective-permute-start.9) | collective-permute-done | bytes 40992 | tf_op jit(solution)/shard_map/ppermute | solution.py:350
  69.4 0.0 collective-permute-done.10.refs_4_
  69.4 0.0 collective-permute-done.13.refs_9_
  69.4 0.0 collective-permute-done.12.refs_8_
  69.5 2.2 %collective-permute-done.11.refs_5_ = f32[10,16,64]{2,1,0:T(8,128)S(1)} collective-permute-done((f32[10,16,64]{2,1,0:T(8,128)S(1)}, f32[10,16,64]{2,1,0:T(8,128)S(1)}, u32[]{:S(2)}, u32[]{:S(2)}) %collective-permute-start.11) | collective-permute-done | bytes 40992 | tf_op jit(solution)/shard_map/ppermute | solution.py:350
  71.7 0.0 all-to-all-done.refs_0_
  71.7 2.2 %finish.1 = (f32[4,4,96,256]{3,2,1,0:T(8,128)}, f32[10,1,24,64]{3,2,1,0:T(8,128)}) custom-call(f32[32,8,128]{2,1,0:T(8,128)S(1)} %all-to-all-done.refs_0_, f32[10,16,64]{2,1,0:T(8,128)S(1)} %get-tuple-element.66.refs_1_, f32[10,16,64]{2,1,0:T(8,128)S(1)} %collective-permute-done.9.refs_2_, f32[2,10,16,64]{3,2,1,0:T(8,128)S(1)} %get-tuple-element.67.refs_3_, ...), custom_call_target="tpu_custom_call" | custom-call | tf_op jit(solution)/shard_map/finish/pallas_call | solution.py:24
  (2 shorter events, 0.0 us)
Async XLA Ops:
  0.6 1.4 %copy-start = (f32[4,4,96,256]{3,2,1,0:T(8,128)S(1)}, f32[4,4,96,256]{3,2,1,0:T(8,128)}, u32[]{:S(2)}) copy-start(f32[4,4,96,256]{3,2,1,0:T(8,128)} %refs_0_.5) | copy-start | bytes 4718596
  2.0 1.0 %copy-start.1 = (f32[4,96,256]{2,1,0:T(8,128)S(1)}, f32[4,96,256]{2,1,0:T(8,128)}, u32[]{:S(2)}) copy-start(f32[4,96,256]{2,1,0:T(8,128)} %refs_1_.5) | copy-start | bytes 1179652
  3.1 15.1 %collective-permute-start = (f32[2,5,48,256]{3,2,1,0:T(8,128)S(1)}, f32[2,5,48,256]{3,2,1,0:T(8,128)S(1)}, u32[]{:S(2)}, u32[]{:S(2)}) collective-permute-start(f32[2,5,48,256]{3,2,1,0:T(8,128)S(1)} %get-tuple-element.36), channel_id=1, source_target_pairs={{0,4},{1,5},{2,6},{3,7},{4,0},{5,1},{6,2},{7,3},{8,12},{9,13},{10,... | collective-permute-start | bytes 1474568 | tf_op jit(solution)/shard_map/ppermute | solution.py:350
  6.2 34.2 %collective-permute-start.7 = (f32[2,5,48,256]{3,2,1,0:T(8,128)S(1)}, f32[2,5,48,256]{3,2,1,0:T(8,128)S(1)}, u32[]{:S(2)}, u32[]{:S(2)}) collective-permute-start(f32[2,5,48,256]{3,2,1,0:T(8,128)S(1)} %get-tuple-element.41.refs_0_.refs_2_), channel_id=1, source_target_pairs={{0,24},{1,25},{2,26},{3,27},{4,12},{5,13},{6,14},{7,15},{8,0},{9,1... | collective-permute-start | bytes 1474568 | tf_op jit(solution)/shard_map/ppermute | solution.py:350
  9.9 31.3 %collective-permute-start.6 = (f32[2,5,48,256]{3,2,1,0:T(8,128)S(1)}, f32[2,5,48,256]{3,2,1,0:T(8,128)S(1)}, u32[]{:S(2)}, u32[]{:S(2)}) collective-permute-start(f32[2,5,48,256]{3,2,1,0:T(8,128)S(1)} %get-tuple-element.48), channel_id=1, source_target_pairs={{0,4},{1,5},{2,6},{3,7},{4,0},{5,1},{6,2},{7,3},{8,12},{9,13},{10,... | collective-permute-start | bytes 1474568 | tf_op jit(solution)/shard_map/ppermute | solution.py:350
  18.2 35.7 %collective-permute-start.1 = (f32[2,5,48,256]{3,2,1,0:T(8,128)S(1)}, f32[2,5,48,256]{3,2,1,0:T(8,128)S(1)}, u32[]{:S(2)}, u32[]{:S(2)}) collective-permute-start(f32[2,5,48,256]{3,2,1,0:T(8,128)S(1)} %collective-permute-done.refs_0_), channel_id=1, source_target_pairs={{0,8},{1,9},{2,10},{3,11},{4,28},{5,29},{6,30},{7,31},{8,16},{9,17... | collective-permute-start | bytes 1474568 | tf_op jit(solution)/shard_map/ppermute | solution.py:350
  20.3 9.3 %collective-permute-start.2 = (f32[2,5,8,256]{3,2,1,0:T(8,128)S(1)}, f32[2,5,8,256]{3,2,1,0:T(8,128)S(1)}, u32[]{:S(2)}, u32[]{:S(2)}) collective-permute-start(f32[2,5,8,256]{3,2,1,0:T(8,128)S(1)} %get-tuple-element.37), channel_id=1, source_target_pairs={{0,4},{1,5},{2,6},{3,7},{4,0},{5,1},{6,2},{7,3},{8,12},{9,13},{10,... | collective-permute-start | bytes 245768 | tf_op jit(solution)/shard_map/ppermute | solution.py:350
  23.8 7.0 %collective-permute-start.3 = (f32[2,5,8,256]{3,2,1,0:T(8,128)S(1)}, f32[2,5,8,256]{3,2,1,0:T(8,128)S(1)}, u32[]{:S(2)}, u32[]{:S(2)}) collective-permute-start(f32[2,5,8,256]{3,2,1,0:T(8,128)S(1)} %get-tuple-element.38), channel_id=1, source_target_pairs={{0,1},{1,2},{2,3},{3,0},{4,7},{5,4},{6,5},{7,6},{8,9},{9,10},{10,1... | collective-permute-start | bytes 245768 | tf_op jit(solution)/shard_map/ppermute | solution.py:350
  29.6 4.9 %collective-permute-start.4 = (f32[2,5,8,256]{3,2,1,0:T(8,128)S(1)}, f32[2,5,8,256]{3,2,1,0:T(8,128)S(1)}, u32[]{:S(2)}, u32[]{:S(2)}) collective-permute-start(f32[2,5,8,256]{3,2,1,0:T(8,128)S(1)} %get-tuple-element.39), channel_id=1, source_target_pairs={{0,7},{1,4},{2,5},{3,6},{4,1},{5,2},{6,3},{7,0},{8,15},{9,12},{10,... | collective-permute-start | bytes 245768 | tf_op jit(solution)/shard_map/ppermute | solution.py:350
  34.6 5.9 %collective-permute-start.8 = (f32[2,5,8,256]{3,2,1,0:T(8,128)S(1)}, f32[2,5,8,256]{3,2,1,0:T(8,128)S(1)}, u32[]{:S(2)}, u32[]{:S(2)}) collective-permute-start(f32[2,5,8,256]{3,2,1,0:T(8,128)S(1)} %get-tuple-element.42.refs_1_.refs_3_), channel_id=1, source_target_pairs={{0,24},{1,25},{2,26},{3,27},{4,12},{5,13},{6,14},{7,15},{8,0},{9,1... | collective-permute-start | bytes 245768 | tf_op jit(solution)/shard_map/ppermute | solution.py:350
  44.4 25.0 %collective-permute-start.13 = (f32[2,4,48,256]{3,2,1,0:T(8,128)S(1)}, f32[2,4,48,256]{3,2,1,0:T(8,128)S(1)}, u32[]{:S(2)}, u32[]{:S(2)}) collective-permute-start(f32[2,4,48,256]{3,2,1,0:T(8,128)S(1)} %get-tuple-element.62.refs_8_), channel_id=1, source_target_pairs={{0,4},{1,5},{2,6},{3,7},{4,0},{5,1},{6,2},{7,3},{8,12},{9,13},{10,... | collective-permute-start | bytes 1179656 | tf_op jit(solution)/shard_map/ppermute | solution.py:350
  46.5 23.0 %collective-permute-start.12 = (f32[2,4,48,256]{3,2,1,0:T(8,128)S(1)}, f32[2,4,48,256]{3,2,1,0:T(8,128)S(1)}, u32[]{:S(2)}, u32[]{:S(2)}) collective-permute-start(f32[2,4,48,256]{3,2,1,0:T(8,128)S(1)} %get-tuple-element.60.refs_6_), channel_id=1, source_target_pairs={{0,4},{1,5},{2,6},{3,7},{4,0},{5,1},{6,2},{7,3},{8,12},{9,13},{10,... | collective-permute-start | bytes 1179656 | tf_op jit(solution)/shard_map/ppermute | solution.py:350
  46.6 7.3 %collective-permute-start.5 = (f32[2,5,8,256]{3,2,1,0:T(8,128)S(1)}, f32[2,5,8,256]{3,2,1,0:T(8,128)S(1)}, u32[]{:S(2)}, u32[]{:S(2)}) collective-permute-start(f32[2,5,8,256]{3,2,1,0:T(8,128)S(1)} %get-tuple-element.40.refs_1_), channel_id=1, source_target_pairs={{0,8},{1,9},{2,10},{3,11},{4,28},{5,29},{6,30},{7,31},{8,16},{9,17... | collective-permute-start | bytes 245768 | tf_op jit(solution)/shard_map/ppermute | solution.py:350
  49.9 19.5 %collective-permute-start.10 = (f32[2,10,16,64]{3,2,1,0:T(8,128)S(1)}, f32[2,10,16,64]{3,2,1,0:T(8,128)S(1)}, u32[]{:S(2)}, u32[]{:S(2)}) collective-permute-start(f32[2,10,16,64]{3,2,1,0:T(8,128)S(1)} %get-tuple-element.67.refs_3_), channel_id=1, source_target_pairs={{0,4},{1,5},{2,6},{3,7},{4,0},{5,1},{6,2},{7,3},{8,12},{9,13},{10,... | collective-permute-start | bytes 245768 | tf_op jit(solution)/shard_map/ppermute | solution.py:350
  56.5 15.1 %all-to-all-start = ((f32[32,8,128]{2,1,0:T(8,128)}), f32[32,8,128]{2,1,0:T(8,128)S(1)}, u32[]{:S(2)}, u32[]{:S(2)}) async-start(f32[32,8,128]{2,1,0:T(8,128)} %broadcast_in_dim.3), calls=%async_computation | async-start | bytes 262144 | tf_op jit(solution)/shard_map/all_to_all | solution.py:450
  60.4 9.0 %collective-permute-start.9 = (f32[10,16,64]{2,1,0:T(8,128)S(1)}, f32[10,16,64]{2,1,0:T(8,128)S(1)}, u32[]{:S(2)}, u32[]{:S(2)}) collective-permute-start(f32[10,16,64]{2,1,0:T(8,128)S(1)} %slice_bitcast_fusion), channel_id=1, source_target_pairs={{0,8},{1,9},{2,10},{3,11},{4,28},{5,29},{6,30},{7,31},{8,16},{9,17... | collective-permute-start | bytes 122888 | tf_op jit(solution)/shard_map/ppermute | solution.py:350
  62.2 9.4 %collective-permute-start.11 = (f32[10,16,64]{2,1,0:T(8,128)S(1)}, f32[10,16,64]{2,1,0:T(8,128)S(1)}, u32[]{:S(2)}, u32[]{:S(2)}) collective-permute-start(f32[10,16,64]{2,1,0:T(8,128)S(1)} %get-tuple-element.66.refs_1_), channel_id=1, source_target_pairs={{0,28},{1,29},{2,30},{3,31},{4,8},{5,9},{6,10},{7,11},{8,4},{9,5},... | collective-permute-start | bytes 122888 | tf_op jit(solution)/shard_map/ppermute | solution.py:350

commit v2 on v0

v2 whole, which is shorter than its diff:
```python
import functools
import types
import jax
import jax.numpy as jnp
from jax import lax
from jax.experimental import pallas as pl
from jax.experimental.pallas import tpu as pltpu
from jax.sharding import PartitionSpec as P

RELAX_WEIGHT = 2.0 / 3.0
PAIRS = ((0, 0), (0, 1), (0, 2), (0, 3), (1, 1), (1, 2), (1, 3), (2, 2), (2, 3), (3, 3))
AT = {pair: k for k, pair in enumerate(PAIRS)}
BLOCK = 4
EDGE = 8
VMEM_LIMIT = 40 * 1024 * 1024

COST = {'inner': 10, 'pack_near': 8}


def call(body, ins, outs, scratch=(), far=(), alias=None):
    names_in, names_out = list(ins), list(outs)

    def kernel(*refs):
        cut = len(names_in) + len(names_out)
        i = types.SimpleNamespace(**dict(zip(names_in, refs)))
        o = types.SimpleNamespace(**dict(zip(names_out, refs[len(names_in) :])))
        body(i, o, *refs[cut:])

    def spec(name):
        return pl.BlockSpec(memory_space=pltpu.HBM if name in far else pltpu.VMEM)

    got = pl.pallas_call(
        kernel,
        out_shape=[jax.ShapeDtypeStruct(outs[k], jnp.float32) for k in names_out],
        in_specs=[spec(k) for k in names_in],
        out_specs=[spec(k) for k in names_out],
        scratch_shapes=list(scratch),
        input_output_aliases={names_in.index(a): names_out.index(b) for a, b in (alias or {}).items()},
        compiler_params=pltpu.CompilerParams(vmem_limit_bytes=VMEM_LIMIT),
        cost_estimate=pl.CostEstimate(flops=int(COST.get(body.__name__, 0) * 1e9), bytes_accessed=0, transcendentals=0),
        name=body.__name__,
    )(*[ins[k] for k in names_in])
    return types.SimpleNamespace(**dict(zip(names_out, got)))


def parity():
    return lax.rem(lax.axis_index("gz"), 2)


def natural(k, odd, planes):
    return k + odd * (planes - 1 - 2 * k)


def half_of_tile(shape):
    return lax.broadcasted_iota(jnp.int32, shape, 0) // BLOCK


def rows_at(start, size):
    return pl.ds(pl.multiple_of(start, 8), size)


def copies(jobs, sems):
    started = [pltpu.make_async_copy(a, b, sems.at[n]) for n, (a, b) in enumerate(jobs)]
    for one in started:
        one.start()
    return started


def plane_jobs(i, k, odd, start, target):
    fields, planes = i.tv.shape[:2]
    half = i.tv.shape[2] // 2
    at, rows = natural(k, odd, planes), rows_at(start, half)
    return [
        (i.tv.at[:, at, rows, :], target.at[pl.ds(0, fields), pl.ds(0, half), :]),
        (i.coef.at[at, rows, :], target.at[fields, pl.ds(0, half), :]),
    ]


def tile_jobs(i, start, target):
    fields, rows = i.tv.shape[0], rows_at(start, EDGE)
    return [
        (i.tv.at[:, :, rows, :], target.at[pl.ds(0, fields)]),
        (i.coef.at[:, rows, :], target.at[fields]),
    ]


def packed(tiles, q, f, side, odd, which):
    planes = tiles.shape[1]
    u, v = tiles[f, natural(2 * q, odd, planes)], tiles[f, natural(2 * q + 1, odd, planes)]
    return jnp.where(which == side, u, pltpu.roll(v, BLOCK, 0))


def unpacked(tile, k):
    return tile if k % 2 == 0 else pltpu.roll(tile, BLOCK, 0)


def pack_first(i, o, extra, halo, cross, edge, sems, late_sems):
    odd = parity()
    fields, planes, rows, width = i.tv.shape
    half = rows // 2
    jobs = tile_jobs(i, half - EDGE * (1 - odd), extra)
    jobs += tile_jobs(i, (rows - EDGE) * (1 - odd), halo) + tile_jobs(i, (rows - EDGE) * odd, cross)
    jobs += plane_jobs(i, 0, odd, (1 - odd) * half, o.far0)
    for k in range(2):
        jobs += plane_jobs(i, k, odd, odd * half, o.own.at[k])
    started = copies(jobs, sems)
    for one in started[:6]:
        one.wait()
    which = half_of_tile((EDGE, width))
    for q in range(planes // 2):
        for f in range(fields + 1):
            edge[q, f] = packed(extra, q, f, 1 - odd, odd, which)
            o.halo[q, f] = packed(halo, q, f, 1 - odd, odd, which)
            o.cross[q, f] = packed(cross, q, f, odd, odd, which)
    more = [(edge.at[q], o.far0.at[:, pl.ds(half + q * EDGE, EDGE), :]) for q in range(planes // 2)]
    for one in started[6:] + copies(more, late_sems):
        one.wait()


def pack_second(i, o, extra, sems):
    odd = parity()
    fields, planes, rows, width = i.tv.shape
    half = rows // 2
    jobs = tile_jobs(i, half - EDGE * odd, extra)
    jobs += plane_jobs(i, 1, odd, (1 - odd) * half, o.far1)
    for k in range(2):
        jobs += plane_jobs(i, 2 + k, odd, odd * half, o.near.at[k])
    started = copies(jobs, sems)
    o.far[:, :, :half] = i.own[...]
    for q in range(planes // 2):
        o.far1[:, pl.ds(half + q * EDGE, EDGE), :] = i.cross[q]
    for one in started:
        one.wait()
    which = half_of_tile((EDGE, width))
    for k in range(planes):
        for f in range(fields + 1):
            own = extra[f, natural(k, odd, planes)]
            window_of = (o.far if k < 2 else o.near)
            tile = jnp.where(which == odd, own, unpacked(i.halo[k // 2, f], k))
            window_of[k % 2, f, half:] = tile
            if k < 2:
                o.far_edge[k, f] = tile


def pack_near(i, o, sems):
    odd = parity()
    half = i.tv.shape[2] // 2
    jobs = []
    for k in range(2):
        jobs += plane_jobs(i, 2 + k, odd, (1 - odd) * half, (o.send1 if k else o.send0))
    started = copies(jobs, sems)
    o.on[...] = i.far0[:, :half]
    for one in started:
        one.wait()


def pack_third(i, o):
    odd = parity()
    fields, tall, width = i.far0.shape
    half = tall - 2 * EDGE
    which = half_of_tile((EDGE, width))
    for k in range(4):
        for f in range(fields):
            extra = i.far0[f, pl.ds(half + k // 2 * EDGE, EDGE), :]
            cross = i.far1[f, pl.ds(half + k // 2 * EDGE, EDGE), :]
            tile = jnp.where(which == odd, unpacked(extra, k), unpacked(cross, k))
            if k < 2:
                plane = (i.far1 if k else i.far0)[f, :half]
                o.far[k, f, :half] = plane
                o.far[k, f, half:] = tile
                o.send[f, pl.ds(half + (1 - k) * EDGE, EDGE), :] = tile
                if k == 1:
                    o.send[f, :half] = plane
            else:
                o.near_edge[k - 2, f] = tile


def inverse(x):
    guess = pl.reciprocal(x, approx=True)
    return guess * (2.0 - x * guess)


def onward(x, axis):
    return pltpu.roll(x, x.shape[axis] - 1, axis)


def backward(x, axis):
    return pltpu.roll(x, 1, axis)


def joint(a, b):
    return a * b * inverse(a + b)


def weigh(before, here, after, c):
    wx = joint(here, onward(here, 1))
    wy = joint(here, onward(here, 0))
    wm = joint(here, before)
    wp = joint(here, after)
    c[0] = wx
    c[1] = wy
    c[2] = wm
    c[3] = wp
    c[4] = RELAX_WEIGHT * inverse(wx + backward(wx, 1) + wy + backward(wy, 0) + wm + wp)


def step(before, here, after, c):
    fx = c[0] * (here - onward(here, 1))
    fy = c[1] * (here - onward(here, 0))
    flux = (fx - backward(fx, 1)) + (fy - backward(fy, 0))
    flux = flux + c[2] * (here - before) + c[3] * (here - after)
    return here - c[4] * flux


def window(whole, at):
    return lambda f: whole[at, f]


def joined(keep, edge, at):
    return lambda f: jnp.concatenate([keep[f], edge[at, f]], axis=0)


def sweep_first(planes, z, c, out):
    last = 4
    weigh(planes[z - 1](last), planes[z](last), planes[z + 1](last), c)
    for f in range(last):
        out[f] = step(planes[z - 1](f), planes[z](f), planes[z + 1](f), c)


def sweep_second(first, z, c, keep, edge):
    half = keep.shape[1]
    for f in range(first[z].shape[0]):
        value = step(first[z - 1][f], first[z][f], first[z + 1][f], c)
        keep[f] = value[:half]
        edge[f] = value[half:]


def early(i, o):
    planes = {k: window(i.far, k) for k in (0, 1)} | {k + 2: window(i.near, k) for k in (0, 1)}
    sweep_first(planes, 1, o.c1, o.f1)
    sweep_first(planes, 2, o.c2, o.f2)


def outer(i, o, c8):
    planes = {7 - k: window(i.far, k) for k in (0, 1)}
    planes |= {8 + k: joined(i.next.at[k], i.next_edge, k) for k in (0, 1)}
    sweep_first(planes, 7, o.c7, o.f7)
    sweep_first(planes, 8, c8, o.f8)


def inner_last(i, o):
    planes = {7 - k: window(i.far, k) for k in (0, 1)} | {5: joined(i.near5, i.near_edge, 0)}
    sweep_first(planes, 6, o.c6, o.f6)
    sweep_second({6: o.f6, 7: i.f7, 8: i.f8}, 7, i.c7, o.rel, o.rel_edge)


def inner(i, o):
    planes = {3: window(i.own, 1), 6: window(i.far, 1)}
    planes |= {5 - k: joined((i.near4 if k else i.near5), i.near_edge, k) for k in (0, 1)}
    sweep_first(planes, 5, o.c5, o.f5)
    sweep_first(planes, 4, o.c4, o.f4)
    first = {4: o.f4, 5: o.f5, 6: i.f6, 7: i.f7}
    sweep_second(first, 6, i.c6, o.rel.at[0], o.rel_edge.at[0])
    sweep_second(first, 5, o.c5, o.rel.at[1], o.rel_edge.at[1])


def squares(refs, sums, before=None):
    fields, half, width = refs[0].shape
    for f in range(fields):
        total = jnp.zeros((EDGE, width), jnp.float32)
        for ref in refs:
            for tile in range(half // EDGE):
                part = ref[f, pl.ds(tile * EDGE, EDGE), :]
                total = total + part * part
        total = jnp.sum(total[:, : width // 2] + total[:, width // 2 :], axis=0, keepdims=True)
        sums[f : f + 1] = total if before is None else total + before[f : f + 1]


def near_rest(i, o, c3, f3):
    planes = {2 + k: window(i.near, k) for k in (0, 1)} | {4: joined(i.near4, i.near_edge, 1)}
    sweep_first(planes, 3, c3, f3)
    first = {1: i.f1, 2: i.f2, 4: i.f4, 5: i.f5} | {3: f3}
    sweep_second(first, 4, i.c4, o.rel4, o.rel4_edge)
    sweep_second(first, 2, i.c2, o.rel.at[0], o.rel_edge.at[0])
    sweep_second(first, 3, c3, o.rel.at[1], o.rel_edge.at[1])
    squares([o.rel4, o.rel.at[0], o.rel.at[1], i.rel7, i.rel.at[0], i.rel.at[1]], o.sums)


def far_rest(i, o, cm, c0, fm, f0, own_sums):
    planes = {k: window(i.far, k) for k in (0, 1)}
    tall = i.far.shape[2]
    planes[-1] = lambda f: jnp.concatenate([i.prev0[f], i.prev1[f, tall:]], axis=0)
    planes[-2] = lambda f: i.prev1[f, :tall]
    sweep_first(planes, -1, cm, fm)
    sweep_first(planes, 0, c0, f0)
    first = {-1: fm, 0: f0, 1: i.f1, 2: i.f2}
    sweep_second(first, 0, c0, o.rel.at[0], o.rel_edge.at[0])
    sweep_second(first, 1, i.c1, o.rel.at[1], o.rel_edge.at[1])
    squares([o.rel.at[0], o.rel.at[1]], own_sums, i.sums)
    for n in range(o.sums.shape[0]):
        o.sums[n] = own_sums[...]


def split(x):
    high = x.astype(jnp.bfloat16)
    return high, (x - high.astype(jnp.float32)).astype(jnp.bfloat16)


def times_table(x, table):
    high, low = split(x)
    return jnp.dot(high, table, preferred_element_type=jnp.float32) + jnp.dot(
        low, table, preferred_element_type=jnp.float32
    )


def lane_table(width, spread):
    part = width // BLOCK
    shape = (part, width) if spread else (width, part)
    cell = lax.broadcasted_iota(jnp.int32, shape, 1 if spread else 0)
    block = lax.broadcasted_iota(jnp.int32, shape, 0 if spread else 1)
    moved = jnp.where(cell < 2, cell + width - 2, cell - 2)
    return (moved // BLOCK == block).astype(jnp.bfloat16)


def group_count(half):
    return (half // BLOCK + 1 + 7) // 8 * 8


def grams(planes, out, stacked, folded):
    half, width = planes[0][0].shape[1:]
    tall, part, groups = half + EDGE, width // BLOCK, group_count(half)
    for at, (a, b) in enumerate(PAIRS):
        total = None
        for keep, edge in planes:
            left = jnp.concatenate([keep[a], edge[a]], axis=0)
            right = left if a == b else jnp.concatenate([keep[b], edge[b]], axis=0)
            total = left * right if total is None else total + left * right
        stacked[pl.ds(at * tall, tall), :] = total
    across = times_table(stacked[...], lane_table(width, False))
    for at in range(len(PAIRS)):
        two = across[at * tall : (at + 1) * tall]
        two = two + backward(two, 0)
        folded[at, :tall] = two + pltpu.roll(two, 2, 0)
        folded[at, tall:] = jnp.zeros((groups * BLOCK - tall, part), jnp.float32)
    for at in range(len(PAIRS)):
        value = folded[at, pl.ds(1, groups, stride=BLOCK), :]
        out[pl.ds(at // BLOCK * groups, groups), pl.ds(at % BLOCK * part, part)] = value


def products(i, o, stacked, folded):
    rel4 = (i.rel4, i.rel4_edge)
    far, near = [(i.rel.at[k], i.rel_edge.at[k]) for k in range(2)]
    own = [(i.own.at[k], i.own_edge.at[k]) for k in range(2)]
    mid = [(i.mid.at[k], i.mid_edge.at[k]) for k in range(2)]
    count = o.far.shape[0]
    grams([(i.rel7, i.rel7_edge), far], o.far, stacked, folded)
    grams(own, o.gram, stacked, folded)
    grams(mid + [rel4, near], o.mid, stacked, folded)
    o.both[:count] = o.far[...]
    o.both[count:] = o.mid[...]


def solve_rows(rel, spread, base, scale, result, z):
    fields, half, width = result.shape[1:]
    rel = rel if isinstance(rel, list) else [rel.at[f] for f in range(fields)]
    within = lax.broadcasted_iota(jnp.int32, (EDGE, width), 0)
    for tile in range(half // EDGE):
        entry = {}
        for at, key in enumerate(PAIRS):
            three = [jnp.broadcast_to(spread[at, pl.ds(base + 2 * tile + n, 1), :], (EDGE, width)) for n in range(3)]
            entry[key] = jnp.where(within < 2, three[0], jnp.where(within < 6, three[1], three[2]))
        rows = pl.ds(tile * EDGE, EDGE)
        columns = []
        for b in range(fields):
            accum = rel[b][rows, :] * scale[b]
            for a in range(b):
                accum = accum - entry[a, b] * columns[a]
            columns.append(accum * entry[b, b])
            result[z, b, rows, :] = columns[b]


def write_plane(result, z, prolong, start, odd, sems):
    planes, half = prolong.shape[1], result.shape[2]
    target = prolong.at[:, natural(z, odd, planes), rows_at(start, half), :]
    one = pltpu.make_async_copy(result.at[z], target, sems.at[z])
    one.start()
    return one


def triangle(scale, values):
    fields = len(scale)
    matrix = {(a, b): values(at) * (scale[a] * scale[b]) for at, (a, b) in enumerate(PAIRS)}
    trace = matrix[0, 0] + matrix[1, 1] + matrix[2, 2] + matrix[3, 3]
    ridge = 0.64 * (trace / 256.0 + 1e-06)
    upper, inv = {}, {}
    for a in range(fields):
        for b in range(a, fields):
            accum = matrix[a, b] + ridge if a == b else matrix[a, b]
            for c in range(a):
                accum = accum - upper[c, a] * upper[c, b]
            if a == b:
                upper[a, a] = jnp.sqrt(accum)
                inv[a] = 1.0 / upper[a, a]
            else:
                upper[a, b] = accum * inv[a]
    return upper, inv


def spread_all(upper, inv, lanes, spread):
    entries = [inv[a] if a == b else upper[a, b] for a, b in PAIRS]
    rows = entries[0].shape[0]
    wide = times_table(jnp.concatenate(entries, axis=0), lanes)
    for at in range(len(PAIRS)):
        spread[at] = wide[at * rows : (at + 1) * rows]


def gram_at(ref, at, groups, start=0):
    part = ref.shape[-1] // BLOCK
    return ref[pl.ds(start + at // BLOCK * groups, groups), pl.ds(at % BLOCK * part, part)]


def finish_own(cells, i, o, result, spread, sems):
    odd = parity()
    fields, planes, rows, width = o.prolong.shape
    half = rows // 2
    groups = group_count(half)
    totals = jnp.sum(jnp.sum(i.totals[...], axis=0), axis=1, keepdims=True)
    scales = lax.rsqrt(totals / cells + 1e-06)
    o.scales[...] = jnp.broadcast_to(scales, o.scales.shape)
    scale = [scales[f : f + 1] for f in range(fields)]
    upper, inv = triangle(
        scale,
        lambda at: jnp.concatenate(
            [gram_at(i.gram, at, groups) + gram_at(i.same, at, groups), gram_at(i.mid, at, groups)], axis=0
        ),
    )
    lanes = lane_table(width, True)
    for at, (a, b) in enumerate(PAIRS):
        value = upper[a, b]
        o.mine[at] = jnp.where(odd == 0, value[groups:], value[:groups])
    spread_all(upper, inv, lanes, spread)
    writes = []
    for z in range(planes):
        solve_rows((i.far if z < 2 else i.near).at[z % 2], spread, z // 2 * groups, scale, result, z)
        writes.append(write_plane(result, z, o.prolong, odd * half, odd, sems))
    for one in writes:
        one.wait()


def finish_other(i, o, result, spread, sems):
    odd = parity()
    fields, planes, rows, width = o.prolong.shape
    half = rows // 2
    groups = group_count(half)
    scale = [i.scales[f : f + 1, :1] for f in range(fields)]
    both = i.both
    mid_start = i.cross.shape[0]
    upper, inv = triangle(
        scale,
        lambda at: jnp.concatenate(
            [gram_at(both, at, groups) + gram_at(i.cross, at, groups), gram_at(both, at, groups, mid_start)],
            axis=0,
        ),
    )
    lanes = lane_table(width, True)
    count = rows // BLOCK
    line = lax.broadcasted_iota(jnp.int32, (count, width // BLOCK), 0)
    pad = jnp.zeros((count - groups, width // BLOCK), jnp.float32)
    for at, (a, b) in enumerate(PAIRS):
        value = upper[a, b]
        mine, theirs = i.mine[at], jnp.where(odd == 0, value[groups:], value[:groups])
        low = jnp.concatenate([jnp.where(odd == 0, mine, theirs), pad], axis=0)
        top = jnp.concatenate([jnp.where(odd == 0, theirs, mine), pad], axis=0)
        low, top = onward(low, 0), pltpu.roll(top, half // BLOCK - 1, 0)
        o.factors[at, 0] = jnp.where(line < half // BLOCK, low, top)
    spread_all(upper, inv, lanes, spread)
    writes = []
    for z in range(planes):
        rel = i.last if z == 0 else i.back.at[z - 1] if z < planes - 1 else i.back4
        solve_rows(rel, spread, z // 2 * groups, scale, result, z)
        writes.append(write_plane(result, z, o.prolong, (1 - odd) * half, odd, sems))
    for one in writes:
        one.wait()


def moved(name, x, even_by, odd_by):
    nz, ny = lax.axis_size("gz"), lax.axis_size("gy")
    route = []
    for z in range(nz):
        dz, dy = odd_by if z % 2 else even_by
        for y in range(ny):
            route.append((z * ny + y, (z + dz) % nz * ny + (y + dy) % ny))
    with jax.named_scope(name):
        return lax.ppermute(x, ("gz", "gy"), route)


def body(tv, coef):
    fields, planes, rows, width = tv.shape
    half = rows // 2
    devices = lax.axis_size("gz") * lax.axis_size("gy")
    cells = devices * planes * rows * width
    groups = group_count(half)
    tall = half + EDGE
    windows, edge = (2, fields + 1, tall, width), (2, fields + 1, EDGE, width)
    keep, keeps = (fields + 1, half, width), (2, fields + 1, half, width)
    first, coefs = (fields, tall, width), (5, tall, width)
    gram = (-(-len(PAIRS) // BLOCK) * groups, width)
    sums = (8, width // 2)
    rel, rel_edge = (fields, half, width), (fields, EDGE, width)

    def local(shape):
        return pltpu.VMEM(shape, jnp.float32)

    tiles = local((fields + 1, planes, EDGE, width))
    args = dict(tv=tv, coef=coef)
    sent = call(
        pack_first,
        args,
        dict(far0=(fields + 1, half + 2 * EDGE, width), own=keeps, halo=edge, cross=edge),
        [tiles] * 3 + [local(edge), pltpu.SemaphoreType.DMA((12,)), pltpu.SemaphoreType.DMA((2,))],
        far=("tv", "coef"),
    )
    far0 = moved("far0", sent.far0, (1, 0), (-1, 0))
    halo = moved("halo", sent.halo, (0, 1), (0, -1))
    cross = moved("cross", sent.cross, (0, -1), (0, 1))
    after = moved("after", sent.own, (-2, 0), (2, 0))
    own = call(
        pack_second,
        dict(halo=halo, cross=cross, own=sent.own, **args),
        dict(
            far=windows,
            near=windows,
            far1=(fields + 1, half + 2 * EDGE, width),
            far_edge=edge,
        ),
        [tiles, pltpu.SemaphoreType.DMA((8,))],
        far=("tv", "coef"),
    )
    to_near = call(
        pack_near,
        dict(far0=far0, **args),
        dict(send0=keep, send1=keep, on=keep),
        [pltpu.SemaphoreType.DMA((4,))],
        far=("tv", "coef"),
    )
    prev0 = moved("prev0", to_near.on, (2, 0), (-2, 0))
    far1 = moved("far1", own.far1, (1, 0), (-1, 0))
    near5 = moved("near5", to_near.send0, (1, 0), (-1, 0))
    near4 = moved("near4", to_near.send1, (1, 0), (-1, 0))
    after_edge = moved("after_edge", own.far_edge, (-2, 0), (2, 0))
    a = call(
        early,
        dict(far=own.far, near=own.near, gate=after_edge),
        dict(c1=coefs, c2=coefs, f1=first, f2=first),
    )
    par = call(
        pack_third,
        dict(far0=far0, far1=far1, gate=a.c1),
        dict(far=windows, near_edge=edge, send=(fields + 1, tall + EDGE, width)),
    )
    prev1 = moved("prev1", par.send, (2, 0), (-2, 0))
    b = call(
        outer,
        dict(far=par.far, next=after, next_edge=after_edge),
        dict(c7=coefs, f7=first, f8=first),
        [local(coefs)],
    )
    c = call(
        inner_last,
        dict(far=par.far, near5=near5, near_edge=par.near_edge, gate=prev0, c7=b.c7, f7=b.f7, f8=b.f8),
        dict(c6=coefs, f6=first, rel=rel, rel_edge=rel_edge),
    )
    last = moved("last", c.rel, (1, 0), (-1, 0))
    d = call(
        inner,
        dict(
            own=own.near,
            far=par.far,
            near5=near5,
            near4=near4,
            near_edge=par.near_edge,
            f6=c.f6,
            f7=b.f7,
            c6=c.c6,
        ),
        dict(c4=coefs, c5=coefs, f4=first, f5=first, rel=(2,) + rel, rel_edge=(2,) + rel_edge),
    )
    back = moved("back", d.rel, (1, 0), (-1, 0))
    n = call(
        near_rest,
        dict(
            near=own.near,
            near4=near4,
            near_edge=par.near_edge,
            f1=a.f1, f2=a.f2, c2=a.c2,
            f4=d.f4, f5=d.f5, c4=d.c4, rel=d.rel,
            rel7=c.rel,
        ),
        dict(rel=(2,) + rel, rel_edge=(2,) + rel_edge, rel4=rel, rel4_edge=rel_edge, sums=sums),
        [local(coefs), local(first)],
    )
    back4 = moved("back4", n.rel4, (1, 0), (-1, 0))
    r = call(
        far_rest,
        dict(
            prev0=prev0,
            prev1=prev1,
            far=own.far,
            f1=a.f1, f2=a.f2, c1=a.c1,
            sums=n.sums,
            gate=last,
        ),
        dict(rel=(2,) + rel, rel_edge=(2,) + rel_edge, sums=(devices,) + sums),
        [local(coefs)] * 2 + [local(first)] * 2 + [local(sums)],
    )
    totals = lax.all_to_all(r.sums, ("gz", "gy"), 0, 0)
    e = call(
        products,
        dict(
            own=r.rel,
            own_edge=r.rel_edge,
            mid=n.rel,
            mid_edge=n.rel_edge,
            rel4=n.rel4,
            rel4_edge=n.rel4_edge,
            rel=d.rel, rel_edge=d.rel_edge,
            rel7=c.rel,
            rel7_edge=c.rel_edge,
        ),
        dict(gram=gram, far=gram, mid=gram, both=(2 * gram[0], width)),
        [local((len(PAIRS) * tall, width)), local((len(PAIRS), groups * BLOCK, width // BLOCK))],
    )
    both = moved("both", e.both, (1, 0), (-1, 0))
    same = moved("same", e.far, (2, 0), (-2, 0))
    crossed = moved("crossed", e.gram, (-1, 0), (1, 0))
    finish = functools.partial(finish_own, float(cells))
    finish.__name__ = "finish_own"
    result = [
        local((planes, fields, half, width)),
        local((len(PAIRS), 2 * groups, width)),
        pltpu.SemaphoreType.DMA((planes,)),
    ]
    mine = call(
        finish,
        dict(totals=totals, gram=e.gram, same=same, mid=e.mid, far=r.rel, near=n.rel),
        dict(prolong=tv.shape, mine=(len(PAIRS), groups, width // BLOCK), scales=sums),
        result,
        far=("prolong",),
    )
    whole = call(
        finish_other,
        dict(
            last=last,
            back=back,
            back4=back4,
            both=both,
            cross=crossed,
            scales=mine.scales,
            mine=mine.mine,
            own_part=mine.prolong,
        ),
        dict(prolong=tv.shape, factors=(len(PAIRS), planes // BLOCK, rows // BLOCK, width // BLOCK)),
        result,
        far=("prolong", "own_part"),
        alias=dict(own_part="prolong"),
    )
    return whole.prolong, whole.factors


def solution(mesh):
    return jax.shard_map(
        body,
        mesh=mesh,
        in_specs=(P(None, "gz", "gy", None), P("gz", "gy", None)),
        out_specs=(P(None, "gz", "gy", None), P(None, "gz", "gy", None)),
        check_vma=False,
    )
```

time: 178 us -> 62 us (0.35)
  blocking collectives: 51.8 us -> 0 us
  waiting for transfers between devices: 62.2 us -> 15.4 us
  local copies, waits for them, and re-layouts: 23.2 us -> 2.4 us
  other arithmetic: 16.1 us -> 0 us
  Pallas kernels: 0 us -> 14.5 us
  starting transfers between devices: 22 us -> 28.8 us
    psum x1 -> x0, blocking collectives: 51.8 us -> none  [body(): totals = lax.psum(squares, ('gz', 'gy'))]
    ppermute x12 -> x16, waiting for transfers between devices: 62.2 us -> 15.4 us  [moved(): return lax.ppermute(x, ('gz', 'gy'), route)]
    pallas_call x0 -> x13, Pallas kernels: none -> 14.5 us  [call(): pl.pallas_call(kernel, out_shape=[jax.ShapeDtypeStruct(outs[k], jnp.float...]
    another operation x27 -> x0, local copies, waits for them, and re-layouts: 10.8 us -> none  [the longest x11 9.93 us: pair_products(): jnp.stack([fields[left_idx] * fields[right_idx] for left_idx, right_idx i...]
    unnamed x32 -> x4, local copies, waits for them, and re-layouts: 9.12 us -> 2.4 us
    reduce_sum x2 -> x0, other arithmetic: 6.44 us -> none  [the longest x1 3.34 us: block_sums(): values.reshape(number, layers // 4, 4, height // 4, 4, across)]
    all_to_all x0 -> x1, starting transfers between devices: none -> 4.18 us  [body(): totals = lax.all_to_all(r.sums, ('gz', 'gy'), 0, 0)]
    sub x1 -> x0, other arithmetic: 2.76 us -> none  [sweep(): return center_vals - RELAX_WEIGHT * fluxes / diagonal]
  transfers between devices with their start and end apart: 12 -> 17, of which waited for: 9 -> 7; matrix products, arithmetic and copies ran while one was open for 1% -> 0% of each run, Pallas kernels for 0% -> 18%
where the time goes in v2:
time: 62 us; the launch traced here: 61.8 us
  starting transfers between devices  28.8 us (46%)
  waiting for transfers between devices  15.4 us (25%)
  Pallas kernels  14.5 us (23%)
  local copies, waits for them, and re-layouts  2.4 us (4%)
  between operations  0.76 us (1%)
    ppermute x16, starting transfers between devices, moved(): return lax.ppermute(x, ('gz', 'gy'), route)  24.6 us
    ppermute x16, waiting for transfers between devices, moved(): return lax.ppermute(x, ('gz', 'gy'), route)  15.4 us
    pallas_call x13, Pallas kernels, call(): pl.pallas_call(kernel, out_shape=[jax.ShapeDtypeStruct(outs[k], jnp.float...  14.5 us
    all_to_all x1, starting transfers between devices, body(): totals = lax.all_to_all(r.sums, ('gz', 'gy'), 0, 0)  4.18 us
    unnamed x4, local copies, waits for them, and re-layouts  2.4 us
  transfers between devices with their start and end apart: 17, of which 7 were waited for; matrix products, arithmetic and copies ran while one was open for 0% of the time, Pallas kernels for 18%

profile of v2, /device:TPU:0, one launch (start us, length us, event | category | flops | bytes accessed | tf_op | source)
XLA Modules:
  0.0 61.8 jit_solution(9965003517304820748)
XLA Ops:
  0.6 0.0 copy-start
  0.6 1.4 %copy-done = f32[4,4,96,256]{3,2,1,0:T(8,128)S(1)} copy-done((f32[4,4,96,256]{3,2,1,0:T(8,128)S(1)}, f32[4,4,96,256]{3,2,1,0:T(8,128)}, u32[]{:S(2)}) %copy-start) | copy-done | bytes 1572888
  2.0 0.0 copy-start.1
  2.0 1.0 %copy-done.1 = f32[4,96,256]{2,1,0:T(8,128)S(1)} copy-done((f32[4,96,256]{2,1,0:T(8,128)S(1)}, f32[4,96,256]{2,1,0:T(8,128)}, u32[]{:S(2)}) %copy-start.1) | copy-done | bytes 393240
  3.0 0.7 %pack_first.1 = (f32[5,64,256]{2,1,0:T(8,128)S(1)}, f32[2,5,48,256]{3,2,1,0:T(8,128)S(1)}, f32[2,5,8,256]{3,2,1,0:T(8,128)S(1)}, f32[2,5,8,256]{3,2,1,0:T(8,128)S(1)}) custom-call(f32[4,4,96,256]{3,2,1,0:T(8,128)S(1)} %copy-done, f32[4,96,256]{2,1,0:T(8,128)S(1)} %copy-done.1), custom_call_target="tpu_custom_call" | custom-call | tf_op jit(solution)/shard_map/pack_first/pallas_call | solution.py:32
  3.7 3.0 %collective-permute-start = (f32[5,64,256]{2,1,0:T(8,128)S(1)}, f32[5,64,256]{2,1,0:T(8,128)S(1)}, u32[]{:S(2)}, u32[]{:S(2)}) collective-permute-start(f32[5,64,256]{2,1,0:T(8,128)S(1)} %get-tuple-element.47), channel_id=1, source_target_pairs={{0,4},{1,5},{2,6},{3,7},{4,0},{5,1},{6,2},{7,3},{8,12},{9,13},{10,... | collective-permute-start | bytes 983048 | tf_op jit(solution)/shard_map/far0/ppermute | solution.py:494
  6.7 0.0 collective-permute-start.1
  6.7 1.7 %collective-permute-start.2 = (f32[2,5,8,256]{3,2,1,0:T(8,128)S(1)}, f32[2,5,8,256]{3,2,1,0:T(8,128)S(1)}, u32[]{:S(2)}, u32[]{:S(2)}) collective-permute-start(f32[2,5,8,256]{3,2,1,0:T(8,128)S(1)} %get-tuple-element.49), channel_id=1, source_target_pairs={{0,3},{1,0},{2,1},{3,2},{4,5},{5,6},{6,7},{7,4},{8,11},{9,8},{10,9... | collective-permute-start | bytes 245768 | tf_op jit(solution)/shard_map/cross/ppermute | solution.py:494
  8.5 3.6 %collective-permute-start.7 = (f32[2,5,48,256]{3,2,1,0:T(8,128)S(1)}, f32[2,5,48,256]{3,2,1,0:T(8,128)S(1)}, u32[]{:S(2)}, u32[]{:S(2)}) collective-permute-start(f32[2,5,48,256]{3,2,1,0:T(8,128)S(1)} %get-tuple-element.50.refs_2_), channel_id=1, source_target_pairs={{0,24},{1,25},{2,26},{3,27},{4,12},{5,13},{6,14},{7,15},{8,0},{9,1... | collective-permute-start | bytes 1474568 | tf_op jit(solution)/shard_map/after/ppermute | solution.py:494
  12.1 0.0 collective-permute-done.1.refs_0_
  12.1 0.0 collective-permute-done.2.refs_1_
  12.1 0.6 pack_second.1
  12.7 2.2 %collective-permute-start.4 = (f32[2,5,8,256]{3,2,1,0:T(8,128)S(1)}, f32[2,5,8,256]{3,2,1,0:T(8,128)S(1)}, u32[]{:S(2)}, u32[]{:S(2)}) collective-permute-start(f32[2,5,8,256]{3,2,1,0:T(8,128)S(1)} %get-tuple-element.54), channel_id=1, source_target_pairs={{0,24},{1,25},{2,26},{3,27},{4,12},{5,13},{6,14},{7,15},{8,0},{9,1... | collective-permute-start | bytes 245768 | tf_op jit(solution)/shard_map/after_edge/ppermute | solution.py:494
  14.8 0.0 collective-permute-start.3
  14.8 0.0 collective-permute-done.refs_0_
  14.8 0.3 pack_near.1
  15.2 2.1 %collective-permute-start.5 = (f32[5,48,256]{2,1,0:T(8,128)S(1)}, f32[5,48,256]{2,1,0:T(8,128)S(1)}, u32[]{:S(2)}, u32[]{:S(2)}) collective-permute-start(f32[5,48,256]{2,1,0:T(8,128)S(1)} %get-tuple-element.57), channel_id=1, source_target_pairs={{0,4},{1,5},{2,6},{3,7},{4,0},{5,1},{6,2},{7,3},{8,12},{9,13},{10,... | collective-permute-start | bytes 737288 | tf_op jit(solution)/shard_map/near5/ppermute | solution.py:494
  17.2 0.9 %collective-permute-start.6 = (f32[5,48,256]{2,1,0:T(8,128)S(1)}, f32[5,48,256]{2,1,0:T(8,128)S(1)}, u32[]{:S(2)}, u32[]{:S(2)}) collective-permute-start(f32[5,48,256]{2,1,0:T(8,128)S(1)} %get-tuple-element.59), channel_id=1, source_target_pairs={{0,8},{1,9},{2,10},{3,11},{4,28},{5,29},{6,30},{7,31},{8,16},{9,17... | collective-permute-start | bytes 737288 | tf_op jit(solution)/shard_map/prev0/ppermute | solution.py:494
  18.2 7.4 %collective-permute-done.4.refs_2_ = f32[2,5,8,256]{3,2,1,0:T(8,128)S(1)} collective-permute-done((f32[2,5,8,256]{3,2,1,0:T(8,128)S(1)}, f32[2,5,8,256]{3,2,1,0:T(8,128)S(1)}, u32[]{:S(2)}, u32[]{:S(2)}) %collective-permute-start.4) | collective-permute-done | bytes 81952 | tf_op jit(solution)/shard_map/after_edge/ppermute | solution.py:494
  25.5 0.2 collective-permute-start.9
  25.7 0.8 %early.1 = (f32[5,56,256]{2,1,0:T(8,128)S(1)}, f32[5,56,256]{2,1,0:T(8,128)S(1)}, f32[4,56,256]{2,1,0:T(8,128)S(1)}, f32[4,56,256]{2,1,0:T(8,128)S(1)}) custom-call(f32[2,5,56,256]{3,2,1,0:T(8,128)S(1)} %get-tuple-element.52.refs_0_.refs_2_, f32[2,5,56,256]{3,2,1,0:T(8,128)S(1)} %get-tuple-element.53.refs_1_.refs_0_, ...), custom_call_target="tpu_custom_call" | custom-call | tf_op jit(solution)/shard_map/early/pallas_call | solution.py:32
  26.5 0.0 collective-permute-done.3.refs_1_
  26.5 0.1 pack_third.1
  26.6 0.1 collective-permute-start.12
  26.6 0.0 collective-permute-done.7.refs_1_
  26.6 0.8 %outer.1 = (f32[5,56,256]{2,1,0:T(8,128)S(1)}, f32[4,56,256]{2,1,0:T(8,128)S(1)}, f32[4,56,256]{2,1,0:T(8,128)S(1)}) custom-call(f32[2,5,56,256]{3,2,1,0:T(8,128)S(1)} %get-tuple-element.56.refs_0_.refs_1_, f32[2,5,48,256]{3,2,1,0:T(8,128)S(1)} %collective-permute-done.7.refs_1_, f32[2,5,8,256]{3,2,1,0:T(8,128)S(1)} %collective-permute-done.4.refs_2_), custom_call_target="tpu_custom_call" | custom-call | tf_op jit(solution)/shard_map/outer/pallas_call | solution.py:32
  27.5 2.6 %collective-permute-done.5.refs_1_.refs_2_ = f32[5,48,256]{2,1,0:T(8,128)S(1)} collective-permute-done((f32[5,48,256]{2,1,0:T(8,128)S(1)}, f32[5,48,256]{2,1,0:T(8,128)S(1)}, u32[]{:S(2)}, u32[]{:S(2)}) %collective-permute-start.5) | collective-permute-done | bytes 245792 | tf_op jit(solution)/shard_map/near5/ppermute | solution.py:494
  30.1 0.7 %collective-permute-done.6.refs_3_.refs_0_ = f32[5,48,256]{2,1,0:T(8,128)S(1)} collective-permute-done((f32[5,48,256]{2,1,0:T(8,128)S(1)}, f32[5,48,256]{2,1,0:T(8,128)S(1)}, u32[]{:S(2)}, u32[]{:S(2)}) %collective-permute-start.6) | collective-permute-done | bytes 245792 | tf_op jit(solution)/shard_map/prev0/ppermute | solution.py:494
  30.8 0.7 %inner_last.1 = (f32[5,56,256]{2,1,0:T(8,128)S(1)}, f32[4,56,256]{2,1,0:T(8,128)S(1)}, f32[4,48,256]{2,1,0:T(8,128)S(1)}, f32[4,8,256]{2,1,0:T(8,128)S(1)}) custom-call(f32[2,5,56,256]{3,2,1,0:T(8,128)S(1)} %get-tuple-element.56.refs_0_.refs_1_, f32[5,48,256]{2,1,0:T(8,128)S(1)} %collective-permute-done.5.refs_1_.refs_2_, ...), custom_call_target="tpu_custom_call" | custom-call | tf_op jit(solution)/shard_map/inner_last/pallas_call | solution.py:32
  31.5 3.7 %collective-permute-start.8 = (f32[4,48,256]{2,1,0:T(8,128)S(1)}, f32[4,48,256]{2,1,0:T(8,128)S(1)}, u32[]{:S(2)}, u32[]{:S(2)}) collective-permute-start(f32[4,48,256]{2,1,0:T(8,128)S(1)} %get-tuple-element.63.refs_10_.refs_8_), channel_id=1, source_target_pairs={{0,4},{1,5},{2,6},{3,7},{4,0},{5,1},{6,2},{7,3},{8,12},{9,13},{10,... | collective-permute-start | bytes 589832 | tf_op jit(solution)/shard_map/last/ppermute | solution.py:494
  35.2 0.2 collective-permute-done.9.refs_3_.refs_1_
  35.4 1.6 %inner.1 = (f32[5,56,256]{2,1,0:T(8,128)S(1)}, f32[5,56,256]{2,1,0:T(8,128)}, f32[4,56,256]{2,1,0:T(8,128)S(1)}, f32[4,56,256]{2,1,0:T(8,128)S(1)}, f32[2,4,48,2...) custom-call(f32[2,5,56,256]{3,2,1,0:T(8,128)S(1)} %get-tuple-element.53.refs_1_.refs_0_, ...), custom_call_target="tpu_custom_call" | custom-call | flops 10000000000 | tf_op jit(solution)/shard_map/inner/pallas_call | solution.py:32
  37.0 0.0 collective-permute-start.10
  37.0 1.4 %near_rest.1 = (f32[2,4,48,256]{3,2,1,0:T(8,128)S(1)}, f32[2,4,8,256]{3,2,1,0:T(8,128)S(1)}, f32[4,48,256]{2,1,0:T(8,128)S(1)}, f32[4,8,256]{2,1,0:T(8,128)S(1)}, f32[8,128]{1,0:T(8,128)S(1)}) custom-call(f32[2,5,56,256]{3,2,1,0:T(8,128)S(1)} %get-tuple-element.53.refs_1_.refs_0_, f32[5,48,256]{2,1,0:T(8,128)S(1)} %collective-permute-done.9.refs_3_.refs_1_, ...), custom_call_target="tpu_custom_call" | custom-call | tf_op jit(solution)/shard_map/near_rest/pallas_call | solution.py:32
  38.4 2.8 %collective-permute-done.12.refs_1_ = f32[5,64,256]{2,1,0:T(8,128)S(1)} collective-permute-done((f32[5,64,256]{2,1,0:T(8,128)S(1)}, f32[5,64,256]{2,1,0:T(8,128)S(1)}, u32[]{:S(2)}, u32[]{:S(2)}) %collective-permute-start.12) | collective-permute-done | bytes 327712 | tf_op jit(solution)/shard_map/prev1/ppermute | solution.py:494
  41.2 0.0 collective-permute-done.8.refs_7_.refs_0_
  41.2 2.3 %far_rest.1 = (f32[2,4,48,256]{3,2,1,0:T(8,128)S(1)}, f32[2,4,8,256]{3,2,1,0:T(8,128)S(1)}, f32[32,8,128]{2,1,0:T(8,128)}) custom-call(f32[5,48,256]{2,1,0:T(8,128)S(1)} %collective-permute-done.6.refs_3_.refs_0_, f32[5,64,256]{2,1,0:T(8,128)S(1)} %collective-permute-done.12.refs_1_, f32[2,5,56,256]{3,2,1,0:T(8,128)S(1)} %get-tuple-element.52.refs_0_.refs_2_, ...), custom_call_target="tpu_custom_call" | custom-call | tf_op jit(solution)/shard_map/far_rest/pallas_call | solution.py:32
  43.5 4.2 %all-to-all-start = ((f32[32,8,128]{2,1,0:T(8,128)}), f32[32,8,128]{2,1,0:T(8,128)S(1)}, u32[]{:S(2)}, u32[]{:S(2)}) async-start(f32[32,8,128]{2,1,0:T(8,128)} %get-tuple-element.86), calls=%async_computation | async-start | bytes 262144 | tf_op jit(solution)/shard_map/all_to_all | solution.py:616
  47.7 1.8 %collective-permute-start.11 = (f32[4,48,256]{2,1,0:T(8,128)S(1)}, f32[4,48,256]{2,1,0:T(8,128)S(1)}, u32[]{:S(2)}, u32[]{:S(2)}) collective-permute-start(f32[4,48,256]{2,1,0:T(8,128)S(1)} %get-tuple-element.74.refs_4_), channel_id=1, source_target_pairs={{0,4},{1,5},{2,6},{3,7},{4,0},{5,1},{6,2},{7,3},{8,12},{9,13},{10,... | collective-permute-start | bytes 589832 | tf_op jit(solution)/shard_map/back4/ppermute | solution.py:494
  49.5 1.0 %products.1 = (f32[48,256]{1,0:T(8,128)S(1)}, f32[48,256]{1,0:T(8,128)S(1)}, f32[48,256]{1,0:T(8,128)S(1)}, f32[96,256]{1,0:T(8,128)S(1)}) custom-call(f32[2,4,48,256]{3,2,1,0:T(8,128)S(1)} %get-tuple-element.77.refs_0_.refs_4_, f32[2,4,8,256]{3,2,1,0:T(8,128)S(1)} %get-tuple-element.78.refs_1_, f32[2,4,48,256]{3,2,1,0:T(8,128)S(1)} %get-tuple-element.79.refs_2_.refs_5_, ...), custom_call_target="tpu_custom_call" | custom-call | tf_op jit(solution)/shard_map/products/pallas_call | solution.py:32
  50.6 0.3 collective-permute-start.13
  50.8 1.8 %collective-permute-start.15 = (f32[48,256]{1,0:T(8,128)S(1)}, f32[48,256]{1,0:T(8,128)S(1)}, u32[]{:S(2)}, u32[]{:S(2)}) collective-permute-start(f32[48,256]{1,0:T(8,128)S(1)} %get-tuple-element.87), channel_id=1, source_target_pairs={{0,8},{1,9},{2,10},{3,11},{4,28},{5,29},{6,30},{7,31},{8,16},{9,17... | collective-permute-start | bytes 147464 | tf_op jit(solution)/shard_map/same/ppermute | solution.py:494
  52.6 3.3 %collective-permute-start.14 = (f32[48,256]{1,0:T(8,128)S(1)}, f32[48,256]{1,0:T(8,128)S(1)}, u32[]{:S(2)}, u32[]{:S(2)}) collective-permute-start(f32[48,256]{1,0:T(8,128)S(1)} %get-tuple-element.85.refs_1_), channel_id=1, source_target_pairs={{0,28},{1,29},{2,30},{3,31},{4,8},{5,9},{6,10},{7,11},{8,4},{9,5},... | collective-permute-start | bytes 147464 | tf_op jit(solution)/shard_map/crossed/ppermute | solution.py:494
  55.9 1.2 %collective-permute-done.15.refs_2_ = f32[48,256]{1,0:T(8,128)S(1)} collective-permute-done((f32[48,256]{1,0:T(8,128)S(1)}, f32[48,256]{1,0:T(8,128)S(1)}, u32[]{:S(2)}, u32[]{:S(2)}) %collective-permute-start.15) | collective-permute-done | bytes 49184 | tf_op jit(solution)/shard_map/same/ppermute | solution.py:494
  57.1 0.0 all-to-all-done.refs_0_
  57.1 1.8 %finish_own.1 = (f32[4,4,96,256]{3,2,1,0:T(8,128)}, f32[10,16,64]{2,1,0:T(8,128)S(1)}, f32[8,128]{1,0:T(8,128)S(1)}) custom-call(f32[32,8,128]{2,1,0:T(8,128)S(1)} %all-to-all-done.refs_0_, f32[48,256]{1,0:T(8,128)S(1)} %get-tuple-element.85.refs_1_, f32[48,256]{1,0:T(8,128)S(1)} %collective-permute-done.15.refs_2_, ...), custom_call_target="tpu_custom_call" | custom-call | tf_op jit(solution)/shard_map/finish_own/pallas_call | solution.py:32
  59.0 0.0 collective-permute-done.11.refs_2_
  59.0 0.4 collective-permute-done.14.refs_4_
  59.4 0.0 collective-permute-done.13.refs_3_
  59.4 0.0 collective-permute-done.10.refs_1_
  59.4 2.4 %finish_other.1 = (f32[4,4,96,256]{3,2,1,0:T(8,128)}, f32[10,1,24,64]{3,2,1,0:T(8,128)}) custom-call(f32[4,48,256]{2,1,0:T(8,128)S(1)} %collective-permute-done.8.refs_7_.refs_0_, f32[2,4,48,256]{3,2,1,0:T(8,128)S(1)} %collective-permute-done.10.refs_1_, f32[4,48,256]{2,1,0:T(8,128)S(1)} %collective-permute-done.11.refs_2_, ...), custom_call_target="tpu_custom_call", output_to_operand_aliasing={{0}: (7, {})} | custom-call | tf_op jit(solution)/shard_map/finish_other/pallas_call | solution.py:32
Async XLA Ops:
  0.6 1.4 %copy-start = (f32[4,4,96,256]{3,2,1,0:T(8,128)S(1)}, f32[4,4,96,256]{3,2,1,0:T(8,128)}, u32[]{:S(2)}) copy-start(f32[4,4,96,256]{3,2,1,0:T(8,128)} %refs_1_.3) | copy-start | bytes 4718596
  2.0 1.0 %copy-start.1 = (f32[4,96,256]{2,1,0:T(8,128)S(1)}, f32[4,96,256]{2,1,0:T(8,128)}, u32[]{:S(2)}) copy-start(f32[4,96,256]{2,1,0:T(8,128)} %refs_2_.1) | copy-start | bytes 1179652
  3.7 11.1 %collective-permute-start = (f32[5,64,256]{2,1,0:T(8,128)S(1)}, f32[5,64,256]{2,1,0:T(8,128)S(1)}, u32[]{:S(2)}, u32[]{:S(2)}) collective-permute-start(f32[5,64,256]{2,1,0:T(8,128)S(1)} %get-tuple-element.47), channel_id=1, source_target_pairs={{0,4},{1,5},{2,6},{3,7},{4,0},{5,1},{6,2},{7,3},{8,12},{9,13},{10,... | collective-permute-start | bytes 983048 | tf_op jit(solution)/shard_map/far0/ppermute | solution.py:494
  6.7 5.4 %collective-permute-start.1 = (f32[2,5,8,256]{3,2,1,0:T(8,128)S(1)}, f32[2,5,8,256]{3,2,1,0:T(8,128)S(1)}, u32[]{:S(2)}, u32[]{:S(2)}) collective-permute-start(f32[2,5,8,256]{3,2,1,0:T(8,128)S(1)} %get-tuple-element.48), channel_id=1, source_target_pairs={{0,1},{1,2},{2,3},{3,0},{4,7},{5,4},{6,5},{7,6},{8,9},{9,10},{10,1... | collective-permute-start | bytes 245768 | tf_op jit(solution)/shard_map/halo/ppermute | solution.py:494
  6.7 5.4 %collective-permute-start.2 = (f32[2,5,8,256]{3,2,1,0:T(8,128)S(1)}, f32[2,5,8,256]{3,2,1,0:T(8,128)S(1)}, u32[]{:S(2)}, u32[]{:S(2)}) collective-permute-start(f32[2,5,8,256]{3,2,1,0:T(8,128)S(1)} %get-tuple-element.49), channel_id=1, source_target_pairs={{0,3},{1,0},{2,1},{3,2},{4,5},{5,6},{6,7},{7,4},{8,11},{9,8},{10,9... | collective-permute-start | bytes 245768 | tf_op jit(solution)/shard_map/cross/ppermute | solution.py:494
  8.5 18.1 %collective-permute-start.7 = (f32[2,5,48,256]{3,2,1,0:T(8,128)S(1)}, f32[2,5,48,256]{3,2,1,0:T(8,128)S(1)}, u32[]{:S(2)}, u32[]{:S(2)}) collective-permute-start(f32[2,5,48,256]{3,2,1,0:T(8,128)S(1)} %get-tuple-element.50.refs_2_), channel_id=1, source_target_pairs={{0,24},{1,25},{2,26},{3,27},{4,12},{5,13},{6,14},{7,15},{8,0},{9,1... | collective-permute-start | bytes 1474568 | tf_op jit(solution)/shard_map/after/ppermute | solution.py:494
  12.7 12.8 %collective-permute-start.4 = (f32[2,5,8,256]{3,2,1,0:T(8,128)S(1)}, f32[2,5,8,256]{3,2,1,0:T(8,128)S(1)}, u32[]{:S(2)}, u32[]{:S(2)}) collective-permute-start(f32[2,5,8,256]{3,2,1,0:T(8,128)S(1)} %get-tuple-element.54), channel_id=1, source_target_pairs={{0,24},{1,25},{2,26},{3,27},{4,12},{5,13},{6,14},{7,15},{8,0},{9,1... | collective-permute-start | bytes 245768 | tf_op jit(solution)/shard_map/after_edge/ppermute | solution.py:494
  14.8 11.7 %collective-permute-start.3 = (f32[5,64,256]{2,1,0:T(8,128)S(1)}, f32[5,64,256]{2,1,0:T(8,128)S(1)}, u32[]{:S(2)}, u32[]{:S(2)}) collective-permute-start(f32[5,64,256]{2,1,0:T(8,128)S(1)} %get-tuple-element.51), channel_id=1, source_target_pairs={{0,4},{1,5},{2,6},{3,7},{4,0},{5,1},{6,2},{7,3},{8,12},{9,13},{10,... | collective-permute-start | bytes 983048 | tf_op jit(solution)/shard_map/far1/ppermute | solution.py:494
  15.2 14.9 %collective-permute-start.5 = (f32[5,48,256]{2,1,0:T(8,128)S(1)}, f32[5,48,256]{2,1,0:T(8,128)S(1)}, u32[]{:S(2)}, u32[]{:S(2)}) collective-permute-start(f32[5,48,256]{2,1,0:T(8,128)S(1)} %get-tuple-element.57), channel_id=1, source_target_pairs={{0,4},{1,5},{2,6},{3,7},{4,0},{5,1},{6,2},{7,3},{8,12},{9,13},{10,... | collective-permute-start | bytes 737288 | tf_op jit(solution)/shard_map/near5/ppermute | solution.py:494
  17.2 13.5 %collective-permute-start.6 = (f32[5,48,256]{2,1,0:T(8,128)S(1)}, f32[5,48,256]{2,1,0:T(8,128)S(1)}, u32[]{:S(2)}, u32[]{:S(2)}) collective-permute-start(f32[5,48,256]{2,1,0:T(8,128)S(1)} %get-tuple-element.59), channel_id=1, source_target_pairs={{0,8},{1,9},{2,10},{3,11},{4,28},{5,29},{6,30},{7,31},{8,16},{9,17... | collective-permute-start | bytes 737288 | tf_op jit(solution)/shard_map/prev0/ppermute | solution.py:494
  25.5 9.8 %collective-permute-start.9 = (f32[5,48,256]{2,1,0:T(8,128)S(1)}, f32[5,48,256]{2,1,0:T(8,128)S(1)}, u32[]{:S(2)}, u32[]{:S(2)}) collective-permute-start(f32[5,48,256]{2,1,0:T(8,128)S(1)} %get-tuple-element.64), channel_id=1, source_target_pairs={{0,4},{1,5},{2,6},{3,7},{4,0},{5,1},{6,2},{7,3},{8,12},{9,13},{10,... | collective-permute-start | bytes 737288 | tf_op jit(solution)/shard_map/near4/ppermute | solution.py:494
  26.6 14.7 %collective-permute-start.12 = (f32[5,64,256]{2,1,0:T(8,128)S(1)}, f32[5,64,256]{2,1,0:T(8,128)S(1)}, u32[]{:S(2)}, u32[]{:S(2)}) collective-permute-start(f32[5,64,256]{2,1,0:T(8,128)S(1)} %get-tuple-element.75), channel_id=1, source_target_pairs={{0,8},{1,9},{2,10},{3,11},{4,28},{5,29},{6,30},{7,31},{8,16},{9,17... | collective-permute-start | bytes 983048 | tf_op jit(solution)/shard_map/prev1/ppermute | solution.py:494
  31.5 9.8 %collective-permute-start.8 = (f32[4,48,256]{2,1,0:T(8,128)S(1)}, f32[4,48,256]{2,1,0:T(8,128)S(1)}, u32[]{:S(2)}, u32[]{:S(2)}) collective-permute-start(f32[4,48,256]{2,1,0:T(8,128)S(1)} %get-tuple-element.63.refs_10_.refs_8_), channel_id=1, source_target_pairs={{0,4},{1,5},{2,6},{3,7},{4,0},{5,1},{6,2},{7,3},{8,12},{9,13},{10,... | collective-permute-start | bytes 589832 | tf_op jit(solution)/shard_map/last/ppermute | solution.py:494
  37.0 22.4 %collective-permute-start.10 = (f32[2,4,48,256]{3,2,1,0:T(8,128)S(1)}, f32[2,4,48,256]{3,2,1,0:T(8,128)S(1)}, u32[]{:S(2)}, u32[]{:S(2)}) collective-permute-start(f32[2,4,48,256]{3,2,1,0:T(8,128)S(1)} %get-tuple-element.67.refs_9_.refs_6_), channel_id=1, source_target_pairs={{0,4},{1,5},{2,6},{3,7},{4,0},{5,1},{6,2},{7,3},{8,12},{9,13},{10,... | collective-permute-start | bytes 1179656 | tf_op jit(solution)/shard_map/back/ppermute | solution.py:494
  43.5 13.6 %all-to-all-start = ((f32[32,8,128]{2,1,0:T(8,128)}), f32[32,8,128]{2,1,0:T(8,128)S(1)}, u32[]{:S(2)}, u32[]{:S(2)}) async-start(f32[32,8,128]{2,1,0:T(8,128)} %get-tuple-element.86), calls=%async_computation | async-start | bytes 262144 | tf_op jit(solution)/shard_map/all_to_all | solution.py:616
  47.7 11.3 %collective-permute-start.11 = (f32[4,48,256]{2,1,0:T(8,128)S(1)}, f32[4,48,256]{2,1,0:T(8,128)S(1)}, u32[]{:S(2)}, u32[]{:S(2)}) collective-permute-start(f32[4,48,256]{2,1,0:T(8,128)S(1)} %get-tuple-element.74.refs_4_), channel_id=1, source_target_pairs={{0,4},{1,5},{2,6},{3,7},{4,0},{5,1},{6,2},{7,3},{8,12},{9,13},{10,... | collective-permute-start | bytes 589832 | tf_op jit(solution)/shard_map/back4/ppermute | solution.py:494
  50.6 8.8 %collective-permute-start.13 = (f32[96,256]{1,0:T(8,128)S(1)}, f32[96,256]{1,0:T(8,128)S(1)}, u32[]{:S(2)}, u32[]{:S(2)}) collective-permute-start(f32[96,256]{1,0:T(8,128)S(1)} %get-tuple-element.84), channel_id=1, source_target_pairs={{0,4},{1,5},{2,6},{3,7},{4,0},{5,1},{6,2},{7,3},{8,12},{9,13},{10,... | collective-permute-start | bytes 294920 | tf_op jit(solution)/shard_map/both/ppermute | solution.py:494
  50.8 6.3 %collective-permute-start.15 = (f32[48,256]{1,0:T(8,128)S(1)}, f32[48,256]{1,0:T(8,128)S(1)}, u32[]{:S(2)}, u32[]{:S(2)}) collective-permute-start(f32[48,256]{1,0:T(8,128)S(1)} %get-tuple-element.87), channel_id=1, source_target_pairs={{0,8},{1,9},{2,10},{3,11},{4,28},{5,29},{6,30},{7,31},{8,16},{9,17... | collective-permute-start | bytes 147464 | tf_op jit(solution)/shard_map/same/ppermute | solution.py:494
  52.6 6.8 %collective-permute-start.14 = (f32[48,256]{1,0:T(8,128)S(1)}, f32[48,256]{1,0:T(8,128)S(1)}, u32[]{:S(2)}, u32[]{:S(2)}) collective-permute-start(f32[48,256]{1,0:T(8,128)S(1)} %get-tuple-element.85.refs_1_), channel_id=1, source_target_pairs={{0,28},{1,29},{2,30},{3,31},{4,8},{5,9},{6,10},{7,11},{8,4},{9,5},... | collective-permute-start | bytes 147464 | tf_op jit(solution)/shard_map/crossed/ppermute | solution.py:494

commit v3 on v2

--- a/solution.py
+++ b/solution.py
@@ -13,11 +13,12 @@
 BLOCK = 4
 EDGE = 8
 VMEM_LIMIT = 40 * 1024 * 1024
-
-COST = {'inner': 10, 'pack_near': 8}
-
-
-def call(body, ins, outs, scratch=(), far=(), alias=None):
+FIRST_LIMIT = 60 * 1024 * 1024
+
+COST = {'inner': 10, 'pack_near': 8, 'early': 3, 'arrived': 1, 'near_rest': 3}
+
+
+def call(body, ins, outs, scratch=(), far=(), limit=VMEM_LIMIT):
     names_in, names_out = list(ins), list(outs)
 
     def kernel(*refs):
@@ -27,7 +28,7 @@
         body(i, o, *refs[cut:])
 
     def spec(name):
-        return pl.BlockSpec(memory_space=pltpu.HBM if name in far else pltpu.VMEM)
+        return pl.BlockSpec(memory_space=pl.ANY if name in far or name == "gate" else pltpu.VMEM)
 
     got = pl.pallas_call(
         kernel,
@@ -35,8 +36,7 @@
         in_specs=[spec(k) for k in names_in],
         out_specs=[spec(k) for k in names_out],
         scratch_shapes=list(scratch),
-        input_output_aliases={names_in.index(a): names_out.index(b) for a, b in (alias or {}).items()},
-        compiler_params=pltpu.CompilerParams(vmem_limit_bytes=VMEM_LIMIT),
+        compiler_params=pltpu.CompilerParams(vmem_limit_bytes=limit),
         cost_estimate=pl.CostEstimate(flops=int(COST.get(body.__name__, 0) * 1e9), bytes_accessed=0, transcendentals=0),
         name=body.__name__,
     )(*[ins[k] for k in names_in])
@@ -101,8 +101,6 @@
     jobs = tile_jobs(i, half - EDGE * (1 - odd), extra)
     jobs += tile_jobs(i, (rows - EDGE) * (1 - odd), halo) + tile_jobs(i, (rows - EDGE) * odd, cross)
     jobs += plane_jobs(i, 0, odd, (1 - odd) * half, o.far0)
-    for k in range(2):
-        jobs += plane_jobs(i, k, odd, odd * half, o.own.at[k])
     started = copies(jobs, sems)
     for one in started[:6]:
         one.wait()
@@ -113,7 +111,18 @@
             o.halo[q, f] = packed(halo, q, f, 1 - odd, odd, which)
             o.cross[q, f] = packed(cross, q, f, odd, odd, which)
     more = [(edge.at[q], o.far0.at[:, pl.ds(half + q * EDGE, EDGE), :]) for q in range(planes // 2)]
+    o.mark[...] = jnp.zeros_like(o.mark)
     for one in started[6:] + copies(more, late_sems):
+        one.wait()
+
+
+def pack_own(i, o, sems):
+    odd = parity()
+    half = i.tv.shape[2] // 2
+    jobs = []
+    for k in range(2):
+        jobs += plane_jobs(i, k, odd, odd * half, o.own.at[k])
+    for one in copies(jobs, sems):
         one.wait()
 
 
@@ -149,7 +158,6 @@
     for k in range(2):
         jobs += plane_jobs(i, 2 + k, odd, (1 - odd) * half, (o.send1 if k else o.send0))
     started = copies(jobs, sems)
-    o.on[...] = i.far0[:, :half]
     for one in started:
         one.wait()
 
@@ -168,9 +176,6 @@
                 plane = (i.far1 if k else i.far0)[f, :half]
                 o.far[k, f, :half] = plane
                 o.far[k, f, half:] = tile
-                o.send[f, pl.ds(half + (1 - k) * EDGE, EDGE), :] = tile
-                if k == 1:
-                    o.send[f, :half] = plane
             else:
                 o.near_edge[k - 2, f] = tile
 
@@ -254,14 +259,24 @@
     sweep_second({6: o.f6, 7: i.f7, 8: i.f8}, 7, i.c7, o.rel, o.rel_edge)
 
 
-def inner(i, o):
+def inner(i, o, c5, stacked, folded):
     planes = {3: window(i.own, 1), 6: window(i.far, 1)}
     planes |= {5 - k: joined((i.near4 if k else i.near5), i.near_edge, k) for k in (0, 1)}
-    sweep_first(planes, 5, o.c5, o.f5)
+    sweep_first(planes, 5, c5, o.f5)
     sweep_first(planes, 4, o.c4, o.f4)
     first = {4: o.f4, 5: o.f5, 6: i.f6, 7: i.f7}
     sweep_second(first, 6, i.c6, o.rel.at[0], o.rel_edge.at[0])
-    sweep_second(first, 5, o.c5, o.rel.at[1], o.rel_edge.at[1])
+    sweep_second(first, 5, c5, o.rel.at[1], o.rel_edge.at[1])
+    grams([(i.rel7, i.rel7_edge), (o.rel.at[0], o.rel_edge.at[0])], o.gram, stacked, folded)
+    flat(o.send, [o.rel.at[0], o.rel.at[1]], o.gram)
+
+
+def flat(send, planes, gram):
+    fields, half = planes[0].shape[:2]
+    for n, plane in enumerate(planes):
+        for f in range(fields):
+            send[pl.ds((n * fields + f) * half, half), :] = plane[f]
+    send[pl.ds(len(planes) * fields * half, gram.shape[0]), :] = gram[...]
 
 
 def squares(refs, sums, before=None):
@@ -276,21 +291,21 @@
         sums[f : f + 1] = total if before is None else total + before[f : f + 1]
 
 
-def near_rest(i, o, c3, f3):
-    planes = {2 + k: window(i.near, k) for k in (0, 1)} | {4: joined(i.near4, i.near_edge, 1)}
+def near_rest(i, o, c3, f3, stacked, folded):
+    planes = {2: window(i.own, 0), 3: window(i.own, 1), 4: joined(i.near4, i.near_edge, 1)}
     sweep_first(planes, 3, c3, f3)
-    first = {1: i.f1, 2: i.f2, 4: i.f4, 5: i.f5} | {3: f3}
-    sweep_second(first, 4, i.c4, o.rel4, o.rel4_edge)
+    first = {1: i.f1, 2: i.f2, 3: f3, 4: i.f4, 5: i.f5}
+    sweep_second(first, 4, i.c4, o.rel.at[2], o.rel_edge.at[2])
     sweep_second(first, 2, i.c2, o.rel.at[0], o.rel_edge.at[0])
     sweep_second(first, 3, c3, o.rel.at[1], o.rel_edge.at[1])
-    squares([o.rel4, o.rel.at[0], o.rel.at[1], i.rel7, i.rel.at[0], i.rel.at[1]], o.sums)
+    own = [(o.rel.at[k], o.rel_edge.at[k]) for k in range(3)]
+    grams(own + [(i.rel.at[1], i.rel_edge.at[1])], o.gram, stacked, folded)
+    flat(o.send, [o.rel.at[2]], o.gram)
+    squares([o.rel.at[k] for k in range(3)] + [i.rel7, i.rel.at[0], i.rel.at[1]], o.sums)
 
 
 def far_rest(i, o, cm, c0, fm, f0, own_sums):
-    planes = {k: window(i.far, k) for k in (0, 1)}
-    tall = i.far.shape[2]
-    planes[-1] = lambda f: jnp.concatenate([i.prev0[f], i.prev1[f, tall:]], axis=0)
-    planes[-2] = lambda f: i.prev1[f, :tall]
+    planes = {k: window(i.far, k) for k in (0, 1)} | {-1 - k: window(i.prev, k) for k in (0, 1)}
     sweep_first(planes, -1, cm, fm)
     sweep_first(planes, 0, c0, f0)
     first = {-1: fm, 0: f0, 1: i.f1, 2: i.f2}
@@ -324,6 +339,14 @@
 
 def group_count(half):
     return (half // BLOCK + 1 + 7) // 8 * 8
+
+
+def places(at, groups, part):
+    row = at // BLOCK * groups
+    if at < len(PAIRS) // BLOCK * BLOCK:
+        return [(row, at % BLOCK * part, 0, groups)]
+    low = groups // 2
+    return [(row, (at % BLOCK + 2 * n) * part, n * low, low) for n in range(2)]
 
 
 def grams(planes, out, stacked, folded):
@@ -344,25 +367,23 @@
         folded[at, tall:] = jnp.zeros((groups * BLOCK - tall, part), jnp.float32)
     for at in range(len(PAIRS)):
         value = folded[at, pl.ds(1, groups, stride=BLOCK), :]
-        out[pl.ds(at // BLOCK * groups, groups), pl.ds(at % BLOCK * part, part)] = value
-
-
-def products(i, o, stacked, folded):
-    rel4 = (i.rel4, i.rel4_edge)
-    far, near = [(i.rel.at[k], i.rel_edge.at[k]) for k in range(2)]
-    own = [(i.own.at[k], i.own_edge.at[k]) for k in range(2)]
-    mid = [(i.mid.at[k], i.mid_edge.at[k]) for k in range(2)]
-    count = o.far.shape[0]
-    grams([(i.rel7, i.rel7_edge), far], o.far, stacked, folded)
-    grams(own, o.gram, stacked, folded)
-    grams(mid + [rel4, near], o.mid, stacked, folded)
-    o.both[:count] = o.far[...]
-    o.both[count:] = o.mid[...]
-
-
-def solve_rows(rel, spread, base, scale, result, z):
+        for row, lane, piece, size in places(at, groups, part):
+            out[pl.ds(row, size), pl.ds(lane, part)] = value[piece : piece + size]
+
+
+def far_products(i, o, stacked, folded):
+    grams([(i.rel.at[k], i.rel_edge.at[k]) for k in range(2)], o.gram, stacked, folded)
+    count = o.gram.shape[0]
+    o.send[:count] = o.gram[...]
+    o.send[count:] = i.back[pl.ds(i.back.shape[0] - count, count), :]
+
+
+def arrived(i, o):
+    o.mark[...] = jnp.zeros_like(o.mark)
+
+
+def solve_rows(rels, spread, base, scale, result, z):
     fields, half, width = result.shape[1:]
-    rel = rel if isinstance(rel, list) else [rel.at[f] for f in range(fields)]
     within = lax.broadcasted_iota(jnp.int32, (EDGE, width), 0)
     for tile in range(half // EDGE):
         entry = {}
@@ -370,19 +391,20 @@
             three = [jnp.broadcast_to(spread[at, pl.ds(base + 2 * tile + n, 1), :], (EDGE, width)) for n in range(3)]
             entry[key] = jnp.where(within < 2, three[0], jnp.where(within < 6, three[1], three[2]))
         rows = pl.ds(tile * EDGE, EDGE)
-        columns = []
-        for b in range(fields):
-            accum = rel[b][rows, :] * scale[b]
-            for a in range(b):
-                accum = accum - entry[a, b] * columns[a]
-            columns.append(accum * entry[b, b])
-            result[z, b, rows, :] = columns[b]
-
-
-def write_plane(result, z, prolong, start, odd, sems):
+        for n, rel in enumerate(rels):
+            columns = []
+            for b in range(fields):
+                accum = rel(b, tile) * scale[b]
+                for a in range(b):
+                    accum = accum - entry[a, b] * columns[a]
+                columns.append(accum * entry[b, b])
+                result[z + n, b, rows, :] = columns[b]
+
+
+def write_plane(result, slot, z, prolong, start, odd, sems):
     planes, half = prolong.shape[1], result.shape[2]
     target = prolong.at[:, natural(z, odd, planes), rows_at(start, half), :]
-    one = pltpu.make_async_copy(result.at[z], target, sems.at[z])
+    one = pltpu.make_async_copy(result.at[slot], target, sems.at[slot])
     one.start()
     return one
 
@@ -416,82 +438,72 @@
 
 def gram_at(ref, at, groups, start=0):
     part = ref.shape[-1] // BLOCK
-    return ref[pl.ds(start + at // BLOCK * groups, groups), pl.ds(at % BLOCK * part, part)]
-
-
-def finish_own(cells, i, o, result, spread, sems):
+    pieces = [ref[pl.ds(start + row, size), pl.ds(lane, part)] for row, lane, _, size in places(at, groups, part)]
+    return jnp.concatenate(pieces, axis=0)
+
+
+def in_plane(ref):
+    return lambda b, tile: ref[b, pl.ds(tile * EDGE, EDGE), :]
+
+
+def in_flat(ref, n, fields, half):
+    return lambda b, tile: ref[pl.ds((n * fields + b) * half + tile * EDGE, EDGE), :]
+
+
+def finish_all(cells, i, o, result, spread, sems):
     odd = parity()
     fields, planes, rows, width = o.prolong.shape
     half = rows // 2
     groups = group_count(half)
     totals = jnp.sum(jnp.sum(i.totals[...], axis=0), axis=1, keepdims=True)
     scales = lax.rsqrt(totals / cells + 1e-06)
-    o.scales[...] = jnp.broadcast_to(scales, o.scales.shape)
     scale = [scales[f : f + 1] for f in range(fields)]
-    upper, inv = triangle(
-        scale,
-        lambda at: jnp.concatenate(
-            [gram_at(i.gram, at, groups) + gram_at(i.same, at, groups), gram_at(i.mid, at, groups)], axis=0
-        ),
-    )
-    lanes = lane_table(width, True)
-    for at, (a, b) in enumerate(PAIRS):
-        value = upper[a, b]
-        o.mine[at] = jnp.where(odd == 0, value[groups:], value[:groups])
-    spread_all(upper, inv, lanes, spread)
+    count = i.mid.shape[0]
+    in_back, in_tail = i.back.shape[0] - count, i.tail.shape[0] - count
+
+    def values(at):
+        own_far = gram_at(i.gram, at, groups) + gram_at(i.cross, at, groups, count)
+        other_far = gram_at(i.back, at, groups, in_back) + gram_at(i.cross, at, groups)
+        return jnp.concatenate(
+            [own_far, other_far, gram_at(i.mid, at, groups), gram_at(i.tail, at, groups, in_tail)], axis=0
+        )
+
+    upper, inv = triangle(scale, values)
+    spread_all(upper, inv, lane_table(width, True), spread)
     writes = []
-    for z in range(planes):
-        solve_rows((i.far if z < 2 else i.near).at[z % 2], spread, z // 2 * groups, scale, result, z)
-        writes.append(write_plane(result, z, o.prolong, odd * half, odd, sems))
+    for block, rels in enumerate(
+        (
+            [in_plane(i.far.at[k]) for k in range(2)],
+            [in_plane(i.last), in_flat(i.back, 0, fields, half)],
+            [in_plane(i.near.at[k]) for k in range(2)],
+            [in_flat(i.back, 1, fields, half), in_flat(i.tail, 0, fields, half)],
+        )
+    ):
+        z, side = block // 2 * 2, block % 2
+        solve_rows(rels, spread, block * groups, scale, result, 2 * block)
+        start = (side + odd - 2 * side * odd) * half
+        writes += [write_plane(result, 2 * block + k, z + k, o.prolong, start, odd, sems) for k in range(2)]
+    per_half = half // BLOCK
+    line = lax.broadcasted_iota(jnp.int32, (2 * per_half, width // BLOCK), 0)
+    pad = jnp.zeros((2 * per_half - groups, width // BLOCK), jnp.float32)
+    for at, pair in enumerate(PAIRS):
+        value = jnp.where(odd == 0, upper[pair][2 * groups :], upper[pair][: 2 * groups])
+        mine, others = value[:groups], value[groups:]
+        low = jnp.concatenate([jnp.where(odd == 0, mine, others), pad], axis=0)
+        top = jnp.concatenate([jnp.where(odd == 0, others, mine), pad], axis=0)
+        o.factors[at, 0] = jnp.where(line < per_half, onward(low, 0), pltpu.roll(top, per_half - 1, 0))
     for one in writes:
         one.wait()
 
 
-def finish_other(i, o, result, spread, sems):
-    odd = parity()
-    fields, planes, rows, width = o.prolong.shape
-    half = rows // 2
-    groups = group_count(half)
-    scale = [i.scales[f : f + 1, :1] for f in range(fields)]
-    both = i.both
-    mid_start = i.cross.shape[0]
-    upper, inv = triangle(
-        scale,
-        lambda at: jnp.concatenate(
-            [gram_at(both, at, groups) + gram_at(i.cross, at, groups), gram_at(both, at, groups, mid_start)],
-            axis=0,
-        ),
-    )
-    lanes = lane_table(width, True)
-    count = rows // BLOCK
-    line = lax.broadcasted_iota(jnp.int32, (count, width // BLOCK), 0)
-    pad = jnp.zeros((count - groups, width // BLOCK), jnp.float32)
-    for at, (a, b) in enumerate(PAIRS):
-        value = upper[a, b]
-        mine, theirs = i.mine[at], jnp.where(odd == 0, value[groups:], value[:groups])
-        low = jnp.concatenate([jnp.where(odd == 0, mine, theirs), pad], axis=0)
-        top = jnp.concatenate([jnp.where(odd == 0, theirs, mine), pad], axis=0)
-        low, top = onward(low, 0), pltpu.roll(top, half // BLOCK - 1, 0)
-        o.factors[at, 0] = jnp.where(line < half // BLOCK, low, top)
-    spread_all(upper, inv, lanes, spread)
-    writes = []
-    for z in range(planes):
-        rel = i.last if z == 0 else i.back.at[z - 1] if z < planes - 1 else i.back4
-        solve_rows(rel, spread, z // 2 * groups, scale, result, z)
-        writes.append(write_plane(result, z, o.prolong, (1 - odd) * half, odd, sems))
-    for one in writes:
-        one.wait()
-
-
-def moved(name, x, even_by, odd_by):
+def moved(x, even_by, odd_by):
     nz, ny = lax.axis_size("gz"), lax.axis_size("gy")
     route = []
     for z in range(nz):
         dz, dy = odd_by if z % 2 else even_by
         for y in range(ny):
             route.append((z * ny + y, (z + dz) % nz * ny + (y + dy) % ny))
-    with jax.named_scope(name):
-        return lax.ppermute(x, ("gz", "gy"), route)
+    return lax.ppermute(x, ("gz", "gy"), route)
 
 
 def body(tv, coef):
@@ -504,7 +516,7 @@
     windows, edge = (2, fields + 1, tall, width), (2, fields + 1, EDGE, width)
     keep, keeps = (fields + 1, half, width), (2, fields + 1, half, width)
     first, coefs = (fields, tall, width), (5, tall, width)
-    gram = (-(-len(PAIRS) // BLOCK) * groups, width)
+    gram = (len(PAIRS) // BLOCK * groups + groups // 2, width)
     sums = (8, width // 2)
     rel, rel_edge = (fields, half, width), (fields, EDGE, width)
 
@@ -516,17 +528,25 @@
     sent = call(
         pack_first,
         args,
-        dict(far0=(fields + 1, half + 2 * EDGE, width), own=keeps, halo=edge, cross=edge),
-        [tiles] * 3 + [local(edge), pltpu.SemaphoreType.DMA((12,)), pltpu.SemaphoreType.DMA((2,))],
+        dict(far0=(fields + 1, half + 2 * EDGE, width), halo=edge, cross=edge, mark=sums),
+        [tiles] * 3 + [local(edge), pltpu.SemaphoreType.DMA((8,)), pltpu.SemaphoreType.DMA((2,))],
         far=("tv", "coef"),
-    )
-    far0 = moved("far0", sent.far0, (1, 0), (-1, 0))
-    halo = moved("halo", sent.halo, (0, 1), (0, -1))
-    cross = moved("cross", sent.cross, (0, -1), (0, 1))
-    after = moved("after", sent.own, (-2, 0), (2, 0))
+        limit=FIRST_LIMIT,
+    )
+    far_own = call(
+        pack_own,
+        dict(gate=sent.mark, **args),
+        dict(own=keeps),
+        [pltpu.SemaphoreType.DMA((4,))],
+        far=("tv", "coef"),
+    ).own
+    far0 = moved(sent.far0, (1, 0), (-1, 0))
+    halo = moved(sent.halo, (0, 1), (0, -1))
+    cross = moved(sent.cross, (0, -1), (0, 1))
+    after = moved(far_own, (-2, 0), (2, 0))
     own = call(
         pack_second,
-        dict(halo=halo, cross=cross, own=sent.own, **args),
+        dict(halo=halo, cross=cross, own=far_own, **args),
         dict(
             far=windows,
             near=windows,
@@ -538,39 +558,39 @@
     )
     to_near = call(
         pack_near,
-        dict(far0=far0, **args),
-        dict(send0=keep, send1=keep, on=keep),
+        dict(gate=far0, **args),
+        dict(send0=keep, send1=keep),
         [pltpu.SemaphoreType.DMA((4,))],
         far=("tv", "coef"),
     )
-    prev0 = moved("prev0", to_near.on, (2, 0), (-2, 0))
-    far1 = moved("far1", own.far1, (1, 0), (-1, 0))
-    near5 = moved("near5", to_near.send0, (1, 0), (-1, 0))
-    near4 = moved("near4", to_near.send1, (1, 0), (-1, 0))
-    after_edge = moved("after_edge", own.far_edge, (-2, 0), (2, 0))
+    far1 = moved(own.far1, (1, 0), (-1, 0))
+    near5 = moved(to_near.send0, (1, 0), (-1, 0))
+    near4 = moved(to_near.send1, (1, 0), (-1, 0))
+    after_edge = moved(own.far_edge, (-2, 0), (2, 0))
     a = call(
         early,
-        dict(far=own.far, near=own.near, gate=after_edge),
+        dict(far=own.far, near=own.near),
         dict(c1=coefs, c2=coefs, f1=first, f2=first),
     )
     par = call(
         pack_third,
-        dict(far0=far0, far1=far1, gate=a.c1),
-        dict(far=windows, near_edge=edge, send=(fields + 1, tall + EDGE, width)),
-    )
-    prev1 = moved("prev1", par.send, (2, 0), (-2, 0))
+        dict(far0=far0, far1=far1),
+        dict(far=windows, near_edge=edge),
+    )
+    before = moved(par.far, (2, 0), (-2, 0))
     b = call(
         outer,
-        dict(far=par.far, next=after, next_edge=after_edge),
+        dict(far=par.far, next=after, next_edge=after_edge, gate=a.c1),
         dict(c7=coefs, f7=first, f8=first),
         [local(coefs)],
     )
     c = call(
         inner_last,
-        dict(far=par.far, near5=near5, near_edge=par.near_edge, gate=prev0, c7=b.c7, f7=b.f7, f8=b.f8),
+        dict(far=par.far, near5=near5, near_edge=par.near_edge, c7=b.c7, f7=b.f7, f8=b.f8),
         dict(c6=coefs, f6=first, rel=rel, rel_edge=rel_edge),
     )
-    last = moved("last", c.rel, (1, 0), (-1, 0))
+    last = moved(c.rel, (1, 0), (-1, 0))
+    sum_scratch = [local((len(PAIRS) * tall, width)), local((len(PAIRS), groups * BLOCK, width // BLOCK))]
     d = call(
         inner,
         dict(
@@ -582,29 +602,51 @@
             f6=c.f6,
             f7=b.f7,
             c6=c.c6,
+            rel7=c.rel,
+            rel7_edge=c.rel_edge,
         ),
-        dict(c4=coefs, c5=coefs, f4=first, f5=first, rel=(2,) + rel, rel_edge=(2,) + rel_edge),
-    )
-    back = moved("back", d.rel, (1, 0), (-1, 0))
+        dict(
+            c4=coefs,
+            f4=first,
+            f5=first,
+            rel=(2,) + rel,
+            rel_edge=(2,) + rel_edge,
+            gram=gram,
+            send=(2 * fields * half + gram[0], width),
+        ),
+        [local(coefs)] + sum_scratch,
+    )
+    back = moved(d.send, (1, 0), (-1, 0))
     n = call(
         near_rest,
         dict(
-            near=own.near,
+            own=own.near,
             near4=near4,
             near_edge=par.near_edge,
-            f1=a.f1, f2=a.f2, c2=a.c2,
-            f4=d.f4, f5=d.f5, c4=d.c4, rel=d.rel,
+            f1=a.f1,
+            f2=a.f2,
+            f4=d.f4,
+            f5=d.f5,
+            c2=a.c2,
+            c4=d.c4,
+            rel=d.rel,
+            rel_edge=d.rel_edge,
             rel7=c.rel,
         ),
-        dict(rel=(2,) + rel, rel_edge=(2,) + rel_edge, rel4=rel, rel4_edge=rel_edge, sums=sums),
-        [local(coefs), local(first)],
-    )
-    back4 = moved("back4", n.rel4, (1, 0), (-1, 0))
+        dict(
+            rel=(3,) + rel,
+            rel_edge=(3,) + rel_edge,
+            gram=gram,
+            send=(fields * half + gram[0], width),
+            sums=sums,
+        ),
+        [local(coefs), local(first)] + sum_scratch,
+    )
+    tail = moved(n.send, (1, 0), (-1, 0))
     r = call(
         far_rest,
         dict(
-            prev0=prev0,
-            prev1=prev1,
+            prev=before,
             far=own.far,
             f1=a.f1, f2=a.f2, c1=a.c1,
             sums=n.sums,
@@ -615,54 +657,36 @@
     )
     totals = lax.all_to_all(r.sums, ("gz", "gy"), 0, 0)
     e = call(
-        products,
+        far_products,
+        dict(rel=r.rel, rel_edge=r.rel_edge, back=back),
+        dict(gram=gram, send=(2 * gram[0], width)),
+        sum_scratch,
+    )
+    crossed = moved(e.send, (-1, 0), (1, 0))
+    marked = call(arrived, dict(gate=tail, gram=e.gram), dict(mark=sums))
+    finish = functools.partial(finish_all, float(cells))
+    finish.__name__ = "finish_all"
+    whole = call(
+        finish,
         dict(
-            own=r.rel,
-            own_edge=r.rel_edge,
-            mid=n.rel,
-            mid_edge=n.rel_edge,
-            rel4=n.rel4,
-            rel4_edge=n.rel4_edge,
-            rel=d.rel, rel_edge=d.rel_edge,
-            rel7=c.rel,
-            rel7_edge=c.rel_edge,
-        ),
-        dict(gram=gram, far=gram, mid=gram, both=(2 * gram[0], width)),
-        [local((len(PAIRS) * tall, width)), local((len(PAIRS), groups * BLOCK, width // BLOCK))],
-    )
-    both = moved("both", e.both, (1, 0), (-1, 0))
-    same = moved("same", e.far, (2, 0), (-2, 0))
-    crossed = moved("crossed", e.gram, (-1, 0), (1, 0))
-    finish = functools.partial(finish_own, float(cells))
-    finish.__name__ = "finish_own"
-    result = [
-        local((planes, fields, half, width)),
-        local((len(PAIRS), 2 * groups, width)),
-        pltpu.SemaphoreType.DMA((planes,)),
-    ]
-    mine = call(
-        finish,
-        dict(totals=totals, gram=e.gram, same=same, mid=e.mid, far=r.rel, near=n.rel),
-        dict(prolong=tv.shape, mine=(len(PAIRS), groups, width // BLOCK), scales=sums),
-        result,
-        far=("prolong",),
-    )
-    whole = call(
-        finish_other,
-        dict(
+            totals=totals,
+            gram=e.gram,
+            cross=crossed,
+            mid=n.gram,
+            back=back,
+            tail=tail,
             last=last,
-            back=back,
-            back4=back4,
-            both=both,
-            cross=crossed,
-            scales=mine.scales,
-            mine=mine.mine,
-            own_part=mine.prolong,
+            far=r.rel,
+            near=n.rel,
+            mark=marked.mark,
         ),
         dict(prolong=tv.shape, factors=(len(PAIRS), planes // BLOCK, rows // BLOCK, width // BLOCK)),
-        result,
-        far=("prolong", "own_part"),
-        alias=dict(own_part="prolong"),
+        [
+            local((2 * planes, fields, half, width)),
+            local((len(PAIRS), 4 * groups, width)),
+            pltpu.SemaphoreType.DMA((2 * planes,)),
+        ],
+        far=("prolong",),
     )
     return whole.prolong, whole.factors
 

time: 62 us -> 59.7 us (0.963)
  starting transfers between devices: 28.8 us -> 22.6 us
  waiting for transfers between devices: 15.4 us -> 19.9 us
  local copies, waits for them, and re-layouts: 2.4 us -> 0.69 us
  Pallas kernels: 14.5 us -> 15.5 us
    ppermute x16 -> x13, starting transfers between devices: 24.6 us -> 18.2 us  [moved(): return lax.ppermute(x, ('gz', 'gy'), route)]
    ppermute x16 -> x13, waiting for transfers between devices: 15.4 us -> 19.9 us  [moved(): return lax.ppermute(x, ('gz', 'gy'), route)]
    unnamed x4 -> x6, local copies, waits for them, and re-layouts: 2.4 us -> 0.69 us
    pallas_call x13 -> x14, Pallas kernels: 14.5 us -> 15.5 us  [call(): pl.pallas_call(kernel, out_shape=[jax.ShapeDtypeStruct(outs[k], jnp.float...]
  transfers between devices with their start and end apart: 17 -> 14, of which waited for: 7 -> 6; matrix products, arithmetic and copies ran while one was open for 0% -> 0% of each run, Pallas kernels for 18% -> 17%
where the time goes in v3:
time: 59.7 us; the launch traced here: 59.5 us
  starting transfers between devices  22.6 us (38%)
  waiting for transfers between devices  19.9 us (33%)
  Pallas kernels  15.5 us (26%)
  between operations  0.75 us (1%)
  local copies, waits for them, and re-layouts  0.69 us (1%)
    ppermute x13, waiting for transfers between devices, moved(): return lax.ppermute(x, ('gz', 'gy'), route)  19.9 us
    ppermute x13, starting transfers between devices, moved(): return lax.ppermute(x, ('gz', 'gy'), route)  18.2 us
    pallas_call x14, Pallas kernels, call(): pl.pallas_call(kernel, out_shape=[jax.ShapeDtypeStruct(outs[k], jnp.float...  15.5 us
    all_to_all x1, starting transfers between devices, body(): totals = lax.all_to_all(r.sums, ('gz', 'gy'), 0, 0)  4.37 us
  transfers between devices with their start and end apart: 14, of which 6 were waited for; matrix products, arithmetic and copies ran while one was open for 0% of the time, Pallas kernels for 17%

profile of v3, /device:TPU:0, one launch (start us, length us, event | category | flops | bytes accessed | tf_op | source)
XLA Modules:
  0.0 59.5 jit_solution(15091172898997435779)
XLA Ops:
  0.6 0.0 copy-start
  0.6 0.0 copy-start.1
  0.6 2.2 %pack_first.1 = (f32[5,64,256]{2,1,0:T(8,128)}, f32[2,5,8,256]{3,2,1,0:T(8,128)}, f32[2,5,8,256]{3,2,1,0:T(8,128)}, f32[8,128]{1,0:T(8,128)}) custom-call(f32[4,4,96,256]{3,2,1,0:T(8,128)} %refs_1_.5, f32[4,96,256]{2,1,0:T(8,128)} %refs_2_.3), custom_call_target="tpu_custom_call" | custom-call | tf_op jit(solution)/shard_map/pack_first/pallas_call | solution.py:33
  2.8 3.0 %collective-permute-start = (f32[5,64,256]{2,1,0:T(8,128)}, f32[5,64,256]{2,1,0:T(8,128)S(1)}, u32[]{:S(2)}, u32[]{:S(2)}) collective-permute-start(f32[5,64,256]{2,1,0:T(8,128)} %get-tuple-element.40), channel_id=1, source_target_pairs={{0,4},{1,5},{2,6},{3,7},{4,0},{5,1},{6,2},{7,3},{8,12},{9,13},{10,... | collective-permute-start | bytes 983048 | tf_op jit(solution)/shard_map/ppermute | solution.py:506
  5.9 0.0 collective-permute-start.1
  5.9 1.7 %collective-permute-start.2 = (f32[2,5,8,256]{3,2,1,0:T(8,128)}, f32[2,5,8,256]{3,2,1,0:T(8,128)S(1)}, u32[]{:S(2)}, u32[]{:S(2)}) collective-permute-start(f32[2,5,8,256]{3,2,1,0:T(8,128)} %get-tuple-element.42), channel_id=1, source_target_pairs={{0,3},{1,0},{2,1},{3,2},{4,5},{5,6},{6,7},{7,4},{8,11},{9,8},{10,9... | collective-permute-start | bytes 245768 | tf_op jit(solution)/shard_map/ppermute | solution.py:506
  7.6 0.0 copy-done
  7.6 0.0 copy-done.1
  7.6 0.0 copy-start.2
  7.6 0.7 %copy-done.2 = f32[8,128]{1,0:T(8,128)S(1)} copy-done((f32[8,128]{1,0:T(8,128)S(1)}, f32[8,128]{1,0:T(8,128)}, u32[]{:S(2)}) %copy-start.2) | copy-done | bytes 4120
  8.3 0.3 pack_own.1.refs_2_
  8.6 3.7 %collective-permute-start.7 = (f32[2,5,48,256]{3,2,1,0:T(8,128)S(1)}, f32[2,5,48,256]{3,2,1,0:T(8,128)S(1)}, u32[]{:S(2)}, u32[]{:S(2)}) collective-permute-start(f32[2,5,48,256]{3,2,1,0:T(8,128)S(1)} %pack_own.1.refs_2_), channel_id=1, source_target_pairs={{0,24},{1,25},{2,26},{3,27},{4,12},{5,13},{6,14},{7,15},{8,0},{9,1... | collective-permute-start | bytes 1474568 | tf_op jit(solution)/shard_map/ppermute | solution.py:506
  12.3 0.0 collective-permute-done.1.refs_0_
  12.3 0.0 collective-permute-done.2.refs_1_
  12.3 0.6 pack_second.1
  12.8 0.1 collective-permute-start.3
  12.9 2.7 %collective-permute-start.8 = (f32[2,5,8,256]{3,2,1,0:T(8,128)S(1)}, f32[2,5,8,256]{3,2,1,0:T(8,128)S(1)}, u32[]{:S(2)}, u32[]{:S(2)}) collective-permute-start(f32[2,5,8,256]{3,2,1,0:T(8,128)S(1)} %get-tuple-element.54), channel_id=1, source_target_pairs={{0,24},{1,25},{2,26},{3,27},{4,12},{5,13},{6,14},{7,15},{8,0},{9,1... | collective-permute-start | bytes 245768 | tf_op jit(solution)/shard_map/ppermute | solution.py:506
  15.6 0.0 collective-permute-done.refs_0_
  15.6 0.3 pack_near.1
  15.9 0.1 collective-permute-start.6
  16.0 2.0 %collective-permute-start.5 = (f32[5,48,256]{2,1,0:T(8,128)S(1)}, f32[5,48,256]{2,1,0:T(8,128)S(1)}, u32[]{:S(2)}, u32[]{:S(2)}) collective-permute-start(f32[5,48,256]{2,1,0:T(8,128)S(1)} %get-tuple-element.51), channel_id=1, source_target_pairs={{0,4},{1,5},{2,6},{3,7},{4,0},{5,1},{6,2},{7,3},{8,12},{9,13},{10,... | collective-permute-start | bytes 737288 | tf_op jit(solution)/shard_map/ppermute | solution.py:506
  18.0 0.8 %early.1 = (f32[5,56,256]{2,1,0:T(8,128)S(1)}, f32[5,56,256]{2,1,0:T(8,128)S(1)}, f32[4,56,256]{2,1,0:T(8,128)S(1)}, f32[4,56,256]{2,1,0:T(8,128)S(1)}) custom-call(f32[2,5,56,256]{3,2,1,0:T(8,128)S(1)} %get-tuple-element.46.refs_0_.refs_1_, f32[2,5,56,256]{3,2,1,0:T(8,128)S(1)} %get-tuple-element.47.refs_1_.refs_0_), custom_call_target="tpu_custom_call" | custom-call | flops 3000000000 | tf_op jit(solution)/shard_map/early/pallas_call | solution.py:33
  18.8 4.7 %collective-permute-done.3.refs_1_ = f32[5,64,256]{2,1,0:T(8,128)S(1)} collective-permute-done((f32[5,64,256]{2,1,0:T(8,128)S(1)}, f32[5,64,256]{2,1,0:T(8,128)S(1)}, u32[]{:S(2)}, u32[]{:S(2)}) %collective-permute-start.3) | collective-permute-done | bytes 327712 | tf_op jit(solution)/shard_map/ppermute | solution.py:506
  23.6 0.1 collective-permute-start.4
  23.7 1.4 %collective-permute-done.8.refs_2_ = f32[2,5,8,256]{3,2,1,0:T(8,128)S(1)} collective-permute-done((f32[2,5,8,256]{3,2,1,0:T(8,128)S(1)}, f32[2,5,8,256]{3,2,1,0:T(8,128)S(1)}, u32[]{:S(2)}, u32[]{:S(2)}) %collective-permute-start.8) | collective-permute-done | bytes 81952 | tf_op jit(solution)/shard_map/ppermute | solution.py:506
  25.0 0.0 collective-permute-done.7.refs_1_
  25.0 0.8 %outer.1 = (f32[5,56,256]{2,1,0:T(8,128)S(1)}, f32[4,56,256]{2,1,0:T(8,128)S(1)}, f32[4,56,256]{2,1,0:T(8,128)S(1)}) custom-call(f32[2,5,56,256]{3,2,1,0:T(8,128)S(1)} %get-tuple-element.45.refs_0_.refs_1_, f32[2,5,48,256]{3,2,1,0:T(8,128)S(1)} %collective-permute-done.7.refs_1_, f32[2,5,8,256]{3,2,1,0:T(8,128)S(1)} %collective-permute-done.8.refs_2_, ...), custom_call_target="tpu_custom_call" | custom-call | tf_op jit(solution)/shard_map/outer/pallas_call | solution.py:33
  25.8 3.0 %collective-permute-done.6.refs_1_.refs_2_ = f32[5,48,256]{2,1,0:T(8,128)S(1)} collective-permute-done((f32[5,48,256]{2,1,0:T(8,128)S(1)}, f32[5,48,256]{2,1,0:T(8,128)S(1)}, u32[]{:S(2)}, u32[]{:S(2)}) %collective-permute-start.6) | collective-permute-done | bytes 245792 | tf_op jit(solution)/shard_map/ppermute | solution.py:506
  28.8 0.7 %inner_last.1 = (f32[5,56,256]{2,1,0:T(8,128)S(1)}, f32[4,56,256]{2,1,0:T(8,128)S(1)}, f32[4,48,256]{2,1,0:T(8,128)S(1)}, f32[4,8,256]{2,1,0:T(8,128)S(1)}) custom-call(f32[2,5,56,256]{3,2,1,0:T(8,128)S(1)} %get-tuple-element.45.refs_0_.refs_1_, f32[5,48,256]{2,1,0:T(8,128)S(1)} %collective-permute-done.6.refs_1_.refs_2_, ...), custom_call_target="tpu_custom_call" | custom-call | tf_op jit(solution)/shard_map/inner_last/pallas_call | solution.py:33
  29.5 0.1 collective-permute-start.9
  29.6 4.5 %collective-permute-done.5.refs_3_.refs_1_ = f32[5,48,256]{2,1,0:T(8,128)S(1)} collective-permute-done((f32[5,48,256]{2,1,0:T(8,128)S(1)}, f32[5,48,256]{2,1,0:T(8,128)S(1)}, u32[]{:S(2)}, u32[]{:S(2)}) %collective-permute-start.5) | collective-permute-done | bytes 245792 | tf_op jit(solution)/shard_map/ppermute | solution.py:506
  34.1 2.2 %inner.1 = (f32[5,56,256]{2,1,0:T(8,128)S(1)}, f32[4,56,256]{2,1,0:T(8,128)S(1)}, f32[4,56,256]{2,1,0:T(8,128)S(1)}, f32[2,4,48,256]{3,2,1,0:T(8,128)S(1)}, f32[...) custom-call(f32[2,5,56,256]{3,2,1,0:T(8,128)S(1)} %get-tuple-element.47.refs_1_.refs_0_, ...), custom_call_target="tpu_custom_call" | custom-call | flops 10000000000 | tf_op jit(solution)/shard_map/inner/pallas_call | solution.py:33
  36.3 0.0 collective-permute-start.10
  36.3 1.9 %near_rest.1 = (f32[3,4,48,256]{3,2,1,0:T(8,128)S(1)}, f32[3,4,8,256]{3,2,1,0:T(8,128)}, f32[40,256]{1,0:T(8,128)S(1)}, f32[232,256]{1,0:T(8,128)S(1)}, f32[8,128]{1,0:T(8,128)S(1)}) custom-call(f32[2,5,56,256]{3,2,1,0:T(8,128)S(1)} %get-tuple-element.47.refs_1_.refs_0_, f32[5,48,256]{2,1,0:T(8,128)S(1)} %collective-permute-done.5.refs_3_.refs_1_, ...), custom_call_target="tpu_custom_call" | custom-call | flops 3000000000 | tf_op jit(solution)/shard_map/near_rest/pallas_call | solution.py:33
  38.2 2.0 %collective-permute-start.12 = (f32[232,256]{1,0:T(8,128)S(1)}, f32[232,256]{1,0:T(8,128)S(1)}, u32[]{:S(2)}, u32[]{:S(2)}) collective-permute-start(f32[232,256]{1,0:T(8,128)S(1)} %get-tuple-element.76), channel_id=1, source_target_pairs={{0,4},{1,5},{2,6},{3,7},{4,0},{5,1},{6,2},{7,3},{8,12},{9,13},{10,... | collective-permute-start | bytes 712712 | tf_op jit(solution)/shard_map/ppermute | solution.py:506
  40.3 0.0 collective-permute-done.9.refs_6_
  40.3 0.0 collective-permute-done.4.refs_0_
  40.3 2.3 %far_rest.1 = (f32[2,4,48,256]{3,2,1,0:T(8,128)S(1)}, f32[2,4,8,256]{3,2,1,0:T(8,128)S(1)}, f32[32,8,128]{2,1,0:T(8,128)}) custom-call(f32[2,5,56,256]{3,2,1,0:T(8,128)S(1)} %collective-permute-done.4.refs_0_, f32[2,5,56,256]{3,2,1,0:T(8,128)S(1)} %get-tuple-element.46.refs_0_.refs_1_, f32[4,56,256]{2,1,0:T(8,128)S(1)} %get-tuple-element.48.refs_3_.refs_2_, ...), custom_call_target="tpu_custom_call" | custom-call | tf_op jit(solution)/shard_map/far_rest/pallas_call | solution.py:33
  42.6 4.4 %all-to-all-start = ((f32[32,8,128]{2,1,0:T(8,128)}), f32[32,8,128]{2,1,0:T(8,128)S(1)}, u32[]{:S(2)}, u32[]{:S(2)}) async-start(f32[32,8,128]{2,1,0:T(8,128)} %get-tuple-element.69), calls=%async_computation | async-start | bytes 262144 | tf_op jit(solution)/shard_map/all_to_all | solution.py:658
  46.9 1.8 %collective-permute-done.10.refs_2_.refs_4_ = f32[424,256]{1,0:T(8,128)S(1)} collective-permute-done((f32[424,256]{1,0:T(8,128)S(1)}, f32[424,256]{1,0:T(8,128)S(1)}, u32[]{:S(2)}, u32[]{:S(2)}) %collective-permute-start.10) | collective-permute-done | bytes 434208 | tf_op jit(solution)/shard_map/ppermute | solution.py:506
  48.7 0.4 far_products.1
  49.1 2.8 %collective-permute-start.11 = (f32[80,256]{1,0:T(8,128)S(1)}, f32[80,256]{1,0:T(8,128)S(1)}, u32[]{:S(2)}, u32[]{:S(2)}) collective-permute-start(f32[80,256]{1,0:T(8,128)S(1)} %get-tuple-element.74), channel_id=1, source_target_pairs={{0,28},{1,29},{2,30},{3,31},{4,8},{5,9},{6,10},{7,11},{8,4},{9,5},... | collective-permute-start | bytes 245768 | tf_op jit(solution)/shard_map/ppermute | solution.py:506
  51.9 0.0 collective-permute-done.12.refs_0_.refs_5_
  51.9 4.6 %collective-permute-done.11.refs_2_ = f32[80,256]{1,0:T(8,128)S(1)} collective-permute-done((f32[80,256]{1,0:T(8,128)S(1)}, f32[80,256]{1,0:T(8,128)S(1)}, u32[]{:S(2)}, u32[]{:S(2)}) %collective-permute-start.11) | collective-permute-done | bytes 81952 | tf_op jit(solution)/shard_map/ppermute | solution.py:506
  56.5 0.0 all-to-all-done.refs_0_
  56.5 3.0 %finish_all.1 = (f32[4,4,96,256]{3,2,1,0:T(8,128)}, f32[10,1,24,64]{3,2,1,0:T(8,128)}) custom-call(f32[32,8,128]{2,1,0:T(8,128)S(1)} %all-to-all-done.refs_0_, f32[40,256]{1,0:T(8,128)S(1)} %get-tuple-element.73.refs_1_, f32[80,256]{1,0:T(8,128)S(1)} %collective-permute-done.11.refs_2_, f32[40,256]{1,0:T(8,128)S(1)} %get-tuple-element.75.refs_3_, ...), custom_call_target="tpu_custom_call" | custom-call | tf_op jit(solution)/shard_map/finish_all/pallas_call | solution.py:33
  (2 shorter events, 0.0 us)
Async XLA Ops:
  0.6 7.0 %copy-start = (f32[4,4,96,256]{3,2,1,0:T(8,128)S(1)}, f32[4,4,96,256]{3,2,1,0:T(8,128)}, u32[]{:S(2)}) copy-start(f32[4,4,96,256]{3,2,1,0:T(8,128)} %refs_1_.5) | copy-start | bytes 4718596
  0.6 7.0 %copy-start.1 = (f32[4,96,256]{2,1,0:T(8,128)S(1)}, f32[4,96,256]{2,1,0:T(8,128)}, u32[]{:S(2)}) copy-start(f32[4,96,256]{2,1,0:T(8,128)} %refs_2_.3) | copy-start | bytes 1179652
  2.8 12.8 %collective-permute-start = (f32[5,64,256]{2,1,0:T(8,128)}, f32[5,64,256]{2,1,0:T(8,128)S(1)}, u32[]{:S(2)}, u32[]{:S(2)}) collective-permute-start(f32[5,64,256]{2,1,0:T(8,128)} %get-tuple-element.40), channel_id=1, source_target_pairs={{0,4},{1,5},{2,6},{3,7},{4,0},{5,1},{6,2},{7,3},{8,12},{9,13},{10,... | collective-permute-start | bytes 983048 | tf_op jit(solution)/shard_map/ppermute | solution.py:506
  5.9 6.4 %collective-permute-start.1 = (f32[2,5,8,256]{3,2,1,0:T(8,128)}, f32[2,5,8,256]{3,2,1,0:T(8,128)S(1)}, u32[]{:S(2)}, u32[]{:S(2)}) collective-permute-start(f32[2,5,8,256]{3,2,1,0:T(8,128)} %get-tuple-element.41), channel_id=1, source_target_pairs={{0,1},{1,2},{2,3},{3,0},{4,7},{5,4},{6,5},{7,6},{8,9},{9,10},{10,1... | collective-permute-start | bytes 245768 | tf_op jit(solution)/shard_map/ppermute | solution.py:506
  5.9 6.4 %collective-permute-start.2 = (f32[2,5,8,256]{3,2,1,0:T(8,128)}, f32[2,5,8,256]{3,2,1,0:T(8,128)S(1)}, u32[]{:S(2)}, u32[]{:S(2)}) collective-permute-start(f32[2,5,8,256]{3,2,1,0:T(8,128)} %get-tuple-element.42), channel_id=1, source_target_pairs={{0,3},{1,0},{2,1},{3,2},{4,5},{5,6},{6,7},{7,4},{8,11},{9,8},{10,9... | collective-permute-start | bytes 245768 | tf_op jit(solution)/shard_map/ppermute | solution.py:506
  7.6 0.7 %copy-start.2 = (f32[8,128]{1,0:T(8,128)S(1)}, f32[8,128]{1,0:T(8,128)}, u32[]{:S(2)}) copy-start(f32[8,128]{1,0:T(8,128)} %get-tuple-element.43.refs_0_) | copy-start | bytes 12292
  8.6 16.4 %collective-permute-start.7 = (f32[2,5,48,256]{3,2,1,0:T(8,128)S(1)}, f32[2,5,48,256]{3,2,1,0:T(8,128)S(1)}, u32[]{:S(2)}, u32[]{:S(2)}) collective-permute-start(f32[2,5,48,256]{3,2,1,0:T(8,128)S(1)} %pack_own.1.refs_2_), channel_id=1, source_target_pairs={{0,24},{1,25},{2,26},{3,27},{4,12},{5,13},{6,14},{7,15},{8,0},{9,1... | collective-permute-start | bytes 1474568 | tf_op jit(solution)/shard_map/ppermute | solution.py:506
  12.8 10.7 %collective-permute-start.3 = (f32[5,64,256]{2,1,0:T(8,128)S(1)}, f32[5,64,256]{2,1,0:T(8,128)S(1)}, u32[]{:S(2)}, u32[]{:S(2)}) collective-permute-start(f32[5,64,256]{2,1,0:T(8,128)S(1)} %get-tuple-element.44), channel_id=1, source_target_pairs={{0,4},{1,5},{2,6},{3,7},{4,0},{5,1},{6,2},{7,3},{8,12},{9,13},{10,... | collective-permute-start | bytes 983048 | tf_op jit(solution)/shard_map/ppermute | solution.py:506
  12.9 12.1 %collective-permute-start.8 = (f32[2,5,8,256]{3,2,1,0:T(8,128)S(1)}, f32[2,5,8,256]{3,2,1,0:T(8,128)S(1)}, u32[]{:S(2)}, u32[]{:S(2)}) collective-permute-start(f32[2,5,8,256]{3,2,1,0:T(8,128)S(1)} %get-tuple-element.54), channel_id=1, source_target_pairs={{0,24},{1,25},{2,26},{3,27},{4,12},{5,13},{6,14},{7,15},{8,0},{9,1... | collective-permute-start | bytes 245768 | tf_op jit(solution)/shard_map/ppermute | solution.py:506
  15.9 12.9 %collective-permute-start.6 = (f32[5,48,256]{2,1,0:T(8,128)S(1)}, f32[5,48,256]{2,1,0:T(8,128)S(1)}, u32[]{:S(2)}, u32[]{:S(2)}) collective-permute-start(f32[5,48,256]{2,1,0:T(8,128)S(1)} %get-tuple-element.53), channel_id=1, source_target_pairs={{0,4},{1,5},{2,6},{3,7},{4,0},{5,1},{6,2},{7,3},{8,12},{9,13},{10,... | collective-permute-start | bytes 737288 | tf_op jit(solution)/shard_map/ppermute | solution.py:506
  16.0 18.1 %collective-permute-start.5 = (f32[5,48,256]{2,1,0:T(8,128)S(1)}, f32[5,48,256]{2,1,0:T(8,128)S(1)}, u32[]{:S(2)}, u32[]{:S(2)}) collective-permute-start(f32[5,48,256]{2,1,0:T(8,128)S(1)} %get-tuple-element.51), channel_id=1, source_target_pairs={{0,4},{1,5},{2,6},{3,7},{4,0},{5,1},{6,2},{7,3},{8,12},{9,13},{10,... | collective-permute-start | bytes 737288 | tf_op jit(solution)/shard_map/ppermute | solution.py:506
  23.6 16.7 %collective-permute-start.4 = (f32[2,5,56,256]{3,2,1,0:T(8,128)S(1)}, f32[2,5,56,256]{3,2,1,0:T(8,128)S(1)}, u32[]{:S(2)}, u32[]{:S(2)}) collective-permute-start(f32[2,5,56,256]{3,2,1,0:T(8,128)S(1)} %get-tuple-element.45.refs_0_.refs_1_), channel_id=1, source_target_pairs={{0,8},{1,9},{2,10},{3,11},{4,28},{5,29},{6,30},{7,31},{8,16},{9,17... | collective-permute-start | bytes 1720328 | tf_op jit(solution)/shard_map/ppermute | solution.py:506
  29.5 10.8 %collective-permute-start.9 = (f32[4,48,256]{2,1,0:T(8,128)S(1)}, f32[4,48,256]{2,1,0:T(8,128)S(1)}, u32[]{:S(2)}, u32[]{:S(2)}) collective-permute-start(f32[4,48,256]{2,1,0:T(8,128)S(1)} %get-tuple-element.60.refs_8_.refs_11_), channel_id=1, source_target_pairs={{0,4},{1,5},{2,6},{3,7},{4,0},{5,1},{6,2},{7,3},{8,12},{9,13},{10,... | collective-permute-start | bytes 589832 | tf_op jit(solution)/shard_map/ppermute | solution.py:506
  36.3 12.4 %collective-permute-start.10 = (f32[424,256]{1,0:T(8,128)S(1)}, f32[424,256]{1,0:T(8,128)S(1)}, u32[]{:S(2)}, u32[]{:S(2)}) collective-permute-start(f32[424,256]{1,0:T(8,128)S(1)} %get-tuple-element.72), channel_id=1, source_target_pairs={{0,4},{1,5},{2,6},{3,7},{4,0},{5,1},{6,2},{7,3},{8,12},{9,13},{10,... | collective-permute-start | bytes 1302536 | tf_op jit(solution)/shard_map/ppermute | solution.py:506
  38.2 13.7 %collective-permute-start.12 = (f32[232,256]{1,0:T(8,128)S(1)}, f32[232,256]{1,0:T(8,128)S(1)}, u32[]{:S(2)}, u32[]{:S(2)}) collective-permute-start(f32[232,256]{1,0:T(8,128)S(1)} %get-tuple-element.76), channel_id=1, source_target_pairs={{0,4},{1,5},{2,6},{3,7},{4,0},{5,1},{6,2},{7,3},{8,12},{9,13},{10,... | collective-permute-start | bytes 712712 | tf_op jit(solution)/shard_map/ppermute | solution.py:506
  42.6 14.0 %all-to-all-start = ((f32[32,8,128]{2,1,0:T(8,128)}), f32[32,8,128]{2,1,0:T(8,128)S(1)}, u32[]{:S(2)}, u32[]{:S(2)}) async-start(f32[32,8,128]{2,1,0:T(8,128)} %get-tuple-element.69), calls=%async_computation | async-start | bytes 262144 | tf_op jit(solution)/shard_map/all_to_all | solution.py:658
  49.1 7.4 %collective-permute-start.11 = (f32[80,256]{1,0:T(8,128)S(1)}, f32[80,256]{1,0:T(8,128)S(1)}, u32[]{:S(2)}, u32[]{:S(2)}) collective-permute-start(f32[80,256]{1,0:T(8,128)S(1)} %get-tuple-element.74), channel_id=1, source_target_pairs={{0,28},{1,29},{2,30},{3,31},{4,8},{5,9},{6,10},{7,11},{8,4},{9,5},... | collective-permute-start | bytes 245768 | tf_op jit(solution)/shard_map/ppermute | solution.py:506

commit v4 on v3

--- a/solution.py
+++ b/solution.py
@@ -111,7 +111,6 @@
             o.halo[q, f] = packed(halo, q, f, 1 - odd, odd, which)
             o.cross[q, f] = packed(cross, q, f, odd, odd, which)
     more = [(edge.at[q], o.far0.at[:, pl.ds(half + q * EDGE, EDGE), :]) for q in range(planes // 2)]
-    o.mark[...] = jnp.zeros_like(o.mark)
     for one in started[6:] + copies(more, late_sems):
         one.wait()
 
@@ -373,8 +372,11 @@
 
 def far_products(i, o, stacked, folded):
     grams([(i.rel.at[k], i.rel_edge.at[k]) for k in range(2)], o.gram, stacked, folded)
-    count = o.gram.shape[0]
-    o.send[:count] = o.gram[...]
+
+
+def both_sums(i, o):
+    count = i.gram.shape[0]
+    o.send[:count] = i.gram[...]
     o.send[count:] = i.back[pl.ds(i.back.shape[0] - count, count), :]
 
 
@@ -528,14 +530,14 @@
     sent = call(
         pack_first,
         args,
-        dict(far0=(fields + 1, half + 2 * EDGE, width), halo=edge, cross=edge, mark=sums),
+        dict(far0=(fields + 1, half + 2 * EDGE, width), halo=edge, cross=edge),
         [tiles] * 3 + [local(edge), pltpu.SemaphoreType.DMA((8,)), pltpu.SemaphoreType.DMA((2,))],
         far=("tv", "coef"),
         limit=FIRST_LIMIT,
     )
     far_own = call(
         pack_own,
-        dict(gate=sent.mark, **args),
+        args,
         dict(own=keeps),
         [pltpu.SemaphoreType.DMA((4,))],
         far=("tv", "coef"),
@@ -658,12 +660,13 @@
     totals = lax.all_to_all(r.sums, ("gz", "gy"), 0, 0)
     e = call(
         far_products,
-        dict(rel=r.rel, rel_edge=r.rel_edge, back=back),
-        dict(gram=gram, send=(2 * gram[0], width)),
+        dict(rel=r.rel, rel_edge=r.rel_edge),
+        dict(gram=gram),
         sum_scratch,
     )
-    crossed = moved(e.send, (-1, 0), (1, 0))
-    marked = call(arrived, dict(gate=tail, gram=e.gram), dict(mark=sums))
+    pair = call(both_sums, dict(gram=e.gram, back=back), dict(send=(2 * gram[0], width)))
+    crossed = moved(pair.send, (-1, 0), (1, 0))
+    marked = call(arrived, dict(gate=tail, gram=pair.send), dict(mark=sums))
     finish = functools.partial(finish_all, float(cells))
     finish.__name__ = "finish_all"
     whole = call(

time: 59.7 us -> 59.7 us (level)
  starting transfers between devices: 22.6 us -> 24.9 us
  waiting for transfers between devices: 19.9 us -> 18.3 us
  local copies, waits for them, and re-layouts: 0.69 us -> 0.01 us
    ppermute x13, waiting for transfers between devices: 19.9 us -> 18.3 us  [moved(): return lax.ppermute(x, ('gz', 'gy'), route)]
    ppermute x13, starting transfers between devices: 18.2 us -> 19.7 us  [moved(): return lax.ppermute(x, ('gz', 'gy'), route)]
    all_to_all x1, starting transfers between devices: 4.37 us -> 5.15 us  [body(): totals = lax.all_to_all(r.sums, ('gz', 'gy'), 0, 0)]
    unnamed x6 -> x4, local copies, waits for them, and re-layouts: 0.69 us -> 0.01 us
    pallas_call x14 -> x15, Pallas kernels: 15.5 us -> 15.5 us  [call(): pl.pallas_call(kernel, out_shape=[jax.ShapeDtypeStruct(outs[k], jnp.float...]
where the time goes in v4:
time: 59.7 us; the launch traced here: 59.5 us
  starting transfers between devices  24.9 us (42%)
  waiting for transfers between devices  18.3 us (31%)
  Pallas kernels  15.5 us (26%)
  between operations  0.74 us (1%)
    ppermute x13, starting transfers between devices, moved(): return lax.ppermute(x, ('gz', 'gy'), route)  19.7 us
    ppermute x13, waiting for transfers between devices, moved(): return lax.ppermute(x, ('gz', 'gy'), route)  18.3 us
    pallas_call x15, Pallas kernels, call(): pl.pallas_call(kernel, out_shape=[jax.ShapeDtypeStruct(outs[k], jnp.float...  15.5 us
    all_to_all x1, starting transfers between devices, body(): totals = lax.all_to_all(r.sums, ('gz', 'gy'), 0, 0)  5.15 us
  transfers between devices with their start and end apart: 14, of which 6 were waited for; matrix products, arithmetic and copies ran while one was open for 0% of the time, Pallas kernels for 17%

profile of v4, /device:TPU:0, one launch (start us, length us, event | category | flops | bytes accessed | tf_op | source)
XLA Modules:
  0.0 59.5 jit_solution(13140798823408601773)
XLA Ops:
  0.6 0.0 copy-start
  0.6 0.0 copy-start.1
  0.6 2.2 %pack_first.1 = (f32[5,64,256]{2,1,0:T(8,128)}, f32[2,5,8,256]{3,2,1,0:T(8,128)}, f32[2,5,8,256]{3,2,1,0:T(8,128)}) custom-call(f32[4,4,96,256]{3,2,1,0:T(8,128)} %refs_1_.5, f32[4,96,256]{2,1,0:T(8,128)} %refs_2_.1), custom_call_target="tpu_custom_call" | custom-call | tf_op jit(solution)/shard_map/pack_first/pallas_call | solution.py:33
  2.8 3.0 %collective-permute-start = (f32[5,64,256]{2,1,0:T(8,128)}, f32[5,64,256]{2,1,0:T(8,128)S(1)}, u32[]{:S(2)}, u32[]{:S(2)}) collective-permute-start(f32[5,64,256]{2,1,0:T(8,128)} %get-tuple-element.37), channel_id=1, source_target_pairs={{0,4},{1,5},{2,6},{3,7},{4,0},{5,1},{6,2},{7,3},{8,12},{9,13},{10,... | collective-permute-start | bytes 983048 | tf_op jit(solution)/shard_map/ppermute | solution.py:508
  5.9 0.0 collective-permute-start.1
  5.9 1.7 %collective-permute-start.2 = (f32[2,5,8,256]{3,2,1,0:T(8,128)}, f32[2,5,8,256]{3,2,1,0:T(8,128)S(1)}, u32[]{:S(2)}, u32[]{:S(2)}) collective-permute-start(f32[2,5,8,256]{3,2,1,0:T(8,128)} %get-tuple-element.39), channel_id=1, source_target_pairs={{0,3},{1,0},{2,1},{3,2},{4,5},{5,6},{6,7},{7,4},{8,11},{9,8},{10,9... | collective-permute-start | bytes 245768 | tf_op jit(solution)/shard_map/ppermute | solution.py:508
  7.6 0.0 copy-done
  7.6 0.0 copy-done.1
  7.6 0.3 pack_own.1.refs_2_
  7.9 3.7 %collective-permute-start.7 = (f32[2,5,48,256]{3,2,1,0:T(8,128)S(1)}, f32[2,5,48,256]{3,2,1,0:T(8,128)S(1)}, u32[]{:S(2)}, u32[]{:S(2)}) collective-permute-start(f32[2,5,48,256]{3,2,1,0:T(8,128)S(1)} %pack_own.1.refs_2_), channel_id=1, source_target_pairs={{0,24},{1,25},{2,26},{3,27},{4,12},{5,13},{6,14},{7,15},{8,0},{9,1... | collective-permute-start | bytes 1474568 | tf_op jit(solution)/shard_map/ppermute | solution.py:508
  11.6 0.0 collective-permute-done.1.refs_0_
  11.6 0.0 collective-permute-done.2.refs_1_
  11.6 0.6 pack_second.1
  12.1 0.1 collective-permute-start.3
  12.2 3.4 %collective-permute-start.8 = (f32[2,5,8,256]{3,2,1,0:T(8,128)S(1)}, f32[2,5,8,256]{3,2,1,0:T(8,128)S(1)}, u32[]{:S(2)}, u32[]{:S(2)}) collective-permute-start(f32[2,5,8,256]{3,2,1,0:T(8,128)S(1)} %get-tuple-element.50), channel_id=1, source_target_pairs={{0,24},{1,25},{2,26},{3,27},{4,12},{5,13},{6,14},{7,15},{8,0},{9,1... | collective-permute-start | bytes 245768 | tf_op jit(solution)/shard_map/ppermute | solution.py:508
  15.6 0.0 collective-permute-done.refs_0_
  15.6 0.3 pack_near.1
  15.9 0.1 collective-permute-start.6
  16.0 2.0 %collective-permute-start.5 = (f32[5,48,256]{2,1,0:T(8,128)S(1)}, f32[5,48,256]{2,1,0:T(8,128)S(1)}, u32[]{:S(2)}, u32[]{:S(2)}) collective-permute-start(f32[5,48,256]{2,1,0:T(8,128)S(1)} %get-tuple-element.47), channel_id=1, source_target_pairs={{0,4},{1,5},{2,6},{3,7},{4,0},{5,1},{6,2},{7,3},{8,12},{9,13},{10,... | collective-permute-start | bytes 737288 | tf_op jit(solution)/shard_map/ppermute | solution.py:508
  18.0 0.8 %early.1 = (f32[5,56,256]{2,1,0:T(8,128)S(1)}, f32[5,56,256]{2,1,0:T(8,128)S(1)}, f32[4,56,256]{2,1,0:T(8,128)S(1)}, f32[4,56,256]{2,1,0:T(8,128)S(1)}) custom-call(f32[2,5,56,256]{3,2,1,0:T(8,128)S(1)} %get-tuple-element.42.refs_0_.refs_1_, f32[2,5,56,256]{3,2,1,0:T(8,128)S(1)} %get-tuple-element.43.refs_1_.refs_0_), custom_call_target="tpu_custom_call" | custom-call | flops 3000000000 | tf_op jit(solution)/shard_map/early/pallas_call | solution.py:33
  18.8 3.9 %collective-permute-done.3.refs_1_ = f32[5,64,256]{2,1,0:T(8,128)S(1)} collective-permute-done((f32[5,64,256]{2,1,0:T(8,128)S(1)}, f32[5,64,256]{2,1,0:T(8,128)S(1)}, u32[]{:S(2)}, u32[]{:S(2)}) %collective-permute-start.3) | collective-permute-done | bytes 327712 | tf_op jit(solution)/shard_map/ppermute | solution.py:508
  22.8 0.1 collective-permute-start.4
  22.9 1.0 %collective-permute-done.8.refs_2_ = f32[2,5,8,256]{3,2,1,0:T(8,128)S(1)} collective-permute-done((f32[2,5,8,256]{3,2,1,0:T(8,128)S(1)}, f32[2,5,8,256]{3,2,1,0:T(8,128)S(1)}, u32[]{:S(2)}, u32[]{:S(2)}) %collective-permute-start.8) | collective-permute-done | bytes 81952 | tf_op jit(solution)/shard_map/ppermute | solution.py:508
  23.9 0.0 collective-permute-done.7.refs_1_
  23.9 0.8 %outer.1 = (f32[5,56,256]{2,1,0:T(8,128)S(1)}, f32[4,56,256]{2,1,0:T(8,128)S(1)}, f32[4,56,256]{2,1,0:T(8,128)S(1)}) custom-call(f32[2,5,56,256]{3,2,1,0:T(8,128)S(1)} %get-tuple-element.41.refs_0_.refs_1_, f32[2,5,48,256]{3,2,1,0:T(8,128)S(1)} %collective-permute-done.7.refs_1_, f32[2,5,8,256]{3,2,1,0:T(8,128)S(1)} %collective-permute-done.8.refs_2_, ...), custom_call_target="tpu_custom_call" | custom-call | tf_op jit(solution)/shard_map/outer/pallas_call | solution.py:33
  24.7 3.3 %collective-permute-done.6.refs_1_.refs_2_ = f32[5,48,256]{2,1,0:T(8,128)S(1)} collective-permute-done((f32[5,48,256]{2,1,0:T(8,128)S(1)}, f32[5,48,256]{2,1,0:T(8,128)S(1)}, u32[]{:S(2)}, u32[]{:S(2)}) %collective-permute-start.6) | collective-permute-done | bytes 245792 | tf_op jit(solution)/shard_map/ppermute | solution.py:508
  28.0 0.7 %inner_last.1 = (f32[5,56,256]{2,1,0:T(8,128)S(1)}, f32[4,56,256]{2,1,0:T(8,128)S(1)}, f32[4,48,256]{2,1,0:T(8,128)S(1)}, f32[4,8,256]{2,1,0:T(8,128)S(1)}) custom-call(f32[2,5,56,256]{3,2,1,0:T(8,128)S(1)} %get-tuple-element.41.refs_0_.refs_1_, f32[5,48,256]{2,1,0:T(8,128)S(1)} %collective-permute-done.6.refs_1_.refs_2_, ...), custom_call_target="tpu_custom_call" | custom-call | tf_op jit(solution)/shard_map/inner_last/pallas_call | solution.py:33
  28.7 0.1 collective-permute-start.9
  28.8 4.5 %collective-permute-done.5.refs_3_.refs_1_ = f32[5,48,256]{2,1,0:T(8,128)S(1)} collective-permute-done((f32[5,48,256]{2,1,0:T(8,128)S(1)}, f32[5,48,256]{2,1,0:T(8,128)S(1)}, u32[]{:S(2)}, u32[]{:S(2)}) %collective-permute-start.5) | collective-permute-done | bytes 245792 | tf_op jit(solution)/shard_map/ppermute | solution.py:508
  33.3 2.2 %inner.1 = (f32[5,56,256]{2,1,0:T(8,128)S(1)}, f32[4,56,256]{2,1,0:T(8,128)S(1)}, f32[4,56,256]{2,1,0:T(8,128)S(1)}, f32[2,4,48,256]{3,2,1,0:T(8,128)S(1)}, f32[...) custom-call(f32[2,5,56,256]{3,2,1,0:T(8,128)S(1)} %get-tuple-element.43.refs_1_.refs_0_, ...), custom_call_target="tpu_custom_call" | custom-call | flops 10000000000 | tf_op jit(solution)/shard_map/inner/pallas_call | solution.py:33
  35.5 0.1 collective-permute-start.10
  35.6 1.9 %near_rest.1 = (f32[3,4,48,256]{3,2,1,0:T(8,128)S(1)}, f32[3,4,8,256]{3,2,1,0:T(8,128)}, f32[40,256]{1,0:T(8,128)S(1)}, f32[232,256]{1,0:T(8,128)S(1)}, f32[8,128]{1,0:T(8,128)S(1)}) custom-call(f32[2,5,56,256]{3,2,1,0:T(8,128)S(1)} %get-tuple-element.43.refs_1_.refs_0_, f32[5,48,256]{2,1,0:T(8,128)S(1)} %collective-permute-done.5.refs_3_.refs_1_, ...), custom_call_target="tpu_custom_call" | custom-call | flops 3000000000 | tf_op jit(solution)/shard_map/near_rest/pallas_call | solution.py:33
  37.5 2.0 %collective-permute-start.12 = (f32[232,256]{1,0:T(8,128)S(1)}, f32[232,256]{1,0:T(8,128)S(1)}, u32[]{:S(2)}, u32[]{:S(2)}) collective-permute-start(f32[232,256]{1,0:T(8,128)S(1)} %get-tuple-element.70), channel_id=1, source_target_pairs={{0,4},{1,5},{2,6},{3,7},{4,0},{5,1},{6,2},{7,3},{8,12},{9,13},{10,... | collective-permute-start | bytes 712712 | tf_op jit(solution)/shard_map/ppermute | solution.py:508
  39.5 0.0 collective-permute-done.9.refs_6_
  39.5 0.0 collective-permute-done.4.refs_0_
  39.5 2.3 %far_rest.1 = (f32[2,4,48,256]{3,2,1,0:T(8,128)S(1)}, f32[2,4,8,256]{3,2,1,0:T(8,128)S(1)}, f32[32,8,128]{2,1,0:T(8,128)}) custom-call(f32[2,5,56,256]{3,2,1,0:T(8,128)S(1)} %collective-permute-done.4.refs_0_, f32[2,5,56,256]{3,2,1,0:T(8,128)S(1)} %get-tuple-element.42.refs_0_.refs_1_, f32[4,56,256]{2,1,0:T(8,128)S(1)} %get-tuple-element.44.refs_3_.refs_2_, ...), custom_call_target="tpu_custom_call" | custom-call | tf_op jit(solution)/shard_map/far_rest/pallas_call | solution.py:33
  41.8 5.1 %all-to-all-start = ((f32[32,8,128]{2,1,0:T(8,128)}), f32[32,8,128]{2,1,0:T(8,128)S(1)}, u32[]{:S(2)}, u32[]{:S(2)}) async-start(f32[32,8,128]{2,1,0:T(8,128)} %get-tuple-element.65), calls=%async_computation | async-start | bytes 262144 | tf_op jit(solution)/shard_map/all_to_all | solution.py:660
  46.9 0.4 far_products.1.refs_0_.refs_1_
  47.4 1.1 %collective-permute-done.10.refs_1_.refs_4_ = f32[424,256]{1,0:T(8,128)S(1)} collective-permute-done((f32[424,256]{1,0:T(8,128)S(1)}, f32[424,256]{1,0:T(8,128)S(1)}, u32[]{:S(2)}, u32[]{:S(2)}) %collective-permute-start.10) | collective-permute-done | bytes 434208 | tf_op jit(solution)/shard_map/ppermute | solution.py:508
  48.4 3.6 %collective-permute-start.11 = (f32[80,256]{1,0:T(8,128)S(1)}, f32[80,256]{1,0:T(8,128)S(1)}, u32[]{:S(2)}, u32[]{:S(2)}) collective-permute-start(f32[80,256]{1,0:T(8,128)S(1)} %both_sums.1.refs_1_), channel_id=1, source_target_pairs={{0,28},{1,29},{2,30},{3,31},{4,8},{5,9},{6,10},{7,11},{8,4},{9,5},... | collective-permute-start | bytes 245768 | tf_op jit(solution)/shard_map/ppermute | solution.py:508
  52.0 0.0 collective-permute-done.12.refs_0_.refs_5_
  52.0 4.5 %collective-permute-done.11.refs_2_ = f32[80,256]{1,0:T(8,128)S(1)} collective-permute-done((f32[80,256]{1,0:T(8,128)S(1)}, f32[80,256]{1,0:T(8,128)S(1)}, u32[]{:S(2)}, u32[]{:S(2)}) %collective-permute-start.11) | collective-permute-done | bytes 81952 | tf_op jit(solution)/shard_map/ppermute | solution.py:508
  56.5 0.0 all-to-all-done.refs_0_
  56.5 3.0 %finish_all.1 = (f32[4,4,96,256]{3,2,1,0:T(8,128)}, f32[10,1,24,64]{3,2,1,0:T(8,128)}) custom-call(f32[32,8,128]{2,1,0:T(8,128)S(1)} %all-to-all-done.refs_0_, f32[40,256]{1,0:T(8,128)S(1)} %far_products.1.refs_0_.refs_1_, f32[80,256]{1,0:T(8,128)S(1)} %collective-permute-done.11.refs_2_, f32[40,256]{1,0:T(8,128)S(1)} %get-tuple-element.69.refs_3_, ...), custom_call_target="tpu_custom_call" | custom-call | tf_op jit(solution)/shard_map/finish_all/pallas_call | solution.py:33
  (3 shorter events, 0.1 us)
Async XLA Ops:
  0.6 7.0 %copy-start = (f32[4,4,96,256]{3,2,1,0:T(8,128)S(1)}, f32[4,4,96,256]{3,2,1,0:T(8,128)}, u32[]{:S(2)}) copy-start(f32[4,4,96,256]{3,2,1,0:T(8,128)} %refs_1_.5) | copy-start | bytes 4718596
  0.6 7.0 %copy-start.1 = (f32[4,96,256]{2,1,0:T(8,128)S(1)}, f32[4,96,256]{2,1,0:T(8,128)}, u32[]{:S(2)}) copy-start(f32[4,96,256]{2,1,0:T(8,128)} %refs_2_.1) | copy-start | bytes 1179652
  2.8 12.8 %collective-permute-start = (f32[5,64,256]{2,1,0:T(8,128)}, f32[5,64,256]{2,1,0:T(8,128)S(1)}, u32[]{:S(2)}, u32[]{:S(2)}) collective-permute-start(f32[5,64,256]{2,1,0:T(8,128)} %get-tuple-element.37), channel_id=1, source_target_pairs={{0,4},{1,5},{2,6},{3,7},{4,0},{5,1},{6,2},{7,3},{8,12},{9,13},{10,... | collective-permute-start | bytes 983048 | tf_op jit(solution)/shard_map/ppermute | solution.py:508
  5.9 5.7 %collective-permute-start.1 = (f32[2,5,8,256]{3,2,1,0:T(8,128)}, f32[2,5,8,256]{3,2,1,0:T(8,128)S(1)}, u32[]{:S(2)}, u32[]{:S(2)}) collective-permute-start(f32[2,5,8,256]{3,2,1,0:T(8,128)} %get-tuple-element.38), channel_id=1, source_target_pairs={{0,1},{1,2},{2,3},{3,0},{4,7},{5,4},{6,5},{7,6},{8,9},{9,10},{10,1... | collective-permute-start | bytes 245768 | tf_op jit(solution)/shard_map/ppermute | solution.py:508
  5.9 5.7 %collective-permute-start.2 = (f32[2,5,8,256]{3,2,1,0:T(8,128)}, f32[2,5,8,256]{3,2,1,0:T(8,128)S(1)}, u32[]{:S(2)}, u32[]{:S(2)}) collective-permute-start(f32[2,5,8,256]{3,2,1,0:T(8,128)} %get-tuple-element.39), channel_id=1, source_target_pairs={{0,3},{1,0},{2,1},{3,2},{4,5},{5,6},{6,7},{7,4},{8,11},{9,8},{10,9... | collective-permute-start | bytes 245768 | tf_op jit(solution)/shard_map/ppermute | solution.py:508
  7.9 15.9 %collective-permute-start.7 = (f32[2,5,48,256]{3,2,1,0:T(8,128)S(1)}, f32[2,5,48,256]{3,2,1,0:T(8,128)S(1)}, u32[]{:S(2)}, u32[]{:S(2)}) collective-permute-start(f32[2,5,48,256]{3,2,1,0:T(8,128)S(1)} %pack_own.1.refs_2_), channel_id=1, source_target_pairs={{0,24},{1,25},{2,26},{3,27},{4,12},{5,13},{6,14},{7,15},{8,0},{9,1... | collective-permute-start | bytes 1474568 | tf_op jit(solution)/shard_map/ppermute | solution.py:508
  12.1 10.6 %collective-permute-start.3 = (f32[5,64,256]{2,1,0:T(8,128)S(1)}, f32[5,64,256]{2,1,0:T(8,128)S(1)}, u32[]{:S(2)}, u32[]{:S(2)}) collective-permute-start(f32[5,64,256]{2,1,0:T(8,128)S(1)} %get-tuple-element.40), channel_id=1, source_target_pairs={{0,4},{1,5},{2,6},{3,7},{4,0},{5,1},{6,2},{7,3},{8,12},{9,13},{10,... | collective-permute-start | bytes 983048 | tf_op jit(solution)/shard_map/ppermute | solution.py:508
  12.2 11.6 %collective-permute-start.8 = (f32[2,5,8,256]{3,2,1,0:T(8,128)S(1)}, f32[2,5,8,256]{3,2,1,0:T(8,128)S(1)}, u32[]{:S(2)}, u32[]{:S(2)}) collective-permute-start(f32[2,5,8,256]{3,2,1,0:T(8,128)S(1)} %get-tuple-element.50), channel_id=1, source_target_pairs={{0,24},{1,25},{2,26},{3,27},{4,12},{5,13},{6,14},{7,15},{8,0},{9,1... | collective-permute-start | bytes 245768 | tf_op jit(solution)/shard_map/ppermute | solution.py:508
  15.9 12.1 %collective-permute-start.6 = (f32[5,48,256]{2,1,0:T(8,128)S(1)}, f32[5,48,256]{2,1,0:T(8,128)S(1)}, u32[]{:S(2)}, u32[]{:S(2)}) collective-permute-start(f32[5,48,256]{2,1,0:T(8,128)S(1)} %get-tuple-element.49), channel_id=1, source_target_pairs={{0,4},{1,5},{2,6},{3,7},{4,0},{5,1},{6,2},{7,3},{8,12},{9,13},{10,... | collective-permute-start | bytes 737288 | tf_op jit(solution)/shard_map/ppermute | solution.py:508
  16.0 17.3 %collective-permute-start.5 = (f32[5,48,256]{2,1,0:T(8,128)S(1)}, f32[5,48,256]{2,1,0:T(8,128)S(1)}, u32[]{:S(2)}, u32[]{:S(2)}) collective-permute-start(f32[5,48,256]{2,1,0:T(8,128)S(1)} %get-tuple-element.47), channel_id=1, source_target_pairs={{0,4},{1,5},{2,6},{3,7},{4,0},{5,1},{6,2},{7,3},{8,12},{9,13},{10,... | collective-permute-start | bytes 737288 | tf_op jit(solution)/shard_map/ppermute | solution.py:508
  22.8 16.7 %collective-permute-start.4 = (f32[2,5,56,256]{3,2,1,0:T(8,128)S(1)}, f32[2,5,56,256]{3,2,1,0:T(8,128)S(1)}, u32[]{:S(2)}, u32[]{:S(2)}) collective-permute-start(f32[2,5,56,256]{3,2,1,0:T(8,128)S(1)} %get-tuple-element.41.refs_0_.refs_1_), channel_id=1, source_target_pairs={{0,8},{1,9},{2,10},{3,11},{4,28},{5,29},{6,30},{7,31},{8,16},{9,17... | collective-permute-start | bytes 1720328 | tf_op jit(solution)/shard_map/ppermute | solution.py:508
  28.7 10.8 %collective-permute-start.9 = (f32[4,48,256]{2,1,0:T(8,128)S(1)}, f32[4,48,256]{2,1,0:T(8,128)S(1)}, u32[]{:S(2)}, u32[]{:S(2)}) collective-permute-start(f32[4,48,256]{2,1,0:T(8,128)S(1)} %get-tuple-element.56.refs_8_.refs_11_), channel_id=1, source_target_pairs={{0,4},{1,5},{2,6},{3,7},{4,0},{5,1},{6,2},{7,3},{8,12},{9,13},{10,... | collective-permute-start | bytes 589832 | tf_op jit(solution)/shard_map/ppermute | solution.py:508
  35.5 12.9 %collective-permute-start.10 = (f32[424,256]{1,0:T(8,128)S(1)}, f32[424,256]{1,0:T(8,128)S(1)}, u32[]{:S(2)}, u32[]{:S(2)}) collective-permute-start(f32[424,256]{1,0:T(8,128)S(1)} %get-tuple-element.68), channel_id=1, source_target_pairs={{0,4},{1,5},{2,6},{3,7},{4,0},{5,1},{6,2},{7,3},{8,12},{9,13},{10,... | collective-permute-start | bytes 1302536 | tf_op jit(solution)/shard_map/ppermute | solution.py:508
  37.5 14.5 %collective-permute-start.12 = (f32[232,256]{1,0:T(8,128)S(1)}, f32[232,256]{1,0:T(8,128)S(1)}, u32[]{:S(2)}, u32[]{:S(2)}) collective-permute-start(f32[232,256]{1,0:T(8,128)S(1)} %get-tuple-element.70), channel_id=1, source_target_pairs={{0,4},{1,5},{2,6},{3,7},{4,0},{5,1},{6,2},{7,3},{8,12},{9,13},{10,... | collective-permute-start | bytes 712712 | tf_op jit(solution)/shard_map/ppermute | solution.py:508
  41.8 14.7 %all-to-all-start = ((f32[32,8,128]{2,1,0:T(8,128)}), f32[32,8,128]{2,1,0:T(8,128)S(1)}, u32[]{:S(2)}, u32[]{:S(2)}) async-start(f32[32,8,128]{2,1,0:T(8,128)} %get-tuple-element.65), calls=%async_computation | async-start | bytes 262144 | tf_op jit(solution)/shard_map/all_to_all | solution.py:660
  48.4 8.1 %collective-permute-start.11 = (f32[80,256]{1,0:T(8,128)S(1)}, f32[80,256]{1,0:T(8,128)S(1)}, u32[]{:S(2)}, u32[]{:S(2)}) collective-permute-start(f32[80,256]{1,0:T(8,128)S(1)} %both_sums.1.refs_1_), channel_id=1, source_target_pairs={{0,28},{1,29},{2,30},{3,31},{4,8},{5,9},{6,10},{7,11},{8,4},{9,5},... | collective-permute-start | bytes 245768 | tf_op jit(solution)/shard_map/ppermute | solution.py:508
